TPU v7x, 32 devices: a whole 2x2x4 slice. The times are simulated.
32 devices in a mesh: groups: 2 (over y), row: 4 (over z), col: 4 (over x, core).
Axes of the slice: x: 2, y: 2, z: 4, core: 2. Of those that a mesh axis runs over, the one named last changes fastest.
Arguments:
- inputs: bfloat16 [512, 12288], P(('groups', 'col'), 'row'), parts along dimension 0, may hold values from -6 to 6
- weight: bfloat16 [12288, 24576], P('row', 'col'), may hold values from -0.0546875 to 0.0546875
- cotangent: bfloat16 [512, 24576], P(('groups', 'row'), 'col'), parts along dimension 0, may hold values from -6 to 6
Outputs:
- hidden: bfloat16 [512, 24576], P(('groups', 'row'), 'col'), parts along dimension 0
- grad_inputs: bfloat16 [512, 12288], P(('groups', 'col'), 'row'), parts along dimension 0
- grad_weight: bfloat16 [24576, 24576], P(('groups', 'row'), 'col'), parts along dimension 0
There are 2 independent parts, one for each index of `groups`. A program takes and returns all parts, laid end to end along the dimension named above; an argument that names none is the same for every part. Nothing has to cross between parts.
All inputs are finite; a program needn't handle non-finite values.
Results may differ from a plain program's by a relative error of at most 0.014.
Values may be sent and summed in bfloat16 or wider, within the bound.
No kernel may reach another device: no remote copies, remote signals or barrier semaphores. Data moves between devices by JAX's collectives and lax.ppermute only.
A program may use at most 256 MiB of HBM per device.

v0:
```python
import jax
import jax.numpy as jnp
from jax import lax
from jax.sharding import PartitionSpec as P

tanh_scale = 0.7978845608028654
cubic_coef = 0.044715


def gelu_value(preact):
    inner = tanh_scale * (preact + cubic_coef * preact * preact * preact)
    return 0.5 * preact * (1.0 + jnp.tanh(inner))


def gelu_slope(preact):
    inner = tanh_scale * (preact + cubic_coef * preact * preact * preact)
    tangent = jnp.tanh(inner)
    return 0.5 * (1.0 + tangent) + 0.5 * preact * (1.0 - tangent * tangent) * tanh_scale * (
        1.0 + 3.0 * cubic_coef * preact * preact
    )


def on_device(inputs, weight, cotangent):
    all_tokens = lax.all_gather(inputs, "col", axis=0, tiled=True)
    partial_value = jnp.dot(all_tokens, weight, preferred_element_type=jnp.float32)
    preact = lax.psum_scatter(
        partial_value.astype(jnp.bfloat16), "row", scatter_dimension=0, tiled=True
    ).astype(jnp.float32)
    hidden = gelu_value(preact).astype(jnp.bfloat16)
    delta_grad = (cotangent.astype(jnp.float32) * gelu_slope(preact)).astype(jnp.bfloat16)
    delta_all = lax.all_gather(delta_grad, "row", axis=0, tiled=True)
    grad_weight = lax.dot_general(
        all_tokens, delta_all, (((0,), (0,)), ((), ())), preferred_element_type=jnp.float32
    ).astype(jnp.bfloat16)
    grad_inputs = lax.psum_scatter(
        lax.dot_general(
            delta_all, weight, (((1,), (1,)), ((), ())), preferred_element_type=jnp.float32
        ).astype(jnp.bfloat16),
        "col",
        scatter_dimension=0,
        tiled=True,
    )
    return (hidden, grad_inputs, grad_weight)


def solution(mesh):
    in_specs = (P(("groups", "col"), "row"), P("row", "col"), P(("groups", "row"), "col"))
    out_specs = (
        P(("groups", "row"), "col"),
        P(("groups", "col"), "row"),
        P(("groups", "row"), "col"),
    )
    return jax.shard_map(
        on_device, mesh=mesh, in_specs=in_specs, out_specs=out_specs, check_vma=False
    )
```

profile of v0, /device:TPU:0, one launch (start us, length us, event | category | flops | bytes accessed | tf_op | source)
XLA Modules:
  0.0 272.2 jit_solution(352657214738966355)
XLA Ops:
  7.2 0.0 all-gather.3.cloned.1.call-start
  7.2 0.7 all-gather.3.cloned.1.call-update
  7.9 0.0 reduce-scatter.3.cloned.1.call-start
  7.9 24.0 %all-gather.3.cloned.1.call-done = bf16[256,3072]{1,0:T(8,128)(2,1)} async-done(((bf16[64,3072]{1,0:T(8,128)(2,1)}), bf16[256,3072]{1,0:T(8,128)(2,1)}) %all-gather.3.cloned.1.call-update) | async-done | bytes 1572880 | tf_op jit(solution)/shard_map/all_gather | solution.py:24
  31.9 18.4 %convolution_convert_fusion = bf16[256,6144]{1,0:T(8,128)(2,1)} fusion(bf16[256,3072]{1,0:T(8,128)(2,1)} %all-gather.3.cloned.1.call-done, bf16[3072,6144]{1,0:T(8,128)(2,1)} %param.4), kind=kOutput, calls=%fused_computation.1 | convolution fusion | flops 9665249280 | bytes 42467328 | tf_op jit(solution)/shard_map/dot_general | solution.py:25
  50.3 0.0 copy-start.1
  50.3 0.0 reduce-scatter.3.cloned.1.call-update
  50.3 0.0 all-gather.5.cloned.1.call-start
  50.4 60.4 %reduce-scatter.3.cloned.1.call-done = bf16[64,6144]{1,0:T(8,128)(2,1)} async-done(((bf16[256,6144]{1,0:T(8,128)(2,1)}), bf16[64,6144]{1,0:T(8,128)(2,1)}) %reduce-scatter.3.cloned.1.call-update) | async-done | bytes 786448 | tf_op jit(solution)/shard_map/reduce_scatter | solution.py:26
  110.7 0.0 copy-done.1
  110.7 3.4 %fusion.7 = (bf16[64,6144]{1,0:T(8,128)(2,1)}, bf16[64,6144]{1,0:T(8,128)(2,1)}) fusion(bf16[64,6144]{1,0:T(8,128)(2,1)} %reduce-scatter.3.cloned.1.call-done, bf16[64,6144]{1,0:T(8,128)(2,1)S(1)} %copy-done.1), kind=kLoop, calls=%fused_computation.17 | loop fusion | flops 9043968 | bytes 3145728 | tf_op jit(solution)/shard_map/convert_element_type | solution.py:30
  114.2 0.0 all-gather.5.cloned.1.call-update
  114.2 0.2 reduce-scatter.5.cloned.1.call-start
  114.4 63.5 %all-gather.5.cloned.1.call-done = bf16[256,6144]{1,0:T(8,128)(2,1)} async-done(((bf16[64,6144]{1,0:T(8,128)(2,1)}), bf16[256,6144]{1,0:T(8,128)(2,1)}) %all-gather.5.cloned.1.call-update) | async-done | bytes 3145744 | tf_op jit(solution)/shard_map/all_gather | solution.py:31
  177.9 0.0 copy-start
  177.9 21.5 %convolution_convert_fusion.1 = bf16[256,3072]{1,0:T(8,128)(2,1)} fusion(bf16[256,6144]{1,0:T(8,128)(2,1)} %all-gather.5.cloned.1.call-done, bf16[3072,6144]{1,0:T(8,128)(2,1)} %param.4), kind=kOutput, calls=%fused_computation.9 | convolution fusion | flops 9664462848 | bytes 42467328 | tf_op jit(solution)/shard_map/dot_general | solution.py:36
  199.4 0.0 reduce-scatter.5.cloned.1.call-update
  199.4 0.0 copy-done
  199.4 17.7 %convert_bitcast_fusion = bf16[3072,6144]{0,1:T(8,128)(2,1)} fusion(bf16[256,6144]{1,0:T(8,128)(2,1)S(1)} %copy-done, bf16[256,3072]{1,0:T(8,128)(2,1)} %all-gather.3.cloned.1.call-done), kind=kOutput, calls=%fused_computation | convolution fusion | flops 9682550784 | bytes 42467328 | tf_op jit(solution)/shard_map/dot_general | solution.py:32
  217.1 48.5 %copy.6 = bf16[3072,6144]{1,0:T(8,128)(2,1)} copy(bf16[3072,6144]{0,1:T(8,128)(2,1)} %convert_bitcast_fusion) | data formatting | bytes 75497472
  265.7 0.0 reduce-scatter.5.cloned.1.call-done
Async XLA Ops:
  7.2 24.8 %all-gather.3.cloned.1.call-start = ((), (), s32[]{:S(2)}) async-start(), calls=%async_computation.2 | async-start | bytes 1966080 | tf_op jit(solution)/shard_map/all_gather | solution.py:24
  7.9 102.8 %reduce-scatter.3.cloned.1.call-start = ((), (), s32[]{:S(2)}) async-start(), calls=%async_computation.3 | async-start | bytes 3932160 | tf_op jit(solution)/shard_map/reduce_scatter | solution.py:26
  50.3 60.4 %copy-start.1 = (bf16[64,6144]{1,0:T(8,128)(2,1)S(1)}, bf16[64,6144]{1,0:T(8,128)(2,1)}, u32[]{:S(2)}) copy-start(bf16[64,6144]{1,0:T(8,128)(2,1)} %param.5) | copy-start | bytes 2359300
  50.3 127.6 %all-gather.5.cloned.1.call-start = ((), (), s32[]{:S(2)}) async-start(), calls=%async_computation.4 | async-start | bytes 3932160 | tf_op jit(solution)/shard_map/all_gather | solution.py:31
  114.2 151.5 %reduce-scatter.5.cloned.1.call-start = ((), (), s32[]{:S(2)}) async-start(), calls=%async_computation.5 | async-start | bytes 1966080 | tf_op jit(solution)/shard_map/reduce_scatter | solution.py:35
  177.9 21.5 %copy-start = (bf16[256,6144]{1,0:T(8,128)(2,1)S(1)}, bf16[256,6144]{1,0:T(8,128)(2,1)}, u32[]{:S(2)}) copy-start(bf16[256,6144]{1,0:T(8,128)(2,1)} %all-gather.5.cloned.1.call-done) | copy-start | bytes 9437188
Sparse Core Ops, SparseCore 0:
  9.6 22.3 all-gather.2
  50.4 60.2 reduce-scatter.2
  114.3 63.5 all-gather.4
  199.5 26.8 reduce-scatter.4
where the time goes:
time: 274 us; the launch traced here: 272 us
  waiting for transfers between devices  149 us (54%)
  matrix products  57.5 us (21%)
  local copies, waits for them, and re-layouts  48.5 us (18%)
  between operations  13.8 us (5%)
  other arithmetic  3.44 us (1%)
    all_gather x1, waiting for transfers between devices, on_device(): delta_all = lax.all_gather(delta_grad, 'row', axis=0, tiled=True)  63.5 us
    reduce_scatter x1, waiting for transfers between devices, on_device(): lax.psum_scatter(partial_value.astype(jnp.bfloat16), 'row', scatter_dimen...  60.4 us
    unnamed x5, local copies, waits for them, and re-layouts  48.5 us
    all_gather x1, waiting for transfers between devices, on_device(): all_tokens = lax.all_gather(inputs, 'col', axis=0, tiled=True)  24 us
    dot_general x1, matrix products, on_device(): lax.dot_general(delta_all, weight, (((1,), (1,)), ((), ())), preferred_el...  21.5 us
    dot_general x1, matrix products, on_device(): jnp.dot(all_tokens, weight, preferred_element_type=jnp.float32)  18.4 us
    dot_general x1, matrix products, on_device(): lax.dot_general(all_tokens, delta_all, (((0,), (0,)), ((), ())), preferre...  17.7 us
  transfers between devices with their start and end apart: 4, of which 3 were waited for; matrix products, arithmetic and copies ran while one was open for 24% of the time, Pallas kernels for 0%

commit v1 on v0

v1 whole, which is shorter than its diff:
```python
import functools

import jax
import jax.numpy as jnp
from jax import lax
from jax.experimental import pallas as pl
from jax.experimental.pallas import tpu as pltpu
from jax.sharding import PartitionSpec as P

tanh_scale = 0.7978845608028654
cubic_coef = 0.044715
bf16 = jnp.bfloat16
f32 = jnp.float32
MIB = 1 << 20

CORES = ((0, 1), (1, 0), (2, 3), (3, 2))
ACROSS = ((0, 2), (2, 0), (1, 3), (3, 1))
PLANE = ("row", "col")
HALVES = tuple((4 * row + col, 4 * (row ^ 1) + col) for row in range(4) for col in range(4))
MIDDLE = tuple(
    (4 * row + col, 4 * (3 - row) + col if row in (1, 2) else 4 * row + (col ^ 1))
    for row in range(4)
    for col in range(4)
)

CHUNKS = 3
SPLIT = 2


def gelu_both(preact):
    inner = tanh_scale * (preact + cubic_coef * preact * preact * preact)
    tangent = jnp.tanh(inner)
    value = 0.5 * preact * (1.0 + tangent)
    slope = 0.5 * (1.0 + tangent) + 0.5 * preact * (1.0 - tangent * tangent) * tanh_scale * (
        1.0 + 3.0 * cubic_coef * preact * preact
    )
    return value, slope


def send(value, axis, pairs):
    return lax.ppermute(value, axis, pairs)


def place_of(token_block, row):
    same_half = (token_block // 2) == (row // 2)
    return jnp.where(same_half, token_block ^ row, jnp.where(row < 2, token_block, 3 - token_block))


def params(limit=48):
    return pltpu.CompilerParams(vmem_limit_bytes=limit * MIB)


def cost(flops, bytes_accessed):
    return pl.CostEstimate(flops=int(flops), bytes_accessed=int(bytes_accessed), transcendentals=0)


def whole(*shape):
    return pl.BlockSpec(shape, lambda j: (0,) * len(shape))


def forward_kernel(w_ref, x_ref, *outs):
    outs, token = outs[:-1], outs[-1]
    token[...] = jnp.zeros_like(token)
    sums = jnp.dot(x_ref[...], w_ref[...], preferred_element_type=f32).astype(bf16)
    rows = outs[0].shape[0]
    for k, out in enumerate(outs):
        out[...] = sums[k * rows : (k + 1) * rows]


def forward_first_kernel(w_ref, *refs):
    pieces, outs, x_ref = refs[:4], refs[4:9], refs[9]
    rows = outs[0].shape[0]

    @pl.when(pl.program_id(0) == 0)
    def _():
        row, col = lax.axis_index("row"), lax.axis_index("col")
        for k, piece in enumerate(pieces):
            at = pl.multiple_of(place_of(col ^ k, row) * rows, rows)
            x_ref[pl.ds(at, rows), :] = piece[...]

    forward_kernel(w_ref, x_ref, *outs)


def tile_of(size, start, want):
    tile = want
    while size % tile or start % tile:
        tile //= 2
    return tile


TOKEN = jax.ShapeDtypeStruct((8, 128), f32)


def forward(x, weight, start, size, tokens, parts, dep=None):
    depth = weight.shape[0]
    tile = tile_of(size, start, 512)
    rows = tokens // parts
    first = isinstance(x, tuple)
    out_shape = [jax.ShapeDtypeStruct((rows, size), bf16)] * parts + [TOKEN]
    out_specs = [pl.BlockSpec((rows, tile), lambda j: (0, j))] * parts + [whole(8, 128)]
    if first:
        out_shape.append(jax.ShapeDtypeStruct((tokens, depth), bf16))
        out_specs.append(whole(tokens, depth))
        in_x = [whole(rows, depth)] * parts
    else:
        in_x = [whole(tokens, depth)]
        x = (x,)
    return call(
        forward_first_kernel if first else forward_kernel,
        [weight, *x],
        [pl.BlockSpec((depth, tile), lambda j: (0, start // tile + j))] + in_x,
        dep,
        grid=(size // tile,),
        out_specs=out_specs,
        out_shape=out_shape,
        compiler_params=params(),
        cost_estimate=cost(2 * tokens * depth * size, 2 * depth * size),
        name="forward_sums",
    )


def stack_blocks(refs, all_ref):
    rows = refs[0].shape[0]
    own, near, mid_m, mid_e, far_m, far_e = refs
    row = lax.axis_index("row")
    middle = (row == 1) | (row == 2)
    all_ref[0:rows] = own[...]
    all_ref[rows : 2 * rows] = near[...]

    @pl.when(middle)
    def _():
        all_ref[2 * rows : 3 * rows] = mid_m[...]
        all_ref[3 * rows :] = far_m[...]

    @pl.when(jnp.logical_not(middle))
    def _():
        all_ref[2 * rows : 3 * rows] = mid_e[...]
        all_ref[3 * rows :] = far_e[...]


def grad_weight_kernel(count, x_ref, *refs):
    blocks, out, token, all_ref = refs[:count], refs[-3], refs[-2], refs[-1]
    token[...] = jnp.zeros_like(token)
    if count == 1:
        all_ref = blocks[0]
    else:
        pl.when(pl.program_id(0) == 0)(lambda: stack_blocks(blocks, all_ref))
    x_t = x_ref[...].T
    size = all_ref.shape[1]
    step = tile_of(size, 0, 512)
    for at in range(0, size, step):
        out[:, at : at + step] = jnp.dot(
            x_t, all_ref[:, at : at + step], preferred_element_type=f32
        ).astype(bf16)


def grad_weight_part(x, blocks, total, start, width, lo, hi, dep=None):
    tokens, depth = x.shape
    size = blocks[0].shape[1]
    tile = tile_of(hi - lo, lo, 512)
    count = len(blocks)
    operands = [x, *blocks]
    in_specs = [pl.BlockSpec((tokens, tile), lambda j: (0, lo // tile + j))]
    in_specs += [whole(*b.shape) for b in blocks]
    aliases = {}
    if total is not None:
        operands.append(total)
        in_specs.append(pl.BlockSpec(memory_space=pl.ANY))
        aliases = {len(operands) - 1: 0}
    return call(
        functools.partial(grad_weight_kernel, count),
        operands,
        in_specs,
        dep,
        grid=((hi - lo) // tile,),
        out_specs=[
            pl.BlockSpec((tile, size), lambda j: (lo // tile + j, start // size)),
            whole(8, 128),
        ],
        out_shape=[jax.ShapeDtypeStruct((depth, width), bf16), TOKEN],
        scratch_shapes=[pltpu.VMEM((tokens, size), bf16)],
        input_output_aliases=aliases,
        compiler_params=params(),
        cost_estimate=cost(2 * tokens * (hi - lo) * size, 2 * (hi - lo) * size),
        name="grad_weight_part",
    )


def grad_inputs_kernel(count, has_total, parts, w_ref, *refs):
    blocks, outs = refs[:count], refs[count + has_total : count + has_total + parts]
    token, staged, all_ref = refs[-3:]
    token[...] = jnp.zeros_like(token)
    if count == 1:
        all_ref = blocks[0]
    else:
        pl.when(pl.program_id(0) == 0)(lambda: stack_blocks(blocks, all_ref))
    value = lax.dot_general(
        all_ref[...], w_ref[...], (((1,), (1,)), ((), ())), preferred_element_type=f32
    )
    if has_total:
        value = value + refs[count][...]
    if parts == 1:
        outs[0][...] = value.astype(outs[0].dtype)
        return
    staged[...] = value.astype(bf16)
    row, col = lax.axis_index("row"), lax.axis_index("col")
    rows = outs[0].shape[0]
    for k, out in enumerate(outs):
        at = pl.multiple_of(place_of(col ^ k, row) * rows, rows)
        out[...] = staged[pl.ds(at, rows), :]


def grad_inputs_part(weight, blocks, total, start, tokens, last, parts, lo, hi, dep=None):
    size = blocks[0].shape[1]
    tile = tile_of(hi - lo, lo, 512)
    count = len(blocks)
    operands = [weight, *blocks]
    in_specs = [pl.BlockSpec((tile, size), lambda j: (lo // tile + j, start // size))]
    in_specs += [whole(*b.shape) for b in blocks]
    if total is not None:
        operands.append(total)
        in_specs.append(pl.BlockSpec((tokens, tile), lambda j: (0, j)))
    rows = tokens // parts
    out_type = bf16 if last else f32
    return call(
        functools.partial(grad_inputs_kernel, count, total is not None, parts),
        operands,
        in_specs,
        dep,
        grid=((hi - lo) // tile,),
        out_specs=[pl.BlockSpec((rows, tile), lambda j: (0, j))] * parts + [whole(8, 128)],
        out_shape=[jax.ShapeDtypeStruct((rows, hi - lo), out_type)] * parts + [TOKEN],
        scratch_shapes=[pltpu.VMEM((tokens, tile), bf16), pltpu.VMEM((tokens, size), bf16)],
        compiler_params=params(),
        cost_estimate=cost(2 * tokens * (hi - lo) * size, 2 * (hi - lo) * size),
        name="grad_inputs_part",
    )


def call(kernel, operands, in_specs, dep, **options):
    count = len(operands)

    def ordered(*refs):
        kernel(*refs[:count], *refs[count + 1 :])

    if dep is None:
        return pl.pallas_call(kernel, in_specs=in_specs, **options)(*operands)
    in_specs = [*in_specs, pl.BlockSpec(memory_space=pl.ANY)]
    return pl.pallas_call(ordered, in_specs=in_specs, **options)(*operands, dep)


def combine(name, kernel, operands, outs, dep):
    vmem = pl.BlockSpec(memory_space=pltpu.VMEM)
    like = operands[0]
    moved = sum(o.size * 2 for o in operands)
    return call(
        kernel,
        operands,
        [vmem] * len(operands),
        dep,
        out_specs=[vmem] * outs,
        out_shape=[jax.ShapeDtypeStruct(like.shape, bf16)] * outs,
        compiler_params=params(16),
        cost_estimate=cost(moved, moved),
        name=name,
    )


def at_end():
    row = lax.axis_index("row")
    return (row == 0) | (row == 3)


def pick(out, at_ends, at_middles):
    end = at_end()

    @pl.when(end)
    def _():
        out[...] = at_ends[...]

    @pl.when(jnp.logical_not(end))
    def _():
        out[...] = at_middles[...]


def pass_on_kernel(a, out):
    out[...] = a[...]


def ends_in_kernel(far, mid_m, near_d, out, relay):
    pick(out, far, mid_m)
    relay[...] = near_d[...]


def copy_two_kernel(a, b, out_a, out_b):
    out_a[...] = a[...]
    out_b[...] = b[...]


def far_sum_kernel(mid, far_m, far, far_in, out, out_sum):
    pick(out, mid, far_m)
    out_sum[...] = far[...] + far_in[...]


def far_sum_only_kernel(mid, far, far_in, out, out_sum):
    out[...] = mid[...]
    out_sum[...] = far[...] + far_in[...]


def near_sum_kernel(near, far_sum, mid, mid_in, out, out_sum):
    end = at_end()
    out_sum[...] = mid[...] + mid_in[...]

    @pl.when(end)
    def _():
        out[...] = near[...]

    @pl.when(jnp.logical_not(end))
    def _():
        out[...] = near[...] + far_sum[...]


def gelu_kernel(own, near_sum, mid_sum, cotangent, hidden, delta):
    end = at_end()
    width = own.shape[1]
    step = 256 if width % 256 == 0 else width

    def body(j, carry):
        cols = pl.ds(pl.multiple_of(j * step, step), step)
        from_mid = jnp.where(end, 0.0, mid_sum[:, cols].astype(f32))
        preact = own[:, cols].astype(f32) + from_mid + near_sum[:, cols].astype(f32)
        value, slope = gelu_both(preact)
        hidden[:, cols] = value.astype(bf16)
        delta[:, cols] = (cotangent[:, cols].astype(f32) * slope).astype(bf16)
        return carry

    lax.fori_loop(0, width // step, body, 0)


def gather_inputs(inputs):
    across = send(inputs, "col", ACROSS)
    beside = send(inputs, "col", CORES)
    corner = send(across, "col", CORES)
    return (inputs, beside, across, corner)


def scatter_cols(pieces):
    keep, give, keep_far, give_far = pieces
    far_sum = keep_far + send(give_far, "col", CORES)
    across = send(far_sum, "col", ACROSS)
    near_sum = keep + send(give, "col", CORES)
    return (near_sum.astype(f32) + across.astype(f32)).astype(bf16)


class Work:
    def __init__(self):
        self.queue, self.token = [], None

    def add(self, kernel):
        self.queue.append(kernel)

    def run(self, dep):
        if self.queue:
            self.token = self.queue.pop(0)(dep)

    def step(self, name, kernel, operands, pairs):
        values = combine(name, kernel, operands, len(pairs), self.token)
        arrived = [send(value, PLANE, to) for value, to in zip(values, pairs)]
        self.run(values[0])
        return arrived


def on_line(inputs, weight, cotangent):
    depth, width = weight.shape
    tokens = 4 * inputs.shape[0]
    size = width // CHUNKS
    cuts = [depth * k // SPLIT for k in range(SPLIT + 1)]
    bounds = list(zip(cuts[:-1], cuts[1:]))
    work = Work()
    sums, delta, blocks, hidden = {}, {}, {}, {}
    state = {"total": [None] * SPLIT, "grad_weight": None}

    *sums[0], _, x = forward(gather_inputs(inputs), weight, 0, size, tokens, 4)

    def add_forward(k):
        def run(dep):
            *sums[k], token = forward(x, weight, k * size, size, tokens, 4, dep)
            return token

        work.add(run)

    def add_grads(k):
        def run_inputs(part, dep):
            state["total"][part], token = grad_inputs_part(
                weight, blocks[k], state["total"][part], k * size, tokens, False, 1, *bounds[part], dep
            )
            return token

        def run_weight(part, dep):
            state["grad_weight"], token = grad_weight_part(
                x, blocks[k], state["grad_weight"], k * size, width, *bounds[part], dep
            )
            return token

        for run in (run_inputs, run_weight):
            for part in range(SPLIT):
                work.add(functools.partial(run, part))

    for k in range(CHUNKS + 1):
        summing, gathering = k < CHUNKS, k > 0
        if k + 1 < CHUNKS:
            add_forward(k + 1)
        if gathering:
            near_d = send(delta[k - 1], PLANE, HALVES)
            mid_m = send(delta[k - 1], PLANE, MIDDLE)
            work.run(delta[k - 1])
        if summing:
            own, near, mid, far = sums[k]
        if summing and gathering:
            far_in, far_m = work.step("ends_in", ends_in_kernel, (far, mid_m, near_d), (HALVES, MIDDLE))
            mid_in, far_sum = work.step(
                "far_sum", far_sum_kernel, (mid, far_m, far, far_in), (HALVES, MIDDLE)
            )
            mid_e, far_e = far_in, mid_in
        elif summing:
            far_in = send(far, PLANE, HALVES)
            work.run(far)
            mid_in, far_sum = work.step(
                "far_sum", far_sum_only_kernel, (mid, far, far_in), (HALVES, MIDDLE)
            )
        else:
            mid_e, far_m = work.step("relay", copy_two_kernel, (mid_m, near_d), (HALVES, MIDDLE))
            (far_e,) = work.step("relay_far", pass_on_kernel, (far_m,), (HALVES,))
        if gathering:
            blocks[k - 1] = [delta[k - 1], near_d, mid_m, mid_e, far_m, far_e]
            if summing:
                add_grads(k - 1)
        if summing:
            near_sum, mid_sum = work.step(
                "near_sum", near_sum_kernel, (near, far_sum, mid, mid_in), (HALVES, MIDDLE)
            )
            part = cotangent[:, k * size : (k + 1) * size]
            hidden[k], delta[k] = combine(
                "gelu", gelu_kernel, (own, near_sum, mid_sum, part), 2, work.token
            )
    while work.queue:
        work.run(work.token)
    last = CHUNKS - 1
    halves = []
    for part, (lo, hi) in enumerate(bounds):
        *pieces, work.token = grad_inputs_part(
            weight, blocks[last], state["total"][part], last * size, tokens, True, 4, lo, hi, work.token
        )
        halves.append(scatter_cols(pieces))
    grad_weight, _ = grad_weight_part(
        x, blocks[last], state["grad_weight"], last * size, width, 0, depth, work.token
    )
    return (
        jnp.concatenate([hidden[k] for k in range(CHUNKS)], axis=1),
        jnp.concatenate(halves, axis=1),
        grad_weight,
    )


def on_any(inputs, weight, cotangent):
    depth, width = weight.shape
    x = lax.all_gather(inputs, "col", axis=0, tiled=True)
    tokens = x.shape[0]
    sums, _ = forward(x, weight, 0, width, tokens, 1)
    preact = lax.psum_scatter(sums, "row", scatter_dimension=0, tiled=True).astype(f32)
    value, slope = gelu_both(preact)
    delta = (cotangent.astype(f32) * slope).astype(bf16)
    blocks = [lax.all_gather(delta, "row", axis=0, tiled=True)]
    sums, _ = grad_inputs_part(weight, blocks, None, 0, tokens, True, 1, 0, depth)
    grad_inputs = lax.psum_scatter(sums, "col", scatter_dimension=0, tiled=True)
    grad_weight, _ = grad_weight_part(x, blocks, None, 0, width, 0, depth)
    return (value.astype(bf16), grad_inputs, grad_weight)


def solution(mesh):
    in_specs = (P(("groups", "col"), "row"), P("row", "col"), P(("groups", "row"), "col"))
    out_specs = (
        P(("groups", "row"), "col"),
        P(("groups", "col"), "row"),
        P(("groups", "row"), "col"),
    )
    fits = mesh.shape["row"] == 4 and mesh.shape["col"] == 4
    return jax.shard_map(
        on_line if fits else on_any,
        mesh=mesh,
        in_specs=in_specs,
        out_specs=out_specs,
        check_vma=False,
    )
```

time: 274 us -> 174 us (0.64)
  waiting for transfers between devices: 149 us -> 55.3 us
  Pallas kernels: 0 us -> 77.3 us
  matrix products: 57.5 us -> 0 us
  local copies, waits for them, and re-layouts: 48.5 us -> 1.07 us
  starting transfers between devices: 0.34 us -> 36.5 us
  between operations: 13.8 us -> 0.97 us
    all_gather x2 -> x0, waiting for transfers between devices: 87.5 us -> none  [the longest x1 63.5 us: on_device(): delta_all = lax.all_gather(delta_grad, 'row', axis=0, tiled=True)]
    pallas_call x0 -> x27, Pallas kernels: none -> 77.3 us  [the longest x26 69.5 us: call(): return pl.pallas_call(ordered, in_specs=in_specs, **options)(*operands, dep)]
    reduce_scatter x2 -> x0, waiting for transfers between devices: 60.4 us -> none  [the longest x1 60.4 us: on_device(): lax.psum_scatter(partial_value.astype(jnp.bfloat16), 'row', scatter_dimen...]
    dot_general x3 -> x0, matrix products: 57.5 us -> none  [the longest x1 21.5 us: on_device(): lax.dot_general(delta_all, weight, (((1,), (1,)), ((), ())), preferred_el...]
    ppermute x0 -> x35, waiting for transfers between devices: none -> 55.3 us  [send(): return lax.ppermute(value, axis, pairs)]
    unnamed x5 -> x4, local copies, waits for them, and re-layouts: 48.5 us -> 1 us
    ppermute x0 -> x35, starting transfers between devices: none -> 36.5 us  [send(): return lax.ppermute(value, axis, pairs)]
    convert_element_type x1 -> x2, other arithmetic: 3.44 us -> 0.15 us  [scatter_cols(): return (near_sum.astype(f32) + across.astype(f32)).astype(bf16)]
  transfers between devices with their start and end apart: 4 -> 35, of which waited for: 3 -> 14; matrix products, arithmetic and copies ran while one was open for 24% -> 1% of each run, Pallas kernels for 0% -> 36%
where the time goes in v1:
time: 174 us; the launch traced here: 173 us
  Pallas kernels  77.3 us (44%)
  waiting for transfers between devices  55.3 us (32%)
  starting transfers between devices  36.5 us (21%)
  other arithmetic  1.95 us (1%)
    pallas_call x26, Pallas kernels, call(): return pl.pallas_call(ordered, in_specs=in_specs, **options)(*operands, dep)  69.5 us
    ppermute x35, waiting for transfers between devices, send(): return lax.ppermute(value, axis, pairs)  55.3 us
    ppermute x35, starting transfers between devices, send(): return lax.ppermute(value, axis, pairs)  36.5 us
    pallas_call x1, Pallas kernels, call(): return pl.pallas_call(kernel, in_specs=in_specs, **options)(*operands)  7.83 us
  transfers between devices with their start and end apart: 35, of which 14 were waited for; matrix products, arithmetic and copies ran while one was open for 1% of the time, Pallas kernels for 36%

profile of v1, /device:TPU:0, one launch (start us, length us, event | category | flops | bytes accessed | tf_op | source)
XLA Modules:
  0.0 173.2 jit_solution(12008436331404119768)
XLA Ops:
  0.6 3.0 %collective-permute-start.1 = (bf16[64,3072]{1,0:T(8,128)(2,1)}, bf16[64,3072]{1,0:T(8,128)(2,1)S(1)}, u32[]{:S(2)}, u32[]{:S(2)}) collective-permute-start(bf16[64,3072]{1,0:T(8,128)(2,1)} %refs_0_.9), channel_id=1, source_target_pairs={{0,2},{2,0},{1,3},{3,1},{4,6},{6,4},{5,7},{7,5},{8,10},{10,8},{9,1... | collective-permute-start | bytes 1179656 | tf_op jit(solution)/shard_map/ppermute | solution.py:41
  3.6 9.3 %collective-permute-done.1.refs_2_ = bf16[64,3072]{1,0:T(8,128)(2,1)S(1)} collective-permute-done((bf16[64,3072]{1,0:T(8,128)(2,1)}, bf16[64,3072]{1,0:T(8,128)(2,1)S(1)}, u32[]{:S(2)}, u32[]{:S(2)}) %collective-permute-start.1) | collective-permute-done | bytes 393248 | tf_op jit(solution)/shard_map/ppermute | solution.py:41
  13.0 1.7 collective-permute-done.2.refs_3_
  14.7 1.0 copy-done
  15.7 7.8 %forward_sums.3 = (bf16[64,2048]{1,0:T(8,128)(2,1)S(1)}, bf16[64,2048]{1,0:T(8,128)(2,1)S(1)}, bf16[64,2048]{1,0:T(8,128)(2,1)S(1)}, bf16[64,2048]{1,0:T(8,128)(...) custom-call(bf16[3072,6144]{1,0:T(8,128)(2,1)} %refs_0_.17, bf16[64,3072]{1,0:T(8,128)(2,1)S(1)} %copy-done, ...), custom_call_target="tpu_custom_call" | custom-call | flops 3221225472 | bytes 12582912 | tf_op jit(solution)/shard_map/forward_sums/pallas_call | solution.py:247
  23.5 1.8 %collective-permute-start.3 = (bf16[64,2048]{1,0:T(8,128)(2,1)S(1)}, bf16[64,2048]{1,0:T(8,128)(2,1)S(1)}, u32[]{:S(2)}, u32[]{:S(2)}) collective-permute-start(bf16[64,2048]{1,0:T(8,128)(2,1)S(1)} %get-tuple-element.72.refs_2_.refs_1_), channel_id=1, source_target_pairs={{0,4},{1,5},{2,6},{3,7},{4,0},{5,1},{6,2},{7,3},{8,12},{9,13},{10,... | collective-permute-start | bytes 786440 | tf_op jit(solution)/shard_map/ppermute | solution.py:41
  25.3 7.1 %forward_sums.4 = (bf16[64,2048]{1,0:T(8,128)(2,1)S(1)}, bf16[64,2048]{1,0:T(8,128)(2,1)S(1)}, bf16[64,2048]{1,0:T(8,128)(2,1)S(1)}, bf16[64,2048]{1,0:T(8,128)(2,1)S(1)}, f32[8,128]{1,0:T(8,128)S(1)}) custom-call(bf16[3072,6144]{1,0:T(8,128)(2,1)} %refs_0_.17, bf16[256,3072]{1,0:T(8,128)(2,1)S(1)} %get-tuple-element.73.refs_1_.refs_0_, ...), custom_call_target="tpu_custom_call" | custom-call | flops 3221225472 | bytes 12582912 | tf_op jit(solution)/shard_map/forward_sums/pallas_call | solution.py:249
  32.5 0.1 collective-permute-start.4
  32.6 3.1 %collective-permute-start.5 = (bf16[64,2048]{1,0:T(8,128)(2,1)S(1)}, bf16[64,2048]{1,0:T(8,128)(2,1)S(1)}, u32[]{:S(2)}, u32[]{:S(2)}) collective-permute-start(bf16[64,2048]{1,0:T(8,128)(2,1)S(1)} %get-tuple-element.76), channel_id=1, source_target_pairs={{0,4},{1,5},{2,6},{3,7},{4,0},{5,1},{6,2},{7,3},{8,12},{9,13},{10,... | collective-permute-start | bytes 786440 | tf_op jit(solution)/shard_map/ppermute | solution.py:41
  35.7 6.0 %collective-permute-done.5.refs_3_ = bf16[64,2048]{1,0:T(8,128)(2,1)S(1)} collective-permute-done((bf16[64,2048]{1,0:T(8,128)(2,1)S(1)}, bf16[64,2048]{1,0:T(8,128)(2,1)S(1)}, u32[]{:S(2)}, u32[]{:S(2)}) %collective-permute-start.5) | collective-permute-done | bytes 262176 | tf_op jit(solution)/shard_map/ppermute | solution.py:41
  41.8 1.8 %collective-permute-start.6 = (bf16[64,2048]{1,0:T(8,128)(2,1)S(1)}, bf16[64,2048]{1,0:T(8,128)(2,1)S(1)}, u32[]{:S(2)}, u32[]{:S(2)}) collective-permute-start(bf16[64,2048]{1,0:T(8,128)(2,1)S(1)} %get-tuple-element.77), channel_id=1, source_target_pairs={{0,4},{1,5},{2,6},{3,7},{4,0},{5,1},{6,2},{7,3},{8,12},{9,13},{10,... | collective-permute-start | bytes 786440 | tf_op jit(solution)/shard_map/ppermute | solution.py:41
  43.7 5.4 %collective-permute-done.6.refs_1_ = bf16[64,2048]{1,0:T(8,128)(2,1)S(1)} collective-permute-done((bf16[64,2048]{1,0:T(8,128)(2,1)S(1)}, bf16[64,2048]{1,0:T(8,128)(2,1)S(1)}, u32[]{:S(2)}, u32[]{:S(2)}) %collective-permute-start.6) | collective-permute-done | bytes 262176 | tf_op jit(solution)/shard_map/ppermute | solution.py:41
  49.1 0.5 gelu.3
  49.6 2.6 %collective-permute-start.9 = (bf16[64,2048]{1,0:T(8,128)(2,1)S(1)}, bf16[64,2048]{1,0:T(8,128)(2,1)S(1)}, u32[]{:S(2)}, u32[]{:S(2)}) collective-permute-start(bf16[64,2048]{1,0:T(8,128)(2,1)S(1)} %get-tuple-element.84.refs_2_.refs_1_), channel_id=1, source_target_pairs={{0,4},{1,5},{2,6},{3,7},{4,0},{5,1},{6,2},{7,3},{8,12},{9,13},{10,... | collective-permute-start | bytes 786440 | tf_op jit(solution)/shard_map/ppermute | solution.py:41
  52.3 7.1 %forward_sums.5 = (bf16[64,2048]{1,0:T(8,128)(2,1)S(1)}, bf16[64,2048]{1,0:T(8,128)(2,1)S(1)}, bf16[64,2048]{1,0:T(8,128)(2,1)S(1)}, bf16[64,2048]{1,0:T(8,128)(2,1)S(1)}, f32[8,128]{1,0:T(8,128)S(1)}) custom-call(bf16[3072,6144]{1,0:T(8,128)(2,1)} %refs_0_.17, bf16[256,3072]{1,0:T(8,128)(2,1)S(1)} %get-tuple-element.73.refs_1_.refs_0_, ...), custom_call_target="tpu_custom_call" | custom-call | flops 3221225472 | bytes 12582912 | tf_op jit(solution)/shard_map/forward_sums/pallas_call | solution.py:249
  59.5 0.6 collective-permute-start.10
  60.0 1.6 collective-permute-start.11
  61.6 6.7 %collective-permute-done.11.refs_3_.refs_4_ = bf16[64,2048]{1,0:T(8,128)(2,1)S(1)} collective-permute-done((bf16[64,2048]{1,0:T(8,128)(2,1)S(1)}, bf16[64,2048]{1,0:T(8,128)(2,1)S(1)}, u32[]{:S(2)}, u32[]{:S(2)}) %collective-permute-start.11) | collective-permute-done | bytes 262176 | tf_op jit(solution)/shard_map/ppermute | solution.py:41
  68.4 0.1 collective-permute-start.12
  68.4 2.0 %collective-permute-start.13 = (bf16[64,2048]{1,0:T(8,128)(2,1)S(1)}, bf16[64,2048]{1,0:T(8,128)(2,1)S(1)}, u32[]{:S(2)}, u32[]{:S(2)}) collective-permute-start(bf16[64,2048]{1,0:T(8,128)(2,1)S(1)} %get-tuple-element.89), channel_id=1, source_target_pairs={{0,4},{1,5},{2,6},{3,7},{4,0},{5,1},{6,2},{7,3},{8,12},{9,13},{10,... | collective-permute-start | bytes 786440 | tf_op jit(solution)/shard_map/ppermute | solution.py:41
  70.5 6.7 %collective-permute-done.13.refs_3_.refs_6_ = bf16[64,2048]{1,0:T(8,128)(2,1)S(1)} collective-permute-done((bf16[64,2048]{1,0:T(8,128)(2,1)S(1)}, bf16[64,2048]{1,0:T(8,128)(2,1)S(1)}, u32[]{:S(2)}, u32[]{:S(2)}) %collective-permute-start.13) | collective-permute-done | bytes 262176 | tf_op jit(solution)/shard_map/ppermute | solution.py:41
  77.2 0.1 collective-permute-start.15
  77.3 2.0 %collective-permute-start.14 = (bf16[64,2048]{1,0:T(8,128)(2,1)S(1)}, bf16[64,2048]{1,0:T(8,128)(2,1)S(1)}, u32[]{:S(2)}, u32[]{:S(2)}) collective-permute-start(bf16[64,2048]{1,0:T(8,128)(2,1)S(1)} %get-tuple-element.90.refs_7_), channel_id=1, source_target_pairs={{0,4},{1,5},{2,6},{3,7},{4,0},{5,1},{6,2},{7,3},{8,12},{9,13},{10,... | collective-permute-start | bytes 786440 | tf_op jit(solution)/shard_map/ppermute | solution.py:41
  79.3 4.8 %grad_inputs_part.6 = (f32[256,1536]{1,0:T(8,128)S(1)}, f32[8,128]{1,0:T(8,128)S(1)}) custom-call(bf16[3072,6144]{1,0:T(8,128)(2,1)} %refs_0_.17, bf16[64,2048]{1,0:T(8,128)(2,1)S(1)} %get-tuple-element.84.refs_2_.refs_1_, bf16[64,2048]{1,0:T(8,128)(2,1)S(1)} %collective-permute-done.9.refs_2_, bf16[64,2048]{1,0:T(8,128)(2,1)S(1)} %collective-permute-done.8.refs_1_.refs_3_, ...), custom_call_target="tpu_custom_call" | custom-call | flops 1610612736 | bytes 6291456 | tf_op jit(solution)/shard_map/grad_inputs_part/pallas_call | solution.py:249
  84.2 1.9 %collective-permute-done.14.refs_1_ = bf16[64,2048]{1,0:T(8,128)(2,1)S(1)} collective-permute-done((bf16[64,2048]{1,0:T(8,128)(2,1)S(1)}, bf16[64,2048]{1,0:T(8,128)(2,1)S(1)}, u32[]{:S(2)}, u32[]{:S(2)}) %collective-permute-start.14) | collective-permute-done | bytes 262176 | tf_op jit(solution)/shard_map/ppermute | solution.py:41
  86.0 0.5 gelu.4
  86.6 0.7 collective-permute-start.17
  87.3 4.8 %grad_inputs_part.7 = (f32[256,1536]{1,0:T(8,128)S(1)}, f32[8,128]{1,0:T(8,128)S(1)}) custom-call(bf16[3072,6144]{1,0:T(8,128)(2,1)} %refs_0_.17, bf16[64,2048]{1,0:T(8,128)(2,1)S(1)} %get-tuple-element.84.refs_2_.refs_1_, bf16[64,2048]{1,0:T(8,128)(2,1)S(1)} %collective-permute-done.9.refs_2_, bf16[64,2048]{1,0:T(8,128)(2,1)S(1)} %collective-permute-done.8.refs_1_.refs_3_, ...), custom_call_target="tpu_custom_call" | custom-call | flops 1610612736 | bytes 6291456 | tf_op jit(solution)/shard_map/grad_inputs_part/pallas_call | solution.py:249
  92.1 2.4 %collective-permute-done.17.refs_2_ = bf16[64,2048]{1,0:T(8,128)(2,1)S(1)} collective-permute-done((bf16[64,2048]{1,0:T(8,128)(2,1)S(1)}, bf16[64,2048]{1,0:T(8,128)(2,1)S(1)}, u32[]{:S(2)}, u32[]{:S(2)}) %collective-permute-start.17) | collective-permute-done | bytes 262176 | tf_op jit(solution)/shard_map/ppermute | solution.py:41
  94.5 0.1 collective-permute-start.18
  94.6 3.5 %collective-permute-start.19 = (bf16[64,2048]{1,0:T(8,128)(2,1)S(1)}, bf16[64,2048]{1,0:T(8,128)(2,1)S(1)}, u32[]{:S(2)}, u32[]{:S(2)}) collective-permute-start(bf16[64,2048]{1,0:T(8,128)(2,1)S(1)} %get-tuple-element.101.refs_7_), channel_id=1, source_target_pairs={{0,4},{1,5},{2,6},{3,7},{4,0},{5,1},{6,2},{7,3},{8,12},{9,13},{10,... | collective-permute-start | bytes 786440 | tf_op jit(solution)/shard_map/ppermute | solution.py:41
  98.1 4.2 %grad_weight_part.5 = (bf16[3072,6144]{1,0:T(8,128)(2,1)}, f32[8,128]{1,0:T(8,128)S(1)}) custom-call(bf16[256,3072]{1,0:T(8,128)(2,1)S(1)} %get-tuple-element.73.refs_1_.refs_0_, bf16[64,2048]{1,0:T(8,128)(2,1)S(1)} %get-tuple-element.84.refs_2_.refs_1_, bf16[64,2048]{1,0:T(8,128)(2,1)S(1)} %collective-permute-done.9.refs_2_, ...), custom_call_target="tpu_custom_call" | custom-call | flops 1610612736 | bytes 6291456 | tf_op jit(solution)/shard_map/grad_weight_part/pallas_call | solution.py:249
  102.3 1.0 collective-permute-done.19.refs_3_.refs_4_
  103.4 0.1 collective-permute-start.20
  103.5 2.0 %collective-permute-start.21 = (bf16[64,2048]{1,0:T(8,128)(2,1)S(1)}, bf16[64,2048]{1,0:T(8,128)(2,1)S(1)}, u32[]{:S(2)}, u32[]{:S(2)}) collective-permute-start(bf16[64,2048]{1,0:T(8,128)(2,1)S(1)} %get-tuple-element.104.refs_8_), channel_id=1, source_target_pairs={{0,4},{1,5},{2,6},{3,7},{4,0},{5,1},{6,2},{7,3},{8,12},{9,13},{10,... | collective-permute-start | bytes 786440 | tf_op jit(solution)/shard_map/ppermute | solution.py:41
  105.5 4.2 %grad_weight_part.6 = (bf16[3072,6144]{1,0:T(8,128)(2,1)}, f32[8,128]{1,0:T(8,128)S(1)}) custom-call(bf16[256,3072]{1,0:T(8,128)(2,1)S(1)} %get-tuple-element.73.refs_1_.refs_0_, bf16[64,2048]{1,0:T(8,128)(2,1)S(1)} %get-tuple-element.84.refs_2_.refs_1_, bf16[64,2048]{1,0:T(8,128)(2,1)S(1)} %collective-permute-done.9.refs_2_, ...), custom_call_target="tpu_custom_call", output_to_operand_aliasing={{0}: (7, {})} | custom-call | flops 1610612736 | bytes 6291456 | tf_op jit(solution)/shard_map/grad_weight_part/pallas_call | solution.py:249
  109.7 2.5 %collective-permute-done.21.refs_3_.refs_6_ = bf16[64,2048]{1,0:T(8,128)(2,1)S(1)} collective-permute-done((bf16[64,2048]{1,0:T(8,128)(2,1)S(1)}, bf16[64,2048]{1,0:T(8,128)(2,1)S(1)}, u32[]{:S(2)}, u32[]{:S(2)}) %collective-permute-start.21) | collective-permute-done | bytes 262176 | tf_op jit(solution)/shard_map/ppermute | solution.py:41
  112.2 0.2 near_sum.5
  112.5 2.0 %collective-permute-start.22 = (bf16[64,2048]{1,0:T(8,128)(2,1)S(1)}, bf16[64,2048]{1,0:T(8,128)(2,1)S(1)}, u32[]{:S(2)}, u32[]{:S(2)}) collective-permute-start(bf16[64,2048]{1,0:T(8,128)(2,1)S(1)} %get-tuple-element.107.refs_8_), channel_id=1, source_target_pairs={{0,4},{1,5},{2,6},{3,7},{4,0},{5,1},{6,2},{7,3},{8,12},{9,13},{10,... | collective-permute-start | bytes 786440 | tf_op jit(solution)/shard_map/ppermute | solution.py:41
  114.5 4.8 %grad_inputs_part.8 = (f32[256,1536]{1,0:T(8,128)S(1)}, f32[8,128]{1,0:T(8,128)S(1)}) custom-call(bf16[3072,6144]{1,0:T(8,128)(2,1)} %refs_0_.17, bf16[64,2048]{1,0:T(8,128)(2,1)S(1)} %get-tuple-element.98.refs_7_.refs_1_, bf16[64,2048]{1,0:T(8,128)(2,1)S(1)} %collective-permute-done.17.refs_2_, ...), custom_call_target="tpu_custom_call" | custom-call | flops 1610612736 | bytes 6291456 | tf_op jit(solution)/shard_map/grad_inputs_part/pallas_call | solution.py:249
  119.4 1.9 %collective-permute-done.22.refs_1_ = bf16[64,2048]{1,0:T(8,128)(2,1)S(1)} collective-permute-done((bf16[64,2048]{1,0:T(8,128)(2,1)S(1)}, bf16[64,2048]{1,0:T(8,128)(2,1)S(1)}, u32[]{:S(2)}, u32[]{:S(2)}) %collective-permute-start.22) | collective-permute-done | bytes 262176 | tf_op jit(solution)/shard_map/ppermute | solution.py:41
  121.2 0.5 gelu.5
  121.8 0.1 collective-permute-start.25
  121.9 2.0 %collective-permute-start.24 = (bf16[64,2048]{1,0:T(8,128)(2,1)S(1)}, bf16[64,2048]{1,0:T(8,128)(2,1)S(1)}, u32[]{:S(2)}, u32[]{:S(2)}) collective-permute-start(bf16[64,2048]{1,0:T(8,128)(2,1)S(1)} %get-tuple-element.112.refs_8_.refs_1_), channel_id=1, source_target_pairs={{0,4},{1,5},{2,6},{3,7},{4,0},{5,1},{6,2},{7,3},{8,12},{9,13},{10,... | collective-permute-start | bytes 786440 | tf_op jit(solution)/shard_map/ppermute | solution.py:41
  123.9 4.8 %grad_inputs_part.9 = (f32[256,1536]{1,0:T(8,128)S(1)}, f32[8,128]{1,0:T(8,128)S(1)}) custom-call(bf16[3072,6144]{1,0:T(8,128)(2,1)} %refs_0_.17, bf16[64,2048]{1,0:T(8,128)(2,1)S(1)} %get-tuple-element.98.refs_7_.refs_1_, bf16[64,2048]{1,0:T(8,128)(2,1)S(1)} %collective-permute-done.17.refs_2_, ...), custom_call_target="tpu_custom_call" | custom-call | flops 1610612736 | bytes 6291456 | tf_op jit(solution)/shard_map/grad_inputs_part/pallas_call | solution.py:249
  128.7 1.9 %collective-permute-done.24.refs_1_.refs_2_ = bf16[64,2048]{1,0:T(8,128)(2,1)S(1)} collective-permute-done((bf16[64,2048]{1,0:T(8,128)(2,1)S(1)}, bf16[64,2048]{1,0:T(8,128)(2,1)S(1)}, u32[]{:S(2)}, u32[]{:S(2)}) %collective-permute-start.24) | collective-permute-done | bytes 262176 | tf_op jit(solution)/shard_map/ppermute | solution.py:41
  130.7 2.0 %collective-permute-start.26 = (bf16[64,2048]{1,0:T(8,128)(2,1)S(1)}, bf16[64,2048]{1,0:T(8,128)(2,1)S(1)}, u32[]{:S(2)}, u32[]{:S(2)}) collective-permute-start(bf16[64,2048]{1,0:T(8,128)(2,1)S(1)} %get-tuple-element.115.refs_8_), channel_id=1, source_target_pairs={{0,4},{1,5},{2,6},{3,7},{4,0},{5,1},{6,2},{7,3},{8,12},{9,13},{10,... | collective-permute-start | bytes 786440 | tf_op jit(solution)/shard_map/ppermute | solution.py:41
  132.7 4.2 %grad_weight_part.7 = (bf16[3072,6144]{1,0:T(8,128)(2,1)}, f32[8,128]{1,0:T(8,128)S(1)}) custom-call(bf16[256,3072]{1,0:T(8,128)(2,1)S(1)} %get-tuple-element.73.refs_1_.refs_0_, bf16[64,2048]{1,0:T(8,128)(2,1)S(1)} %get-tuple-element.98.refs_7_.refs_1_, bf16[64,2048]{1,0:T(8,128)(2,1)S(1)} %collective-permute-done.17.refs_2_, ...), custom_call_target="tpu_custom_call", output_to_operand_aliasing={{0}: (7, {})} | custom-call | flops 1610612736 | bytes 6291456 | tf_op jit(solution)/shard_map/grad_weight_part/pallas_call | solution.py:249
  137.0 1.7 %collective-permute-start.28 = (bf16[64,2048]{1,0:T(8,128)(2,1)S(1)}, bf16[64,2048]{1,0:T(8,128)(2,1)S(1)}, u32[]{:S(2)}, u32[]{:S(2)}) collective-permute-start(bf16[64,2048]{1,0:T(8,128)(2,1)S(1)} %relay_far.1.refs_8_), channel_id=1, source_target_pairs={{0,4},{1,5},{2,6},{3,7},{4,0},{5,1},{6,2},{7,3},{8,12},{9,13},{10,... | collective-permute-start | bytes 786440 | tf_op jit(solution)/shard_map/ppermute | solution.py:41
  138.7 4.2 %grad_weight_part.8 = (bf16[3072,6144]{1,0:T(8,128)(2,1)}, f32[8,128]{1,0:T(8,128)S(1)}) custom-call(bf16[256,3072]{1,0:T(8,128)(2,1)S(1)} %get-tuple-element.73.refs_1_.refs_0_, bf16[64,2048]{1,0:T(8,128)(2,1)S(1)} %get-tuple-element.98.refs_7_.refs_1_, bf16[64,2048]{1,0:T(8,128)(2,1)S(1)} %collective-permute-done.17.refs_2_, ...), custom_call_target="tpu_custom_call", output_to_operand_aliasing={{0}: (7, {})} | custom-call | flops 1610612736 | bytes 6291456 | tf_op jit(solution)/shard_map/grad_weight_part/pallas_call | solution.py:249
  143.0 2.1 %collective-permute-done.28.refs_6_ = bf16[64,2048]{1,0:T(8,128)(2,1)S(1)} collective-permute-done((bf16[64,2048]{1,0:T(8,128)(2,1)S(1)}, bf16[64,2048]{1,0:T(8,128)(2,1)S(1)}, u32[]{:S(2)}, u32[]{:S(2)}) %collective-permute-start.28) | collective-permute-done | bytes 262176 | tf_op jit(solution)/shard_map/ppermute | solution.py:41
  145.1 4.9 %grad_inputs_part.10 = (bf16[64,1536]{1,0:T(8,128)(2,1)S(1)}, bf16[64,1536]{1,0:T(8,128)(2,1)S(1)}, bf16[64,1536]{1,0:T(8,128)(2,1)S(1)}, bf16[64,1536]{1,0:T(8,128)(2,1)S(1)}, f32[8,128]{1,0:T(8,128)S(1)}) custom-call(bf16[3072,6144]{1,0:T(8,128)(2,1)} %refs_0_.17, bf16[64,2048]{1,0:T(8,128)(2,1)S(1)} %get-tuple-element.112.refs_8_.refs_1_, ...), custom_call_target="tpu_custom_call" | custom-call | flops 1610612736 | bytes 6291456 | tf_op jit(solution)/shard_map/grad_inputs_part/pallas_call | solution.py:249
  150.0 0.9 pad_maximum_fusion
  150.9 0.5 collective-permute-start.29
  151.4 4.9 %grad_inputs_part.11 = (bf16[64,1536]{1,0:T(8,128)(2,1)S(1)}, bf16[64,1536]{1,0:T(8,128)(2,1)S(1)}, bf16[64,1536]{1,0:T(8,128)(2,1)S(1)}, bf16[64,1536]{1,0:T(8,128)(2,1)S(1)}, f32[8,128]{1,0:T(8,128)S(1)}) custom-call(bf16[3072,6144]{1,0:T(8,128)(2,1)} %refs_0_.17, bf16[64,2048]{1,0:T(8,128)(2,1)S(1)} %get-tuple-element.112.refs_8_.refs_1_, ...), custom_call_target="tpu_custom_call" | custom-call | flops 1610612736 | bytes 6291456 | tf_op jit(solution)/shard_map/grad_inputs_part/pallas_call | solution.py:249
  156.3 0.1 collective-permute-start.32
  156.4 0.5 collective-permute-start.33
  157.0 1.6 collective-permute-start.31
  158.5 7.1 %grad_weight_part.9 = (bf16[3072,6144]{1,0:T(8,128)(2,1)}, f32[8,128]{1,0:T(8,128)}) custom-call(bf16[256,3072]{1,0:T(8,128)(2,1)S(1)} %get-tuple-element.73.refs_1_.refs_0_, bf16[64,2048]{1,0:T(8,128)(2,1)S(1)} %get-tuple-element.112.refs_8_.refs_1_, bf16[64,2048]{1,0:T(8,128)(2,1)S(1)} %collective-permute-done.24.refs_1_.refs_2_, ...), custom_call_target="tpu_custom_call", output_to_operand_aliasing={{0}: (7, {})} | custom-call | flops 3221225472 | bytes 12582912 | tf_op jit(solution)/shard_map/grad_weight_part/pallas_call | solution.py:249
  165.6 0.6 collective-permute-start.34
  166.3 0.1 add_convert_fusion.1
  166.3 6.0 %collective-permute-done.34 = bf16[64,1536]{1,0:T(8,128)(2,1)S(1)} collective-permute-done((bf16[64,1536]{1,0:T(8,128)(2,1)S(1)}, bf16[64,1536]{1,0:T(8,128)(2,1)S(1)}, u32[]{:S(2)}, u32[]{:S(2)}) %collective-permute-start.34) | collective-permute-done | bytes 196640 | tf_op jit(solution)/shard_map/ppermute | solution.py:41
  172.3 0.1 add_convert_fusion
  172.4 0.8 pad_maximum_fusion.1
  (44 shorter events, 0.8 us)
Async XLA Ops:
  0.6 12.3 %collective-permute-start.1 = (bf16[64,3072]{1,0:T(8,128)(2,1)}, bf16[64,3072]{1,0:T(8,128)(2,1)S(1)}, u32[]{:S(2)}, u32[]{:S(2)}) collective-permute-start(bf16[64,3072]{1,0:T(8,128)(2,1)} %refs_0_.9), channel_id=1, source_target_pairs={{0,2},{2,0},{1,3},{3,1},{4,6},{6,4},{5,7},{7,5},{8,10},{10,8},{9,1... | collective-permute-start | bytes 1179656 | tf_op jit(solution)/shard_map/ppermute | solution.py:41
  3.6 9.3 %collective-permute-start = (bf16[64,3072]{1,0:T(8,128)(2,1)}, bf16[64,3072]{1,0:T(8,128)(2,1)S(1)}, u32[]{:S(2)}, u32[]{:S(2)}) collective-permute-start(bf16[64,3072]{1,0:T(8,128)(2,1)} %refs_0_.9), channel_id=1, source_target_pairs={{0,1},{1,0},{2,3},{3,2},{4,5},{5,4},{6,7},{7,6},{8,9},{9,8},{10,11... | collective-permute-start | bytes 1179656 | tf_op jit(solution)/shard_map/ppermute | solution.py:41
  13.0 1.7 collective-permute-start.2
  14.7 1.0 copy-start
  23.5 9.0 %collective-permute-start.3 = (bf16[64,2048]{1,0:T(8,128)(2,1)S(1)}, bf16[64,2048]{1,0:T(8,128)(2,1)S(1)}, u32[]{:S(2)}, u32[]{:S(2)}) collective-permute-start(bf16[64,2048]{1,0:T(8,128)(2,1)S(1)} %get-tuple-element.72.refs_2_.refs_1_), channel_id=1, source_target_pairs={{0,4},{1,5},{2,6},{3,7},{4,0},{5,1},{6,2},{7,3},{8,12},{9,13},{10,... | collective-permute-start | bytes 786440 | tf_op jit(solution)/shard_map/ppermute | solution.py:41
  32.4 11.2 %copy-start.1 = (bf16[64,6144]{1,0:T(8,128)(2,1)S(1)}, bf16[64,6144]{1,0:T(8,128)(2,1)}, u32[]{:S(2)}) copy-start(bf16[64,6144]{1,0:T(8,128)(2,1)} %param.5) | copy-start | bytes 2359300
  32.5 3.2 %collective-permute-start.4 = (bf16[64,2048]{1,0:T(8,128)(2,1)S(1)}, bf16[64,2048]{1,0:T(8,128)(2,1)S(1)}, u32[]{:S(2)}, u32[]{:S(2)}) collective-permute-start(bf16[64,2048]{1,0:T(8,128)(2,1)S(1)} %get-tuple-element.75), channel_id=1, source_target_pairs={{0,1},{1,0},{2,3},{3,2},{4,8},{5,9},{6,10},{7,11},{8,4},{9,5},{10,... | collective-permute-start | bytes 786440 | tf_op jit(solution)/shard_map/ppermute | solution.py:41
  32.6 9.2 %collective-permute-start.5 = (bf16[64,2048]{1,0:T(8,128)(2,1)S(1)}, bf16[64,2048]{1,0:T(8,128)(2,1)S(1)}, u32[]{:S(2)}, u32[]{:S(2)}) collective-permute-start(bf16[64,2048]{1,0:T(8,128)(2,1)S(1)} %get-tuple-element.76), channel_id=1, source_target_pairs={{0,4},{1,5},{2,6},{3,7},{4,0},{5,1},{6,2},{7,3},{8,12},{9,13},{10,... | collective-permute-start | bytes 786440 | tf_op jit(solution)/shard_map/ppermute | solution.py:41
  41.8 7.3 %collective-permute-start.6 = (bf16[64,2048]{1,0:T(8,128)(2,1)S(1)}, bf16[64,2048]{1,0:T(8,128)(2,1)S(1)}, u32[]{:S(2)}, u32[]{:S(2)}) collective-permute-start(bf16[64,2048]{1,0:T(8,128)(2,1)S(1)} %get-tuple-element.77), channel_id=1, source_target_pairs={{0,4},{1,5},{2,6},{3,7},{4,0},{5,1},{6,2},{7,3},{8,12},{9,13},{10,... | collective-permute-start | bytes 786440 | tf_op jit(solution)/shard_map/ppermute | solution.py:41
  43.6 5.4 %collective-permute-start.7 = (bf16[64,2048]{1,0:T(8,128)(2,1)S(1)}, bf16[64,2048]{1,0:T(8,128)(2,1)S(1)}, u32[]{:S(2)}, u32[]{:S(2)}) collective-permute-start(bf16[64,2048]{1,0:T(8,128)(2,1)S(1)} %get-tuple-element.78), channel_id=1, source_target_pairs={{0,1},{1,0},{2,3},{3,2},{4,8},{5,9},{6,10},{7,11},{8,4},{9,5},{10,... | collective-permute-start | bytes 786440 | tf_op jit(solution)/shard_map/ppermute | solution.py:41
  49.6 9.7 %collective-permute-start.9 = (bf16[64,2048]{1,0:T(8,128)(2,1)S(1)}, bf16[64,2048]{1,0:T(8,128)(2,1)S(1)}, u32[]{:S(2)}, u32[]{:S(2)}) collective-permute-start(bf16[64,2048]{1,0:T(8,128)(2,1)S(1)} %get-tuple-element.84.refs_2_.refs_1_), channel_id=1, source_target_pairs={{0,4},{1,5},{2,6},{3,7},{4,0},{5,1},{6,2},{7,3},{8,12},{9,13},{10,... | collective-permute-start | bytes 786440 | tf_op jit(solution)/shard_map/ppermute | solution.py:41
  52.3 7.1 %collective-permute-start.8 = (bf16[64,2048]{1,0:T(8,128)(2,1)S(1)}, bf16[64,2048]{1,0:T(8,128)(2,1)S(1)}, u32[]{:S(2)}, u32[]{:S(2)}) collective-permute-start(bf16[64,2048]{1,0:T(8,128)(2,1)S(1)} %get-tuple-element.84.refs_2_.refs_1_), channel_id=1, source_target_pairs={{0,1},{1,0},{2,3},{3,2},{4,8},{5,9},{6,10},{7,11},{8,4},{9,5},{10,... | collective-permute-start | bytes 786440 | tf_op jit(solution)/shard_map/ppermute | solution.py:41
  59.5 2.2 %collective-permute-start.10 = (bf16[64,2048]{1,0:T(8,128)(2,1)S(1)}, bf16[64,2048]{1,0:T(8,128)(2,1)S(1)}, u32[]{:S(2)}, u32[]{:S(2)}) collective-permute-start(bf16[64,2048]{1,0:T(8,128)(2,1)S(1)} %get-tuple-element.86), channel_id=1, source_target_pairs={{0,1},{1,0},{2,3},{3,2},{4,8},{5,9},{6,10},{7,11},{8,4},{9,5},{10,... | collective-permute-start | bytes 786440 | tf_op jit(solution)/shard_map/ppermute | solution.py:41
  60.0 8.3 %collective-permute-start.11 = (bf16[64,2048]{1,0:T(8,128)(2,1)S(1)}, bf16[64,2048]{1,0:T(8,128)(2,1)S(1)}, u32[]{:S(2)}, u32[]{:S(2)}) collective-permute-start(bf16[64,2048]{1,0:T(8,128)(2,1)S(1)} %get-tuple-element.87), channel_id=1, source_target_pairs={{0,4},{1,5},{2,6},{3,7},{4,0},{5,1},{6,2},{7,3},{8,12},{9,13},{10,... | collective-permute-start | bytes 786440 | tf_op jit(solution)/shard_map/ppermute | solution.py:41
  68.4 2.1 %collective-permute-start.12 = (bf16[64,2048]{1,0:T(8,128)(2,1)S(1)}, bf16[64,2048]{1,0:T(8,128)(2,1)S(1)}, u32[]{:S(2)}, u32[]{:S(2)}) collective-permute-start(bf16[64,2048]{1,0:T(8,128)(2,1)S(1)} %get-tuple-element.88), channel_id=1, source_target_pairs={{0,1},{1,0},{2,3},{3,2},{4,8},{5,9},{6,10},{7,11},{8,4},{9,5},{10,... | collective-permute-start | bytes 786440 | tf_op jit(solution)/shard_map/ppermute | solution.py:41
  68.4 8.7 %collective-permute-start.13 = (bf16[64,2048]{1,0:T(8,128)(2,1)S(1)}, bf16[64,2048]{1,0:T(8,128)(2,1)S(1)}, u32[]{:S(2)}, u32[]{:S(2)}) collective-permute-start(bf16[64,2048]{1,0:T(8,128)(2,1)S(1)} %get-tuple-element.89), channel_id=1, source_target_pairs={{0,4},{1,5},{2,6},{3,7},{4,0},{5,1},{6,2},{7,3},{8,12},{9,13},{10,... | collective-permute-start | bytes 786440 | tf_op jit(solution)/shard_map/ppermute | solution.py:41
  77.2 6.9 %collective-permute-start.15 = (bf16[64,2048]{1,0:T(8,128)(2,1)S(1)}, bf16[64,2048]{1,0:T(8,128)(2,1)S(1)}, u32[]{:S(2)}, u32[]{:S(2)}) collective-permute-start(bf16[64,2048]{1,0:T(8,128)(2,1)S(1)} %get-tuple-element.91), channel_id=1, source_target_pairs={{0,1},{1,0},{2,3},{3,2},{4,8},{5,9},{6,10},{7,11},{8,4},{9,5},{10,... | collective-permute-start | bytes 786440 | tf_op jit(solution)/shard_map/ppermute | solution.py:41
  77.3 8.7 %collective-permute-start.14 = (bf16[64,2048]{1,0:T(8,128)(2,1)S(1)}, bf16[64,2048]{1,0:T(8,128)(2,1)S(1)}, u32[]{:S(2)}, u32[]{:S(2)}) collective-permute-start(bf16[64,2048]{1,0:T(8,128)(2,1)S(1)} %get-tuple-element.90.refs_7_), channel_id=1, source_target_pairs={{0,4},{1,5},{2,6},{3,7},{4,0},{5,1},{6,2},{7,3},{8,12},{9,13},{10,... | collective-permute-start | bytes 786440 | tf_op jit(solution)/shard_map/ppermute | solution.py:41
  86.6 7.9 %collective-permute-start.17 = (bf16[64,2048]{1,0:T(8,128)(2,1)S(1)}, bf16[64,2048]{1,0:T(8,128)(2,1)S(1)}, u32[]{:S(2)}, u32[]{:S(2)}) collective-permute-start(bf16[64,2048]{1,0:T(8,128)(2,1)S(1)} %get-tuple-element.98.refs_7_.refs_1_), channel_id=1, source_target_pairs={{0,4},{1,5},{2,6},{3,7},{4,0},{5,1},{6,2},{7,3},{8,12},{9,13},{10,... | collective-permute-start | bytes 786440 | tf_op jit(solution)/shard_map/ppermute | solution.py:41
  87.3 7.2 %collective-permute-start.16 = (bf16[64,2048]{1,0:T(8,128)(2,1)S(1)}, bf16[64,2048]{1,0:T(8,128)(2,1)S(1)}, u32[]{:S(2)}, u32[]{:S(2)}) collective-permute-start(bf16[64,2048]{1,0:T(8,128)(2,1)S(1)} %get-tuple-element.98.refs_7_.refs_1_), channel_id=1, source_target_pairs={{0,1},{1,0},{2,3},{3,2},{4,8},{5,9},{6,10},{7,11},{8,4},{9,5},{10,... | collective-permute-start | bytes 786440 | tf_op jit(solution)/shard_map/ppermute | solution.py:41
  94.5 7.8 %collective-permute-start.18 = (bf16[64,2048]{1,0:T(8,128)(2,1)S(1)}, bf16[64,2048]{1,0:T(8,128)(2,1)S(1)}, u32[]{:S(2)}, u32[]{:S(2)}) collective-permute-start(bf16[64,2048]{1,0:T(8,128)(2,1)S(1)} %get-tuple-element.100), channel_id=1, source_target_pairs={{0,1},{1,0},{2,3},{3,2},{4,8},{5,9},{6,10},{7,11},{8,4},{9,5},{10,... | collective-permute-start | bytes 786440 | tf_op jit(solution)/shard_map/ppermute | solution.py:41
  94.6 8.7 %collective-permute-start.19 = (bf16[64,2048]{1,0:T(8,128)(2,1)S(1)}, bf16[64,2048]{1,0:T(8,128)(2,1)S(1)}, u32[]{:S(2)}, u32[]{:S(2)}) collective-permute-start(bf16[64,2048]{1,0:T(8,128)(2,1)S(1)} %get-tuple-element.101.refs_7_), channel_id=1, source_target_pairs={{0,4},{1,5},{2,6},{3,7},{4,0},{5,1},{6,2},{7,3},{8,12},{9,13},{10,... | collective-permute-start | bytes 786440 | tf_op jit(solution)/shard_map/ppermute | solution.py:41
  103.4 6.3 %collective-permute-start.20 = (bf16[64,2048]{1,0:T(8,128)(2,1)S(1)}, bf16[64,2048]{1,0:T(8,128)(2,1)S(1)}, u32[]{:S(2)}, u32[]{:S(2)}) collective-permute-start(bf16[64,2048]{1,0:T(8,128)(2,1)S(1)} %get-tuple-element.103), channel_id=1, source_target_pairs={{0,1},{1,0},{2,3},{3,2},{4,8},{5,9},{6,10},{7,11},{8,4},{9,5},{10,... | collective-permute-start | bytes 786440 | tf_op jit(solution)/shard_map/ppermute | solution.py:41
  103.5 8.7 %collective-permute-start.21 = (bf16[64,2048]{1,0:T(8,128)(2,1)S(1)}, bf16[64,2048]{1,0:T(8,128)(2,1)S(1)}, u32[]{:S(2)}, u32[]{:S(2)}) collective-permute-start(bf16[64,2048]{1,0:T(8,128)(2,1)S(1)} %get-tuple-element.104.refs_8_), channel_id=1, source_target_pairs={{0,4},{1,5},{2,6},{3,7},{4,0},{5,1},{6,2},{7,3},{8,12},{9,13},{10,... | collective-permute-start | bytes 786440 | tf_op jit(solution)/shard_map/ppermute | solution.py:41
  112.4 6.9 %collective-permute-start.23 = (bf16[64,2048]{1,0:T(8,128)(2,1)S(1)}, bf16[64,2048]{1,0:T(8,128)(2,1)S(1)}, u32[]{:S(2)}, u32[]{:S(2)}) collective-permute-start(bf16[64,2048]{1,0:T(8,128)(2,1)S(1)} %get-tuple-element.108), channel_id=1, source_target_pairs={{0,1},{1,0},{2,3},{3,2},{4,8},{5,9},{6,10},{7,11},{8,4},{9,5},{10,... | collective-permute-start | bytes 786440 | tf_op jit(solution)/shard_map/ppermute | solution.py:41
  112.5 8.7 %collective-permute-start.22 = (bf16[64,2048]{1,0:T(8,128)(2,1)S(1)}, bf16[64,2048]{1,0:T(8,128)(2,1)S(1)}, u32[]{:S(2)}, u32[]{:S(2)}) collective-permute-start(bf16[64,2048]{1,0:T(8,128)(2,1)S(1)} %get-tuple-element.107.refs_8_), channel_id=1, source_target_pairs={{0,4},{1,5},{2,6},{3,7},{4,0},{5,1},{6,2},{7,3},{8,12},{9,13},{10,... | collective-permute-start | bytes 786440 | tf_op jit(solution)/shard_map/ppermute | solution.py:41
  121.8 6.9 %collective-permute-start.25 = (bf16[64,2048]{1,0:T(8,128)(2,1)S(1)}, bf16[64,2048]{1,0:T(8,128)(2,1)S(1)}, u32[]{:S(2)}, u32[]{:S(2)}) collective-permute-start(bf16[64,2048]{1,0:T(8,128)(2,1)S(1)} %get-tuple-element.112.refs_8_.refs_1_), channel_id=1, source_target_pairs={{0,1},{1,0},{2,3},{3,2},{4,8},{5,9},{6,10},{7,11},{8,4},{9,5},{10,... | collective-permute-start | bytes 786440 | tf_op jit(solution)/shard_map/ppermute | solution.py:41
  121.9 8.7 %collective-permute-start.24 = (bf16[64,2048]{1,0:T(8,128)(2,1)S(1)}, bf16[64,2048]{1,0:T(8,128)(2,1)S(1)}, u32[]{:S(2)}, u32[]{:S(2)}) collective-permute-start(bf16[64,2048]{1,0:T(8,128)(2,1)S(1)} %get-tuple-element.112.refs_8_.refs_1_), channel_id=1, source_target_pairs={{0,4},{1,5},{2,6},{3,7},{4,0},{5,1},{6,2},{7,3},{8,12},{9,13},{10,... | collective-permute-start | bytes 786440 | tf_op jit(solution)/shard_map/ppermute | solution.py:41
  130.6 6.3 %collective-permute-start.27 = (bf16[64,2048]{1,0:T(8,128)(2,1)S(1)}, bf16[64,2048]{1,0:T(8,128)(2,1)S(1)}, u32[]{:S(2)}, u32[]{:S(2)}) collective-permute-start(bf16[64,2048]{1,0:T(8,128)(2,1)S(1)} %get-tuple-element.116), channel_id=1, source_target_pairs={{0,1},{1,0},{2,3},{3,2},{4,8},{5,9},{6,10},{7,11},{8,4},{9,5},{10,... | collective-permute-start | bytes 786440 | tf_op jit(solution)/shard_map/ppermute | solution.py:41
  130.7 12.3 %collective-permute-start.26 = (bf16[64,2048]{1,0:T(8,128)(2,1)S(1)}, bf16[64,2048]{1,0:T(8,128)(2,1)S(1)}, u32[]{:S(2)}, u32[]{:S(2)}) collective-permute-start(bf16[64,2048]{1,0:T(8,128)(2,1)S(1)} %get-tuple-element.115.refs_8_), channel_id=1, source_target_pairs={{0,4},{1,5},{2,6},{3,7},{4,0},{5,1},{6,2},{7,3},{8,12},{9,13},{10,... | collective-permute-start | bytes 786440 | tf_op jit(solution)/shard_map/ppermute | solution.py:41
  137.0 8.1 %collective-permute-start.28 = (bf16[64,2048]{1,0:T(8,128)(2,1)S(1)}, bf16[64,2048]{1,0:T(8,128)(2,1)S(1)}, u32[]{:S(2)}, u32[]{:S(2)}) collective-permute-start(bf16[64,2048]{1,0:T(8,128)(2,1)S(1)} %relay_far.1.refs_8_), channel_id=1, source_target_pairs={{0,4},{1,5},{2,6},{3,7},{4,0},{5,1},{6,2},{7,3},{8,12},{9,13},{10,... | collective-permute-start | bytes 786440 | tf_op jit(solution)/shard_map/ppermute | solution.py:41
  149.9 7.0 %collective-permute-start.30 = (bf16[64,1536]{1,0:T(8,128)(2,1)S(1)}, bf16[64,1536]{1,0:T(8,128)(2,1)S(1)}, u32[]{:S(2)}, u32[]{:S(2)}) collective-permute-start(bf16[64,1536]{1,0:T(8,128)(2,1)S(1)} %get-tuple-element.125), channel_id=1, source_target_pairs={{0,1},{1,0},{2,3},{3,2},{4,5},{5,4},{6,7},{7,6},{8,9},{9,8},{10,11... | collective-permute-start | bytes 589832 | tf_op jit(solution)/shard_map/ppermute | solution.py:41
  150.9 15.3 %collective-permute-start.29 = (bf16[64,1536]{1,0:T(8,128)(2,1)S(1)}, bf16[64,1536]{1,0:T(8,128)(2,1)S(1)}, u32[]{:S(2)}, u32[]{:S(2)}) collective-permute-start(bf16[64,1536]{1,0:T(8,128)(2,1)S(1)} %get-tuple-element.123), channel_id=1, source_target_pairs={{0,1},{1,0},{2,3},{3,2},{4,5},{5,4},{6,7},{7,6},{8,9},{9,8},{10,11... | collective-permute-start | bytes 589832 | tf_op jit(solution)/shard_map/ppermute | solution.py:41
  156.3 10.0 %collective-permute-start.32 = (bf16[64,1536]{1,0:T(8,128)(2,1)S(1)}, bf16[64,1536]{1,0:T(8,128)(2,1)S(1)}, u32[]{:S(2)}, u32[]{:S(2)}) collective-permute-start(bf16[64,1536]{1,0:T(8,128)(2,1)S(1)} %get-tuple-element.129), channel_id=1, source_target_pairs={{0,1},{1,0},{2,3},{3,2},{4,5},{5,4},{6,7},{7,6},{8,9},{9,8},{10,11... | collective-permute-start | bytes 589832 | tf_op jit(solution)/shard_map/ppermute | solution.py:41
  156.4 9.2 %collective-permute-start.33 = (bf16[64,1536]{1,0:T(8,128)(2,1)S(1)}, bf16[64,1536]{1,0:T(8,128)(2,1)S(1)}, u32[]{:S(2)}, u32[]{:S(2)}) collective-permute-start(bf16[64,1536]{1,0:T(8,128)(2,1)S(1)} %get-tuple-element.131), channel_id=1, source_target_pairs={{0,1},{1,0},{2,3},{3,2},{4,5},{5,4},{6,7},{7,6},{8,9},{9,8},{10,11... | collective-permute-start | bytes 589832 | tf_op jit(solution)/shard_map/ppermute | solution.py:41
  157.0 9.3 %collective-permute-start.31 = (bf16[64,1536]{1,0:T(8,128)(2,1)S(1)}, bf16[64,1536]{1,0:T(8,128)(2,1)S(1)}, u32[]{:S(2)}, u32[]{:S(2)}) collective-permute-start(bf16[64,1536]{1,0:T(8,128)(2,1)S(1)} %add.19), channel_id=1, source_target_pairs={{0,2},{2,0},{1,3},{3,1},{4,6},{6,4},{5,7},{7,5},{8,10},{10,8},{9,1... | collective-permute-start | bytes 589832 | tf_op jit(solution)/shard_map/ppermute | solution.py:41
  165.6 6.7 %collective-permute-start.34 = (bf16[64,1536]{1,0:T(8,128)(2,1)S(1)}, bf16[64,1536]{1,0:T(8,128)(2,1)S(1)}, u32[]{:S(2)}, u32[]{:S(2)}) collective-permute-start(bf16[64,1536]{1,0:T(8,128)(2,1)S(1)} %add.22), channel_id=1, source_target_pairs={{0,2},{2,0},{1,3},{3,1},{4,6},{6,4},{5,7},{7,5},{8,10},{10,8},{9,1... | collective-permute-start | bytes 589832 | tf_op jit(solution)/shard_map/ppermute | solution.py:41

commit v2 on v0

v2 whole, which is shorter than its diff:
```python
import functools

import jax
import jax.numpy as jnp
from jax import lax
from jax.experimental import pallas as pl
from jax.experimental.pallas import tpu as pltpu
from jax.sharding import PartitionSpec as P

tanh_scale = 0.7978845608028654
cubic_coef = 0.044715
bf16 = jnp.bfloat16
f32 = jnp.float32
MIB = 1 << 20

CORES = ((0, 1), (1, 0), (2, 3), (3, 2))
ACROSS = ((0, 2), (2, 0), (1, 3), (3, 1))
PLANE = ("row", "col")
HALVES = tuple((4 * row + col, 4 * (row ^ 1) + col) for row in range(4) for col in range(4))
MIDDLE = tuple(
    (4 * row + col, 4 * (3 - row) + col if row in (1, 2) else 4 * row + (col ^ 1))
    for row in range(4)
    for col in range(4)
)

STREAMS = 2
ROUNDS = 2
SPLIT = 2


def gelu_both(preact):
    inner = tanh_scale * (preact + cubic_coef * preact * preact * preact)
    tangent = jnp.tanh(inner)
    value = 0.5 * preact * (1.0 + tangent)
    slope = 0.5 * (1.0 + tangent) + 0.5 * preact * (1.0 - tangent * tangent) * tanh_scale * (
        1.0 + 3.0 * cubic_coef * preact * preact
    )
    return value, slope


def send(value, axis, pairs):
    return lax.ppermute(value, axis, pairs)


def place_of(token_block, row):
    same_half = (token_block // 2) == (row // 2)
    return jnp.where(same_half, token_block ^ row, jnp.where(row < 2, token_block, 3 - token_block))


def params(limit=48):
    return pltpu.CompilerParams(vmem_limit_bytes=limit * MIB)


def cost(flops, bytes_accessed):
    return pl.CostEstimate(flops=int(flops), bytes_accessed=int(bytes_accessed), transcendentals=0)


def whole(*shape):
    return pl.BlockSpec(shape, lambda j: (0,) * len(shape))


def resident():
    return pl.BlockSpec(memory_space=pltpu.VMEM)


def tile_of(size, want):
    tile = want
    while size % tile:
        tile //= 2
    return tile


TILE = 512
UNROLL = True
TOKEN = jax.ShapeDtypeStruct((8, 128), f32)


def fetch(source, rows, columns, buffer, sems, tile, by_rows, i):
    at = pl.ds(pl.multiple_of(i * tile, tile), tile)
    if by_rows:
        part = source.at[pl.ds(pl.multiple_of(rows[0] + i * tile, tile), tile), pl.ds(*columns)]
        return pltpu.make_async_copy(part, buffer.at[at, :], sems.at[i])
    part = source.at[pl.ds(*rows), pl.ds(pl.multiple_of(columns[0] + i * tile, tile), tile)]
    return pltpu.make_async_copy(part, buffer.at[:, at], sems.at[i])


def each(count, body):
    def run(i, carry):
        body(i)
        return carry

    lax.fori_loop(0, count, run, 0)


def forward_kernel(start, tile, parts, first, w_ref, *refs):
    *refs, buffer, sems = refs
    depth, size = buffer.shape
    load = functools.partial(fetch, w_ref, (0, depth), (start, size), buffer, sems, tile, False)
    each(size // tile, lambda i: load(i).start())
    if first:
        pieces, outs, token, x_ref = refs[:parts], refs[parts : 2 * parts], refs[-2], refs[-1]
        rows = outs[0].shape[0]
        row, col = lax.axis_index("row"), lax.axis_index("col")
        for k, piece in enumerate(pieces):
            at = pl.multiple_of(place_of(col ^ k, row) * rows, rows)
            x_ref[pl.ds(at, rows), :] = piece[...]
    else:
        x_ref, *outs, token = refs
        rows = outs[0].shape[0]
    token[...] = jnp.zeros_like(token)

    def body(i):
        columns = pl.ds(pl.multiple_of(i * tile, tile), tile)
        load(i).wait()
        sums = jnp.dot(x_ref[...], buffer[:, columns], preferred_element_type=f32).astype(bf16)
        for k, out in enumerate(outs):
            out[:, columns] = sums[k * rows : (k + 1) * rows]

    each(size // tile, body)


def forward(x, weight, start, size, tokens, parts, dep=None):
    depth = weight.shape[0]
    tile = tile_of(size, TILE)
    rows = tokens // parts
    first = isinstance(x, tuple)
    operands = [weight, *x] if first else [weight, x]
    out_shape = [jax.ShapeDtypeStruct((rows, size), bf16)] * parts + [TOKEN]
    if first:
        out_shape.append(jax.ShapeDtypeStruct((tokens, depth), bf16))
    return call(
        functools.partial(forward_kernel, start, tile, parts, first),
        operands,
        [pl.BlockSpec(memory_space=pl.ANY)] + [resident()] * (len(operands) - 1),
        dep,
        out_specs=[resident()] * len(out_shape),
        out_shape=out_shape,
        scratch_shapes=[pltpu.VMEM((depth, size), bf16), pltpu.SemaphoreType.DMA((size // tile,))],
        compiler_params=params(36),
        cost_estimate=cost(2 * tokens * depth * size, 2 * depth * size),
        name="forward_sums",
    )


def stack_blocks(refs, all_ref):
    rows, width = refs[0].shape
    end = at_end()
    for q in range(len(refs) // 6):
        own, near, mid_m, mid_e, far_m, far_e = refs[6 * q : 6 * q + 6]
        columns = slice(q * width, (q + 1) * width)
        all_ref[0:rows, columns] = own[...]
        all_ref[rows : 2 * rows, columns] = near[...]

        @pl.when(jnp.logical_not(end))
        def _():
            all_ref[2 * rows : 3 * rows, columns] = mid_m[...]
            all_ref[3 * rows :, columns] = far_m[...]

        @pl.when(end)
        def _():
            all_ref[2 * rows : 3 * rows, columns] = mid_e[...]
            all_ref[3 * rows :, columns] = far_e[...]


def grads_kernel(names, start, lo, tile, *refs):
    ref = {}
    for name, one in zip(names, refs, strict=True):
        ref.setdefault(name, []).append(one)
    blocks, token = ref["block"], ref["token"][0]
    inputs, weight = "weight" in ref, "grad_weight" in ref
    delta = ref["delta"][0] if len(blocks) > 1 else blocks[0]
    size = delta.shape[1]
    tiles = (ref["loads"] if inputs else ref["stores"])[0].shape[0]
    hidden_copies = []
    if inputs:
        outs, before, w_tiles = ref["grad_inputs"], ref.get("before"), ref["weight_tiles"][0]
        load = functools.partial(
            fetch, ref["weight"][0], (lo, tiles * tile), (start, size), w_tiles, ref["loads"][0], tile, True
        )
        each(tiles, lambda i: load(i).start())
    for k, part in enumerate(ref.get("hidden", ())):
        columns = pl.ds(start + k * part.shape[1], part.shape[1])
        hidden_copies.append(
            pltpu.make_async_copy(part, ref["all_hidden"][0].at[:, columns], ref["hidden_sems"][0].at[k])
        )
        hidden_copies[-1].start()
    if len(blocks) > 1:
        stack_blocks(blocks, delta)
    token[...] = jnp.zeros_like(token)
    step = tile_of(size, 512)

    def store(i):
        at = pl.multiple_of(i * tile, tile)
        return pltpu.make_async_copy(
            ref["made_tiles"][0].at[pl.ds(at, tile), :],
            ref["grad_weight"][0].at[pl.ds(pl.multiple_of(lo + at, tile), tile), pl.ds(start, size)],
            ref["stores"][0].at[i],
        )

    def body(i):
        rows = pl.ds(pl.multiple_of(i * tile, tile), tile)
        if inputs:
            load(i).wait()
            value = lax.dot_general(
                delta[...], w_tiles[rows, :], (((1,), (1,)), ((), ())), preferred_element_type=f32
            )
            if before:
                value = value + before[0][:, rows]
            if len(outs) == 1:
                outs[0][:, rows] = value.astype(outs[0].dtype)
            else:
                staged = ref["staged"][0]
                staged[...] = value.astype(bf16)
                row, col = lax.axis_index("row"), lax.axis_index("col")
                tokens = outs[0].shape[0]
                for k, out in enumerate(outs):
                    at = pl.multiple_of(place_of(col ^ k, row) * tokens, tokens)
                    out[:, rows] = staged[pl.ds(at, tokens), :]
        if weight:
            x_t = ref["x"][0][:, pl.ds(pl.multiple_of(lo + i * tile, tile), tile)].T
            for at in range(0, size, step):
                ref["made_tiles"][0][rows, at : at + step] = jnp.dot(
                    x_t, delta[:, at : at + step], preferred_element_type=f32
                ).astype(bf16)
            store(i).start()

    if weight and UNROLL:
        for i in range(tiles):
            body(i)
    else:
        each(tiles, body)
    if weight:
        each(tiles, lambda i: store(i).wait())
    for copy in hidden_copies:
        copy.wait()


def grads(
    start, lo, hi, blocks, dep=None, *, weight=None, before=None, last=False, parts=1, x=None, into=None, hidden=(), all_hidden=None
):
    hbm = pl.BlockSpec(memory_space=pl.ANY)
    size = sum(b.shape[1] for b in blocks) if len(blocks) == 1 else blocks[0].shape[1] * (len(blocks) // 6)
    tokens = blocks[0].shape[0] * (4 if len(blocks) > 1 else 1)
    tile = tile_of(hi - lo, TILE)
    operands, outs, scratch, aliases = [], [], [], {}

    def give(name, value, spec=None):
        operands.append((name, value, spec or resident()))

    def make(name, shape, spec=None):
        outs.append((name, shape, spec or resident()))

    def carry(name, value):
        if not isinstance(value, jax.ShapeDtypeStruct):
            aliases[len(operands)] = len(outs)
            give(name + "_before", value, hbm)
        make(name, jax.ShapeDtypeStruct(value.shape, value.dtype), hbm)

    for block in blocks:
        give("block", block)
    if len(blocks) > 1:
        scratch.append(("delta", pltpu.VMEM((tokens, size), bf16)))
    tiles, sems = pltpu.VMEM((hi - lo, size), bf16), pltpu.SemaphoreType.DMA(((hi - lo) // tile,))
    if weight is not None:
        give("weight", weight, hbm)
        if before is not None:
            give("before", before)
        for _ in range(parts):
            make("grad_inputs", jax.ShapeDtypeStruct((tokens // parts, hi - lo), bf16 if last else f32))
        scratch += [("weight_tiles", tiles), ("loads", sems)]
        if parts > 1:
            scratch.append(("staged", pltpu.VMEM((tokens, tile), bf16)))
    if x is not None:
        give("x", x)
        carry("grad_weight", into)
        scratch += [("made_tiles", tiles), ("stores", sems)]
    if hidden:
        for part in hidden:
            give("hidden", part)
        carry("all_hidden", all_hidden)
        scratch.append(("hidden_sems", pltpu.SemaphoreType.DMA((len(hidden),))))
    make("token", TOKEN)
    names = [name for name, *_ in operands + outs + scratch]
    work = (weight is not None) + (x is not None)
    return call(
        functools.partial(grads_kernel, names, start, lo, tile),
        [value for _, value, _ in operands],
        [spec for *_, spec in operands],
        dep,
        out_specs=[spec for *_, spec in outs],
        out_shape=[shape for _, shape, _ in outs],
        scratch_shapes=[shape for _, shape in scratch],
        input_output_aliases=aliases,
        compiler_params=params(36),
        cost_estimate=cost(2 * work * tokens * (hi - lo) * size, 2 * work * (hi - lo) * size),
        name="grads",
    )


def call(kernel, operands, in_specs, dep, **options):
    count = len(operands)

    def ordered(*refs):
        kernel(*refs[:count], *refs[count + 1 :])

    if dep is None:
        return pl.pallas_call(kernel, in_specs=in_specs, **options)(*operands)
    in_specs = [*in_specs, pl.BlockSpec(memory_space=pl.ANY)]
    return pl.pallas_call(ordered, in_specs=in_specs, **options)(*operands, dep)


def combine(name, kernel, operands, outs, dep):
    vmem = pl.BlockSpec(memory_space=pltpu.VMEM)
    like = operands[0]
    moved = sum(o.size * 2 for o in operands)
    return call(
        kernel,
        operands,
        [vmem] * len(operands),
        dep,
        out_specs=[vmem] * outs,
        out_shape=[jax.ShapeDtypeStruct(like.shape, bf16)] * outs,
        compiler_params=params(16),
        cost_estimate=cost(moved, moved),
        name=name,
    )


def at_end():
    row = lax.axis_index("row")
    return (row == 0) | (row == 3)


def pick(out, at_ends, at_middles):
    end = at_end()

    @pl.when(end)
    def _():
        out[...] = at_ends[...]

    @pl.when(jnp.logical_not(end))
    def _():
        out[...] = at_middles[...]


def pass_on_kernel(a, out):
    out[...] = a[...]


def ends_in_kernel(far, mid_m, near_d, out, relay):
    pick(out, far, mid_m)
    relay[...] = near_d[...]


def copy_two_kernel(a, b, out_a, out_b):
    out_a[...] = a[...]
    out_b[...] = b[...]


def far_sum_kernel(mid, far_m, far, far_in, out, out_sum):
    pick(out, mid, far_m)
    out_sum[...] = far[...] + far_in[...]


def far_sum_only_kernel(mid, far, far_in, out, out_sum):
    out[...] = mid[...]
    out_sum[...] = far[...] + far_in[...]


def near_sum_kernel(near, far_sum, mid, mid_in, out, out_sum):
    end = at_end()
    out_sum[...] = mid[...] + mid_in[...]

    @pl.when(end)
    def _():
        out[...] = near[...]

    @pl.when(jnp.logical_not(end))
    def _():
        out[...] = near[...] + far_sum[...]


def gelu_kernel(own, near_sum, mid_sum, cotangent, hidden, delta):
    end = at_end()
    width = own.shape[1]
    step = 256 if width % 256 == 0 else width

    def body(j, carry):
        cols = pl.ds(pl.multiple_of(j * step, step), step)
        from_mid = jnp.where(end, 0.0, mid_sum[:, cols].astype(f32))
        preact = own[:, cols].astype(f32) + from_mid + near_sum[:, cols].astype(f32)
        value, slope = gelu_both(preact)
        hidden[:, cols] = value.astype(bf16)
        delta[:, cols] = (cotangent[:, cols].astype(f32) * slope).astype(bf16)
        return carry

    lax.fori_loop(0, width // step, body, 0)


def sum_kernel(a, b, out):
    out[...] = a[...] + b[...]


def finish_kernel(*refs):
    out = refs[-1]
    width = refs[0].shape[1]
    for k in range(SPLIT):
        keep, give, across = refs[3 * k : 3 * k + 3]
        out[:, k * width : (k + 1) * width] = (
            keep[...].astype(f32) + give[...].astype(f32) + across[...].astype(f32)
        ).astype(bf16)


def join(name, kernel, operands, shape, dep):
    moved = sum(o.size * 2 for o in operands)
    return call(
        kernel,
        list(operands),
        [resident()] * len(operands),
        dep,
        grid=(1,),
        out_specs=whole(*shape),
        out_shape=jax.ShapeDtypeStruct(shape, bf16),
        compiler_params=params(16),
        cost_estimate=cost(moved, moved),
        name=name,
    )


def gather_inputs(inputs):
    across = send(inputs, "col", ACROSS)
    (local,) = combine("local", pass_on_kernel, (inputs,), 1, None)
    beside = send(local, "col", CORES)
    corner = send(across, "col", CORES)
    return (local, beside, across, corner)


class Order:
    def __init__(self, plan):
        self.plan, self.steps, self.token = plan, 0, None

    def between(self, name, kernel, operands, outs=2):
        values = combine(name, kernel, operands, outs, self.token)
        self.token = values[0]
        return values

    def work(self):
        for kernel in self.plan.get(self.steps, ()):
            self.token = kernel(self.token)
        self.steps += 1


def on_line(inputs, weight, cotangent):
    depth, width = weight.shape
    tokens = 4 * inputs.shape[0]
    chunks = STREAMS * ROUNDS
    size = width // chunks
    cuts = [depth * k // SPLIT for k in range(SPLIT + 1)]
    bounds = list(zip(cuts[:-1], cuts[1:]))
    sums, delta, blocks, hidden = {}, {}, {}, {}
    total = [None] * SPLIT
    state = {
        "weight": jax.ShapeDtypeStruct(weight.shape, bf16),
        "hidden": jax.ShapeDtypeStruct(cotangent.shape, bf16),
    }
    plan = {}
    order = Order(plan)

    def forward_of(k):
        def run(dep):
            *sums[k], token = forward(x, weight, k * size, size, tokens, 4, dep)
            return token

        return run

    def grads_of(k, cut=SPLIT, part=0, both=True):
        def run(dep):
            mine = range(SPLIT) if cut == 1 else [part]
            more = {}
            if both:
                more = {"x": x, "into": state["weight"]}
                if part == 0:
                    more |= {"hidden": [hidden[k]], "all_hidden": state["hidden"]}
            lo, hi = bounds[mine[0]][0], bounds[mine[-1]][1]
            before = total[mine[0]]
            if before is not None and cut == 1:
                before = jnp.concatenate([total[p] for p in mine], axis=1)
            made = list(
                grads(k * size, lo, hi, blocks[k], dep, weight=weight, before=before, **more)
            )
            total[mine[0]] = made.pop(0)
            if both:
                state["weight"] = made.pop(0)
                if part == 0:
                    state["hidden"] = made.pop(0)
            return made.pop(0)

        return run

    def chain(mine):
        def exchange(values):
            return [send(value, PLANE, to) for value, to in zip(values, (HALVES, MIDDLE))]

        for at, k in enumerate([*mine, None]):
            before = mine[at - 1] if at else None
            if before is not None:
                own, near_sum, mid_sum = pending
                part = cotangent[:, before * size : (before + 1) * size]
                hidden[before], delta[before] = order.between(
                    "gelu", gelu_kernel, (own, near_sum, mid_sum, part)
                )
                near_d, mid_m = exchange((delta[before], delta[before]))
                order.work()
                yield
            if k is not None:
                own, near, mid, far = sums[k]
            if k is None:
                mid_e, far_m = exchange(order.between("relay", copy_two_kernel, (mid_m, near_d)))
                order.work()
                yield
                (far_e,) = exchange(order.between("relay_far", pass_on_kernel, (far_m,), 1))
            elif before is None:
                far_in = send(far, PLANE, HALVES)
                order.work()
                yield
                mid_in, far_sum = exchange(
                    order.between("far_sum", far_sum_only_kernel, (mid, far, far_in))
                )
            else:
                far_in, far_m = exchange(
                    order.between("ends_in", ends_in_kernel, (far, mid_m, near_d))
                )
                order.work()
                yield
                mid_in, far_sum = exchange(
                    order.between("far_sum", far_sum_kernel, (mid, far_m, far, far_in))
                )
                mid_e, far_e = far_in, mid_in
            if before is not None:
                blocks[before] = [delta[before], near_d, mid_m, mid_e, far_m, far_e]
            order.work()
            yield
            if k is not None:
                near_sum, mid_sum = exchange(
                    order.between("near_sum", near_sum_kernel, (near, far_sum, mid, mid_in))
                )
                pending = (own, near_sum, mid_sum)
                order.work()
                yield

    *sums[0], order.token, x = forward(gather_inputs(inputs), weight, 0, size, tokens, 4)
    plan.update(planned(forward_of, grads_of))
    chains = [chain(list(range(s, chunks, STREAMS))) for s in range(STREAMS)]
    live = list(chains)
    while live:
        for one in list(live):
            if next(one, live) is live:
                live.remove(one)

    final = chunks - 1
    for k in range(chunks - STREAMS, final):
        for part in range(SPLIT):
            order.token = grads_of(k, part=part, both=False)(order.token)
    parts, given = [], []
    for part, (lo, hi) in enumerate(bounds):
        *pieces, order.token = grads(
            final * size, lo, hi, blocks[final], order.token, weight=weight, before=total[part], last=True, parts=4
        )
        parts.append(pieces)
        given.append((send(pieces[3], "col", CORES), send(pieces[1], "col", CORES)))
    finals = []
    for (keep, _, keep_far, _), (far_in, near_in) in zip(parts, given):
        (far_sum,) = order.between("far_sum_col", sum_kernel, (keep_far, far_in), 1)
        finals += [keep, near_in, send(far_sum, "col", ACROSS)]
    late = range(chunks - STREAMS, chunks)
    grad_weight, all_hidden, order.token = grads(
        late[0] * size,
        0,
        depth,
        [block for k in late for block in blocks[k]],
        order.token,
        x=x,
        into=state["weight"],
        hidden=[hidden[k] for k in late],
        all_hidden=state["hidden"],
    )
    grad_inputs = join("finish", finish_kernel, finals, inputs.shape, order.token)
    return (all_hidden, grad_inputs, grad_weight)


def planned(forward_of, grads_of):
    return {
        0: [forward_of(1)],
        2: [forward_of(2)],
        4: [forward_of(3)],
        12: [grads_of(0, part=0)],
        14: [grads_of(0, part=1)],
        16: [grads_of(1, part=0)],
        18: [grads_of(1, part=1)],
    }


def on_any(inputs, weight, cotangent):
    depth, width = weight.shape
    x = lax.all_gather(inputs, "col", axis=0, tiled=True)
    tokens = x.shape[0]
    sums, _ = forward(x, weight, 0, width, tokens, 1)
    preact = lax.psum_scatter(sums, "row", scatter_dimension=0, tiled=True).astype(f32)
    value, slope = gelu_both(preact)
    delta = (cotangent.astype(f32) * slope).astype(bf16)
    blocks = [lax.all_gather(delta, "row", axis=0, tiled=True)]
    made = jax.ShapeDtypeStruct(weight.shape, bf16)
    sums, grad_weight, _ = grads(0, 0, depth, blocks, weight=weight, last=True, x=x, into=made)
    grad_inputs = lax.psum_scatter(sums, "col", scatter_dimension=0, tiled=True)
    return (value.astype(bf16), grad_inputs, grad_weight)


def solution(mesh):
    in_specs = (P(("groups", "col"), "row"), P("row", "col"), P(("groups", "row"), "col"))
    out_specs = (
        P(("groups", "row"), "col"),
        P(("groups", "col"), "row"),
        P(("groups", "row"), "col"),
    )
    fits = mesh.shape["row"] == 4 and mesh.shape["col"] == 4
    return jax.shard_map(
        on_line if fits else on_any,
        mesh=mesh,
        in_specs=in_specs,
        out_specs=out_specs,
        check_vma=False,
    )
```

time: 274 us -> 142 us (0.52)
  waiting for transfers between devices: 149 us -> 18.2 us
  Pallas kernels: 0 us -> 66.7 us
  matrix products: 57.5 us -> 0 us
  starting transfers between devices: 0.34 us -> 54.4 us
  local copies, waits for them, and re-layouts: 48.5 us -> 1.08 us
  between operations: 13.8 us -> 1.1 us
  other arithmetic: 3.44 us -> 0 us
    all_gather x2 -> x0, waiting for transfers between devices: 87.5 us -> none  [the longest x1 63.5 us: on_device(): delta_all = lax.all_gather(delta_grad, 'row', axis=0, tiled=True)]
    pallas_call x0 -> x35, Pallas kernels: none -> 66.7 us  [the longest x33 61.8 us: call(): return pl.pallas_call(ordered, in_specs=in_specs, **options)(*operands, dep)]
    reduce_scatter x2 -> x0, waiting for transfers between devices: 60.4 us -> none  [the longest x1 60.4 us: on_device(): lax.psum_scatter(partial_value.astype(jnp.bfloat16), 'row', scatter_dimen...]
    dot_general x3 -> x0, matrix products: 57.5 us -> none  [the longest x1 21.5 us: on_device(): lax.dot_general(delta_all, weight, (((1,), (1,)), ((), ())), preferred_el...]
    ppermute x0 -> x45, starting transfers between devices: none -> 54.4 us  [send(): return lax.ppermute(value, axis, pairs)]
    unnamed x5 -> x4, local copies, waits for them, and re-layouts: 48.5 us -> 1.03 us
    ppermute x0 -> x45, waiting for transfers between devices: none -> 18.2 us  [send(): return lax.ppermute(value, axis, pairs)]
    convert_element_type x1 -> x0, other arithmetic: 3.44 us -> none  [on_device(): (cotangent.astype(jnp.float32) * gelu_slope(preact)).astype(jnp.bfloat16)]
  transfers between devices with their start and end apart: 4 -> 45, of which waited for: 3 -> 11; matrix products, arithmetic and copies ran while one was open for 24% -> 0% of each run, Pallas kernels for 0% -> 41%
where the time goes in v2:
time: 142 us; the launch traced here: 141 us
  Pallas kernels  66.7 us (47%)
  starting transfers between devices  54.4 us (38%)
  waiting for transfers between devices  18.2 us (13%)
    pallas_call x33, Pallas kernels, call(): return pl.pallas_call(ordered, in_specs=in_specs, **options)(*operands, dep)  61.8 us
    ppermute x45, starting transfers between devices, send(): return lax.ppermute(value, axis, pairs)  54.4 us
    ppermute x45, waiting for transfers between devices, send(): return lax.ppermute(value, axis, pairs)  18.2 us
    pallas_call x2, Pallas kernels, call(): return pl.pallas_call(kernel, in_specs=in_specs, **options)(*operands)  4.95 us
  transfers between devices with their start and end apart: 45, of which 11 were waited for; matrix products, arithmetic and copies ran while one was open for 0% of the time, Pallas kernels for 41%

profile of v2, /device:TPU:0, one launch (start us, length us, event | category | flops | bytes accessed | tf_op | source)
XLA Modules:
  0.0 141.4 jit_solution(6566958326529548110)
XLA Ops:
  0.6 3.0 %collective-permute-start.1 = (bf16[64,3072]{1,0:T(8,128)(2,1)}, bf16[64,3072]{1,0:T(8,128)(2,1)S(1)}, u32[]{:S(2)}, u32[]{:S(2)}) collective-permute-start(bf16[64,3072]{1,0:T(8,128)(2,1)} %a.1), channel_id=1, source_target_pairs={{0,2},{2,0},{1,3},{3,1},{4,6},{6,4},{5,7},{7,5},{8,10},{10,8},{9,1... | collective-permute-start | bytes 1179656 | tf_op jit(solution)/shard_map/ppermute | solution.py:42
  3.6 1.0 copy-done
  4.7 0.1 collective-permute-start
  4.8 8.2 %collective-permute-done.1.refs_2_ = bf16[64,3072]{1,0:T(8,128)(2,1)S(1)} collective-permute-done((bf16[64,3072]{1,0:T(8,128)(2,1)}, bf16[64,3072]{1,0:T(8,128)(2,1)S(1)}, u32[]{:S(2)}, u32[]{:S(2)}) %collective-permute-start.1) | collective-permute-done | bytes 393248 | tf_op jit(solution)/shard_map/ppermute | solution.py:42
  13.0 1.7 %collective-permute-done.2.refs_3_ = bf16[64,3072]{1,0:T(8,128)(2,1)S(1)} collective-permute-done((bf16[64,3072]{1,0:T(8,128)(2,1)S(1)}, bf16[64,3072]{1,0:T(8,128)(2,1)S(1)}, u32[]{:S(2)}, u32[]{:S(2)}) %collective-permute-start.2) | collective-permute-done | bytes 393248 | tf_op jit(solution)/shard_map/ppermute | solution.py:42
  14.7 4.9 %forward_sums.4 = (bf16[64,1536]{1,0:T(8,128)(2,1)S(1)}, bf16[64,1536]{1,0:T(8,128)(2,1)S(1)}, bf16[64,1536]{1,0:T(8,128)(2,1)S(1)}, bf16[64,1536]{1,0:T(8,128)(...) custom-call(bf16[3072,6144]{1,0:T(8,128)(2,1)} %refs_6_.15, bf16[64,3072]{1,0:T(8,128)(2,1)S(1)} %local.1.refs_0_, ...), custom_call_target="tpu_custom_call" | custom-call | flops 2415919104 | bytes 9437184 | tf_op jit(solution)/shard_map/forward_sums/pallas_call | solution.py:307
  19.6 1.9 %collective-permute-start.3 = (bf16[64,1536]{1,0:T(8,128)(2,1)S(1)}, bf16[64,1536]{1,0:T(8,128)(2,1)S(1)}, u32[]{:S(2)}, u32[]{:S(2)}) collective-permute-start(bf16[64,1536]{1,0:T(8,128)(2,1)S(1)} %get-tuple-element.89.refs_1_), channel_id=1, source_target_pairs={{0,4},{1,5},{2,6},{3,7},{4,0},{5,1},{6,2},{7,3},{8,12},{9,13},{10,... | collective-permute-start | bytes 589832 | tf_op jit(solution)/shard_map/ppermute | solution.py:42
  21.5 4.9 %forward_sums.5 = (bf16[64,1536]{1,0:T(8,128)(2,1)S(1)}, bf16[64,1536]{1,0:T(8,128)(2,1)S(1)}, bf16[64,1536]{1,0:T(8,128)(2,1)S(1)}, bf16[64,1536]{1,0:T(8,128)(2,1)S(1)}, f32[8,128]{1,0:T(8,128)S(1)}) custom-call(bf16[3072,6144]{1,0:T(8,128)(2,1)} %refs_6_.15, bf16[256,3072]{1,0:T(8,128)(2,1)S(1)} %get-tuple-element.87.refs_1_.refs_7_.refs_8_.refs_12_, ...), custom_call_target="tpu_custom_call" | custom-call | flops 2415919104 | bytes 9437184 | tf_op jit(solution)/shard_map/forward_sums/pallas_call | solution.py:309
  26.4 0.3 collective-permute-start.6
  26.7 1.9 %collective-permute-start.5 = (bf16[64,1536]{1,0:T(8,128)(2,1)S(1)}, bf16[64,1536]{1,0:T(8,128)(2,1)S(1)}, u32[]{:S(2)}, u32[]{:S(2)}) collective-permute-start(bf16[64,1536]{1,0:T(8,128)(2,1)S(1)} %get-tuple-element.92.refs_2_), channel_id=1, source_target_pairs={{0,4},{1,5},{2,6},{3,7},{4,0},{5,1},{6,2},{7,3},{8,12},{9,13},{10,... | collective-permute-start | bytes 589832 | tf_op jit(solution)/shard_map/ppermute | solution.py:42
  28.6 4.9 %forward_sums.6 = (bf16[64,1536]{1,0:T(8,128)(2,1)S(1)}, bf16[64,1536]{1,0:T(8,128)(2,1)S(1)}, bf16[64,1536]{1,0:T(8,128)(2,1)S(1)}, bf16[64,1536]{1,0:T(8,128)(2,1)S(1)}, f32[8,128]{1,0:T(8,128)S(1)}) custom-call(bf16[3072,6144]{1,0:T(8,128)(2,1)} %refs_6_.15, bf16[256,3072]{1,0:T(8,128)(2,1)S(1)} %get-tuple-element.87.refs_1_.refs_7_.refs_8_.refs_12_, ...), custom_call_target="tpu_custom_call" | custom-call | flops 2415919104 | bytes 9437184 | tf_op jit(solution)/shard_map/forward_sums/pallas_call | solution.py:309
  33.6 0.7 collective-permute-done.6.refs_2_
  34.3 2.5 %collective-permute-start.10 = (bf16[64,1536]{1,0:T(8,128)(2,1)S(1)}, bf16[64,1536]{1,0:T(8,128)(2,1)S(1)}, u32[]{:S(2)}, u32[]{:S(2)}) collective-permute-start(bf16[64,1536]{1,0:T(8,128)(2,1)S(1)} %get-tuple-element.103.refs_4_), channel_id=1, source_target_pairs={{0,4},{1,5},{2,6},{3,7},{4,0},{5,1},{6,2},{7,3},{8,12},{9,13},{10,... | collective-permute-start | bytes 589832 | tf_op jit(solution)/shard_map/ppermute | solution.py:42
  36.9 1.0 collective-permute-done.5.refs_3_
  37.9 0.2 collective-permute-start.7
  38.1 5.0 %forward_sums.7 = (bf16[64,1536]{1,0:T(8,128)(2,1)S(1)}, bf16[64,1536]{1,0:T(8,128)(2,1)S(1)}, bf16[64,1536]{1,0:T(8,128)(2,1)S(1)}, bf16[64,1536]{1,0:T(8,128)(2,1)S(1)}, f32[8,128]{1,0:T(8,128)S(1)}) custom-call(bf16[3072,6144]{1,0:T(8,128)(2,1)} %refs_6_.15, bf16[256,3072]{1,0:T(8,128)(2,1)S(1)} %get-tuple-element.87.refs_1_.refs_7_.refs_8_.refs_12_, ...), custom_call_target="tpu_custom_call" | custom-call | flops 2415919104 | bytes 9437184 | tf_op jit(solution)/shard_map/forward_sums/pallas_call | solution.py:309
  43.2 3.8 %collective-permute-start.13 = (bf16[64,1536]{1,0:T(8,128)(2,1)S(1)}, bf16[64,1536]{1,0:T(8,128)(2,1)S(1)}, u32[]{:S(2)}, u32[]{:S(2)}) collective-permute-start(bf16[64,1536]{1,0:T(8,128)(2,1)S(1)} %get-tuple-element.109.refs_4_), channel_id=1, source_target_pairs={{0,4},{1,5},{2,6},{3,7},{4,0},{5,1},{6,2},{7,3},{8,12},{9,13},{10,... | collective-permute-start | bytes 589832 | tf_op jit(solution)/shard_map/ppermute | solution.py:42
  47.0 0.4 gelu.4
  47.5 0.6 collective-permute-start.11
  48.0 1.6 %collective-permute-start.12 = (bf16[64,1536]{1,0:T(8,128)(2,1)S(1)}, bf16[64,1536]{1,0:T(8,128)(2,1)S(1)}, u32[]{:S(2)}, u32[]{:S(2)}) collective-permute-start(bf16[64,1536]{1,0:T(8,128)(2,1)S(1)} %get-tuple-element.110.refs_0_), channel_id=1, source_target_pairs={{0,4},{1,5},{2,6},{3,7},{4,0},{5,1},{6,2},{7,3},{8,12},{9,13},{10,... | collective-permute-start | bytes 589832 | tf_op jit(solution)/shard_map/ppermute | solution.py:42
  49.6 1.0 collective-permute-done.13.refs_1_
  50.6 0.4 gelu.5
  51.0 0.1 collective-permute-start.17
  51.1 6.1 %collective-permute-start.18 = (bf16[64,1536]{1,0:T(8,128)(2,1)S(1)}, bf16[64,1536]{1,0:T(8,128)(2,1)S(1)}, u32[]{:S(2)}, u32[]{:S(2)}) collective-permute-start(bf16[64,1536]{1,0:T(8,128)(2,1)S(1)} %get-tuple-element.118.refs_0_), channel_id=1, source_target_pairs={{0,4},{1,5},{2,6},{3,7},{4,0},{5,1},{6,2},{7,3},{8,12},{9,13},{10,... | collective-permute-start | bytes 589832 | tf_op jit(solution)/shard_map/ppermute | solution.py:42
  57.2 0.1 collective-permute-start.15
  57.3 3.7 %collective-permute-start.16 = (bf16[64,1536]{1,0:T(8,128)(2,1)S(1)}, bf16[64,1536]{1,0:T(8,128)(2,1)S(1)}, u32[]{:S(2)}, u32[]{:S(2)}) collective-permute-start(bf16[64,1536]{1,0:T(8,128)(2,1)S(1)} %get-tuple-element.116.refs_3_), channel_id=1, source_target_pairs={{0,4},{1,5},{2,6},{3,7},{4,0},{5,1},{6,2},{7,3},{8,12},{9,13},{10,... | collective-permute-start | bytes 589832 | tf_op jit(solution)/shard_map/ppermute | solution.py:42
  61.0 0.3 collective-permute-done.18.refs_2_.refs_1_
  61.4 3.8 %collective-permute-start.22 = (bf16[64,1536]{1,0:T(8,128)(2,1)S(1)}, bf16[64,1536]{1,0:T(8,128)(2,1)S(1)}, u32[]{:S(2)}, u32[]{:S(2)}) collective-permute-start(bf16[64,1536]{1,0:T(8,128)(2,1)S(1)} %get-tuple-element.119.refs_4_), channel_id=1, source_target_pairs={{0,4},{1,5},{2,6},{3,7},{4,0},{5,1},{6,2},{7,3},{8,12},{9,13},{10,... | collective-permute-start | bytes 589832 | tf_op jit(solution)/shard_map/ppermute | solution.py:42
  65.2 0.3 collective-permute-done.16.refs_3_
  65.5 0.1 collective-permute-start.19
  65.6 3.8 %collective-permute-start.20 = (bf16[64,1536]{1,0:T(8,128)(2,1)S(1)}, bf16[64,1536]{1,0:T(8,128)(2,1)S(1)}, u32[]{:S(2)}, u32[]{:S(2)}) collective-permute-start(bf16[64,1536]{1,0:T(8,128)(2,1)S(1)} %get-tuple-element.121.refs_4_), channel_id=1, source_target_pairs={{0,4},{1,5},{2,6},{3,7},{4,0},{5,1},{6,2},{7,3},{8,12},{9,13},{10,... | collective-permute-start | bytes 589832 | tf_op jit(solution)/shard_map/ppermute | solution.py:42
  69.5 0.3 collective-permute-done.22.refs_3_
  69.8 0.1 collective-permute-start.25
  69.8 3.8 %collective-permute-start.26 = (bf16[64,1536]{1,0:T(8,128)(2,1)S(1)}, bf16[64,1536]{1,0:T(8,128)(2,1)S(1)}, u32[]{:S(2)}, u32[]{:S(2)}) collective-permute-start(bf16[64,1536]{1,0:T(8,128)(2,1)S(1)} %get-tuple-element.124.refs_4_), channel_id=1, source_target_pairs={{0,4},{1,5},{2,6},{3,7},{4,0},{5,1},{6,2},{7,3},{8,12},{9,13},{10,... | collective-permute-start | bytes 589832 | tf_op jit(solution)/shard_map/ppermute | solution.py:42
  73.7 0.2 collective-permute-done.20.refs_3_.refs_5_
  74.0 2.5 %collective-permute-start.23 = (bf16[64,1536]{1,0:T(8,128)(2,1)S(1)}, bf16[64,1536]{1,0:T(8,128)(2,1)S(1)}, u32[]{:S(2)}, u32[]{:S(2)}) collective-permute-start(bf16[64,1536]{1,0:T(8,128)(2,1)S(1)} %get-tuple-element.125.refs_9_), channel_id=1, source_target_pairs={{0,4},{1,5},{2,6},{3,7},{4,0},{5,1},{6,2},{7,3},{8,12},{9,13},{10,... | collective-permute-start | bytes 589832 | tf_op jit(solution)/shard_map/ppermute | solution.py:42
  76.5 5.7 %grads.9 = (f32[256,1536]{1,0:T(8,128)S(1)}, bf16[3072,6144]{1,0:T(8,128)(2,1)}, bf16[64,6144]{1,0:T(8,128)(2,1)}, f32[8,128]{1,0:T(8,128)S(1)}) custom-call(bf16[64,1536]{1,0:T(8,128)(2,1)S(1)} %get-tuple-element.110.refs_0_, bf16[64,1536]{1,0:T(8,128)(2,1)S(1)} %collective-permute-done.12.refs_2_.refs_1_, ...), custom_call_target="tpu_custom_call" | custom-call | flops 2415919104 | bytes 9437184 | tf_op jit(solution)/shard_map/grads/pallas_call | solution.py:309
  82.3 1.6 %collective-permute-start.29 = (bf16[64,1536]{1,0:T(8,128)(2,1)S(1)}, bf16[64,1536]{1,0:T(8,128)(2,1)S(1)}, u32[]{:S(2)}, u32[]{:S(2)}) collective-permute-start(bf16[64,1536]{1,0:T(8,128)(2,1)S(1)} %get-tuple-element.130.refs_4_), channel_id=1, source_target_pairs={{0,4},{1,5},{2,6},{3,7},{4,0},{5,1},{6,2},{7,3},{8,12},{9,13},{10,... | collective-permute-start | bytes 589832 | tf_op jit(solution)/shard_map/ppermute | solution.py:42
  83.9 0.4 gelu.6
  84.3 2.0 %collective-permute-start.27 = (bf16[64,1536]{1,0:T(8,128)(2,1)S(1)}, bf16[64,1536]{1,0:T(8,128)(2,1)S(1)}, u32[]{:S(2)}, u32[]{:S(2)}) collective-permute-start(bf16[64,1536]{1,0:T(8,128)(2,1)S(1)} %get-tuple-element.131.refs_0_), channel_id=1, source_target_pairs={{0,4},{1,5},{2,6},{3,7},{4,0},{5,1},{6,2},{7,3},{8,12},{9,13},{10,... | collective-permute-start | bytes 589832 | tf_op jit(solution)/shard_map/ppermute | solution.py:42
  86.3 5.7 %grads.10 = (f32[256,1536]{1,0:T(8,128)S(1)}, bf16[3072,6144]{1,0:T(8,128)(2,1)}, f32[8,128]{1,0:T(8,128)S(1)}) custom-call(bf16[64,1536]{1,0:T(8,128)(2,1)S(1)} %get-tuple-element.110.refs_0_, bf16[64,1536]{1,0:T(8,128)(2,1)S(1)} %collective-permute-done.12.refs_2_.refs_1_, ...), custom_call_target="tpu_custom_call", output_to_operand_aliasing={{1}: (8, {})} | custom-call | flops 2415919104 | bytes 9437184 | tf_op jit(solution)/shard_map/grads/pallas_call | solution.py:309
  92.0 0.4 gelu.7
  92.4 0.6 collective-permute-start.33
  93.0 1.6 %collective-permute-start.34 = (bf16[64,1536]{1,0:T(8,128)(2,1)S(1)}, bf16[64,1536]{1,0:T(8,128)(2,1)S(1)}, u32[]{:S(2)}, u32[]{:S(2)}) collective-permute-start(bf16[64,1536]{1,0:T(8,128)(2,1)S(1)} %get-tuple-element.140.refs_0_.refs_6_), channel_id=1, source_target_pairs={{0,4},{1,5},{2,6},{3,7},{4,0},{5,1},{6,2},{7,3},{8,12},{9,13},{10,... | collective-permute-start | bytes 589832 | tf_op jit(solution)/shard_map/ppermute | solution.py:42
  94.7 2.4 %collective-permute-start.31 = (bf16[64,1536]{1,0:T(8,128)(2,1)S(1)}, bf16[64,1536]{1,0:T(8,128)(2,1)S(1)}, u32[]{:S(2)}, u32[]{:S(2)}) collective-permute-start(bf16[64,1536]{1,0:T(8,128)(2,1)S(1)} %get-tuple-element.138.refs_12_), channel_id=1, source_target_pairs={{0,4},{1,5},{2,6},{3,7},{4,0},{5,1},{6,2},{7,3},{8,12},{9,13},{10,... | collective-permute-start | bytes 589832 | tf_op jit(solution)/shard_map/ppermute | solution.py:42
  97.1 5.7 %grads.11 = (f32[256,1536]{1,0:T(8,128)S(1)}, bf16[3072,6144]{1,0:T(8,128)(2,1)}, bf16[64,6144]{1,0:T(8,128)(2,1)}, f32[8,128]{1,0:T(8,128)S(1)}) custom-call(bf16[64,1536]{1,0:T(8,128)(2,1)S(1)} %get-tuple-element.118.refs_0_, bf16[64,1536]{1,0:T(8,128)(2,1)S(1)} %collective-permute-done.18.refs_2_.refs_1_, ...), custom_call_target="tpu_custom_call", output_to_operand_aliasing={{1}: (9, {}), {2}: (11, {})} | custom-call | flops 2415919104 | bytes 9437184 | tf_op jit(solution)/shard_map/grads/pallas_call | solution.py:309
  102.9 0.1 collective-permute-start.37
  103.0 0.6 collective-permute-start.36
  103.7 1.6 %collective-permute-start.35 = (bf16[64,1536]{1,0:T(8,128)(2,1)S(1)}, bf16[64,1536]{1,0:T(8,128)(2,1)S(1)}, u32[]{:S(2)}, u32[]{:S(2)}) collective-permute-start(bf16[64,1536]{1,0:T(8,128)(2,1)S(1)} %relay_far.2.refs_10_), channel_id=1, source_target_pairs={{0,4},{1,5},{2,6},{3,7},{4,0},{5,1},{6,2},{7,3},{8,12},{9,13},{10,... | collective-permute-start | bytes 589832 | tf_op jit(solution)/shard_map/ppermute | solution.py:42
  105.2 5.7 %grads.12 = (f32[256,1536]{1,0:T(8,128)S(1)}, bf16[3072,6144]{1,0:T(8,128)(2,1)}, f32[8,128]{1,0:T(8,128)S(1)}) custom-call(bf16[64,1536]{1,0:T(8,128)(2,1)S(1)} %get-tuple-element.118.refs_0_, bf16[64,1536]{1,0:T(8,128)(2,1)S(1)} %collective-permute-done.18.refs_2_.refs_1_, ...), custom_call_target="tpu_custom_call", output_to_operand_aliasing={{1}: (9, {})} | custom-call | flops 2415919104 | bytes 9437184 | tf_op jit(solution)/shard_map/grads/pallas_call | solution.py:309
  110.9 0.6 collective-permute-start.38
  111.5 3.5 %collective-permute-done.35.refs_5_ = bf16[64,1536]{1,0:T(8,128)(2,1)S(1)} collective-permute-done((bf16[64,1536]{1,0:T(8,128)(2,1)S(1)}, bf16[64,1536]{1,0:T(8,128)(2,1)S(1)}, u32[]{:S(2)}, u32[]{:S(2)}) %collective-permute-start.35) | collective-permute-done | bytes 196640 | tf_op jit(solution)/shard_map/ppermute | solution.py:42
  115.0 3.3 %grads.13 = (f32[256,1536]{1,0:T(8,128)S(1)}, f32[8,128]{1,0:T(8,128)S(1)}) custom-call(bf16[64,1536]{1,0:T(8,128)(2,1)S(1)} %get-tuple-element.131.refs_0_, bf16[64,1536]{1,0:T(8,128)(2,1)S(1)} %collective-permute-done.27.refs_1_, bf16[64,1536]{1,0:T(8,128)(2,1)S(1)} %collective-permute-done.28.refs_0_.refs_2_, ...), custom_call_target="tpu_custom_call" | custom-call | flops 1207959552 | bytes 4718592 | tf_op jit(solution)/shard_map/grads/pallas_call | solution.py:309
  118.3 3.3 %grads.14 = (f32[256,1536]{1,0:T(8,128)S(1)}, f32[8,128]{1,0:T(8,128)S(1)}) custom-call(bf16[64,1536]{1,0:T(8,128)(2,1)S(1)} %get-tuple-element.131.refs_0_, bf16[64,1536]{1,0:T(8,128)(2,1)S(1)} %collective-permute-done.27.refs_1_, bf16[64,1536]{1,0:T(8,128)(2,1)S(1)} %collective-permute-done.28.refs_0_.refs_2_, ...), custom_call_target="tpu_custom_call" | custom-call | flops 1207959552 | bytes 4718592 | tf_op jit(solution)/shard_map/grads/pallas_call | solution.py:309
  121.6 3.3 %grads.15 = (bf16[64,1536]{1,0:T(8,128)(2,1)S(1)}, bf16[64,1536]{1,0:T(8,128)(2,1)S(1)}, bf16[64,1536]{1,0:T(8,128)(2,1)S(1)}, bf16[64,1536]{1,0:T(8,128)(2,1)S(1)}, f32[8,128]{1,0:T(8,128)S(1)}) custom-call(bf16[64,1536]{1,0:T(8,128)(2,1)S(1)} %get-tuple-element.140.refs_0_.refs_6_, bf16[64,1536]{1,0:T(8,128)(2,1)S(1)} %collective-permute-done.34.refs_1_.refs_7_, ...), custom_call_target="tpu_custom_call" | custom-call | flops 1207959552 | bytes 4718592 | tf_op jit(solution)/shard_map/grads/pallas_call | solution.py:309
  125.0 3.3 %grads.16 = (bf16[64,1536]{1,0:T(8,128)(2,1)S(1)}, bf16[64,1536]{1,0:T(8,128)(2,1)S(1)}, bf16[64,1536]{1,0:T(8,128)(2,1)S(1)}, bf16[64,1536]{1,0:T(8,128)(2,1)S(1)}, f32[8,128]{1,0:T(8,128)S(1)}) custom-call(bf16[64,1536]{1,0:T(8,128)(2,1)S(1)} %get-tuple-element.140.refs_0_.refs_6_, bf16[64,1536]{1,0:T(8,128)(2,1)S(1)} %collective-permute-done.34.refs_1_.refs_7_, ...), custom_call_target="tpu_custom_call" | custom-call | flops 1207959552 | bytes 4718592 | tf_op jit(solution)/shard_map/grads/pallas_call | solution.py:309
  128.3 0.6 collective-permute-start.39
  128.8 0.1 collective-permute-start.43
  128.9 0.4 collective-permute-start.41
  129.4 1.5 %collective-permute-start.42 = (bf16[64,1536]{1,0:T(8,128)(2,1)S(1)}, bf16[64,1536]{1,0:T(8,128)(2,1)S(1)}, u32[]{:S(2)}, u32[]{:S(2)}) collective-permute-start(bf16[64,1536]{1,0:T(8,128)(2,1)S(1)} %far_sum_col.2.refs_2_), channel_id=1, source_target_pairs={{0,2},{2,0},{1,3},{3,1},{4,6},{6,4},{5,7},{7,5},{8,10},{10,8},{9,1... | collective-permute-start | bytes 589832 | tf_op jit(solution)/shard_map/ppermute | solution.py:42
  130.9 0.6 collective-permute-start.44
  131.6 8.0 %grads.17 = (bf16[3072,6144]{1,0:T(8,128)(2,1)}, bf16[64,6144]{1,0:T(8,128)(2,1)}, f32[8,128]{1,0:T(8,128)S(1)}) custom-call(bf16[64,1536]{1,0:T(8,128)(2,1)S(1)} %get-tuple-element.131.refs_0_, bf16[64,1536]{1,0:T(8,128)(2,1)S(1)} %collective-permute-done.27.refs_1_, ...), custom_call_target="tpu_custom_call", output_to_operand_aliasing={{0}: (13, {}), {1}: (16, {})} | custom-call | flops 4831838208 | bytes 18874368 | tf_op jit(solution)/shard_map/grads/pallas_call | solution.py:309
  139.6 0.9 collective-permute-done.44.refs_5_
  140.5 0.9 finish.1
  (66 shorter events, 0.9 us)
Async XLA Ops:
  0.6 12.3 %collective-permute-start.1 = (bf16[64,3072]{1,0:T(8,128)(2,1)}, bf16[64,3072]{1,0:T(8,128)(2,1)S(1)}, u32[]{:S(2)}, u32[]{:S(2)}) collective-permute-start(bf16[64,3072]{1,0:T(8,128)(2,1)} %a.1), channel_id=1, source_target_pairs={{0,2},{2,0},{1,3},{3,1},{4,6},{6,4},{5,7},{7,5},{8,10},{10,8},{9,1... | collective-permute-start | bytes 1179656 | tf_op jit(solution)/shard_map/ppermute | solution.py:42
  3.6 1.0 copy-start
  4.7 8.3 %collective-permute-start = (bf16[64,3072]{1,0:T(8,128)(2,1)S(1)}, bf16[64,3072]{1,0:T(8,128)(2,1)S(1)}, u32[]{:S(2)}, u32[]{:S(2)}) collective-permute-start(bf16[64,3072]{1,0:T(8,128)(2,1)S(1)} %local.1.refs_0_), channel_id=1, source_target_pairs={{0,1},{1,0},{2,3},{3,2},{4,5},{5,4},{6,7},{7,6},{8,9},{9,8},{10,11... | collective-permute-start | bytes 1179656 | tf_op jit(solution)/shard_map/ppermute | solution.py:42
  13.0 1.7 %collective-permute-start.2 = (bf16[64,3072]{1,0:T(8,128)(2,1)S(1)}, bf16[64,3072]{1,0:T(8,128)(2,1)S(1)}, u32[]{:S(2)}, u32[]{:S(2)}) collective-permute-start(bf16[64,3072]{1,0:T(8,128)(2,1)S(1)} %collective-permute-done.1.refs_2_), channel_id=1, source_target_pairs={{0,1},{1,0},{2,3},{3,2},{4,5},{5,4},{6,7},{7,6},{8,9},{9,8},{10,11... | collective-permute-start | bytes 1179656 | tf_op jit(solution)/shard_map/ppermute | solution.py:42
  19.6 7.1 %collective-permute-start.3 = (bf16[64,1536]{1,0:T(8,128)(2,1)S(1)}, bf16[64,1536]{1,0:T(8,128)(2,1)S(1)}, u32[]{:S(2)}, u32[]{:S(2)}) collective-permute-start(bf16[64,1536]{1,0:T(8,128)(2,1)S(1)} %get-tuple-element.89.refs_1_), channel_id=1, source_target_pairs={{0,4},{1,5},{2,6},{3,7},{4,0},{5,1},{6,2},{7,3},{8,12},{9,13},{10,... | collective-permute-start | bytes 589832 | tf_op jit(solution)/shard_map/ppermute | solution.py:42
  26.4 7.9 %collective-permute-start.6 = (bf16[64,1536]{1,0:T(8,128)(2,1)S(1)}, bf16[64,1536]{1,0:T(8,128)(2,1)S(1)}, u32[]{:S(2)}, u32[]{:S(2)}) collective-permute-start(bf16[64,1536]{1,0:T(8,128)(2,1)S(1)} %get-tuple-element.101.refs_1_), channel_id=1, source_target_pairs={{0,4},{1,5},{2,6},{3,7},{4,0},{5,1},{6,2},{7,3},{8,12},{9,13},{10,... | collective-permute-start | bytes 589832 | tf_op jit(solution)/shard_map/ppermute | solution.py:42
  26.7 11.1 %collective-permute-start.5 = (bf16[64,1536]{1,0:T(8,128)(2,1)S(1)}, bf16[64,1536]{1,0:T(8,128)(2,1)S(1)}, u32[]{:S(2)}, u32[]{:S(2)}) collective-permute-start(bf16[64,1536]{1,0:T(8,128)(2,1)S(1)} %get-tuple-element.92.refs_2_), channel_id=1, source_target_pairs={{0,4},{1,5},{2,6},{3,7},{4,0},{5,1},{6,2},{7,3},{8,12},{9,13},{10,... | collective-permute-start | bytes 589832 | tf_op jit(solution)/shard_map/ppermute | solution.py:42
  28.6 9.2 %collective-permute-start.4 = (bf16[64,1536]{1,0:T(8,128)(2,1)S(1)}, bf16[64,1536]{1,0:T(8,128)(2,1)S(1)}, u32[]{:S(2)}, u32[]{:S(2)}) collective-permute-start(bf16[64,1536]{1,0:T(8,128)(2,1)S(1)} %get-tuple-element.99), channel_id=1, source_target_pairs={{0,1},{1,0},{2,3},{3,2},{4,8},{5,9},{6,10},{7,11},{8,4},{9,5},{10,... | collective-permute-start | bytes 589832 | tf_op jit(solution)/shard_map/ppermute | solution.py:42
  34.3 8.8 %collective-permute-start.10 = (bf16[64,1536]{1,0:T(8,128)(2,1)S(1)}, bf16[64,1536]{1,0:T(8,128)(2,1)S(1)}, u32[]{:S(2)}, u32[]{:S(2)}) collective-permute-start(bf16[64,1536]{1,0:T(8,128)(2,1)S(1)} %get-tuple-element.103.refs_4_), channel_id=1, source_target_pairs={{0,4},{1,5},{2,6},{3,7},{4,0},{5,1},{6,2},{7,3},{8,12},{9,13},{10,... | collective-permute-start | bytes 589832 | tf_op jit(solution)/shard_map/ppermute | solution.py:42
  36.9 6.3 %collective-permute-start.9 = (bf16[64,1536]{1,0:T(8,128)(2,1)S(1)}, bf16[64,1536]{1,0:T(8,128)(2,1)S(1)}, u32[]{:S(2)}, u32[]{:S(2)}) collective-permute-start(bf16[64,1536]{1,0:T(8,128)(2,1)S(1)} %get-tuple-element.107), channel_id=1, source_target_pairs={{0,1},{1,0},{2,3},{3,2},{4,8},{5,9},{6,10},{7,11},{8,4},{9,5},{10,... | collective-permute-start | bytes 589832 | tf_op jit(solution)/shard_map/ppermute | solution.py:42
  37.9 9.1 %collective-permute-start.7 = (bf16[64,1536]{1,0:T(8,128)(2,1)S(1)}, bf16[64,1536]{1,0:T(8,128)(2,1)S(1)}, u32[]{:S(2)}, u32[]{:S(2)}) collective-permute-start(bf16[64,1536]{1,0:T(8,128)(2,1)S(1)} %get-tuple-element.104.refs_2_), channel_id=1, source_target_pairs={{0,4},{1,5},{2,6},{3,7},{4,0},{5,1},{6,2},{7,3},{8,12},{9,13},{10,... | collective-permute-start | bytes 589832 | tf_op jit(solution)/shard_map/ppermute | solution.py:42
  38.1 8.8 %copy-start.1 = (bf16[64,6144]{1,0:T(8,128)(2,1)S(1)}, bf16[64,6144]{1,0:T(8,128)(2,1)}, u32[]{:S(2)}) copy-start(bf16[64,6144]{1,0:T(8,128)(2,1)} %param.5) | copy-start | bytes 2359300
  38.1 8.9 %collective-permute-start.8 = (bf16[64,1536]{1,0:T(8,128)(2,1)S(1)}, bf16[64,1536]{1,0:T(8,128)(2,1)S(1)}, u32[]{:S(2)}, u32[]{:S(2)}) collective-permute-start(bf16[64,1536]{1,0:T(8,128)(2,1)S(1)} %get-tuple-element.105), channel_id=1, source_target_pairs={{0,1},{1,0},{2,3},{3,2},{4,8},{5,9},{6,10},{7,11},{8,4},{9,5},{10,... | collective-permute-start | bytes 589832 | tf_op jit(solution)/shard_map/ppermute | solution.py:42
  43.2 7.4 %collective-permute-start.13 = (bf16[64,1536]{1,0:T(8,128)(2,1)S(1)}, bf16[64,1536]{1,0:T(8,128)(2,1)S(1)}, u32[]{:S(2)}, u32[]{:S(2)}) collective-permute-start(bf16[64,1536]{1,0:T(8,128)(2,1)S(1)} %get-tuple-element.109.refs_4_), channel_id=1, source_target_pairs={{0,4},{1,5},{2,6},{3,7},{4,0},{5,1},{6,2},{7,3},{8,12},{9,13},{10,... | collective-permute-start | bytes 589832 | tf_op jit(solution)/shard_map/ppermute | solution.py:42
  47.0 3.7 %collective-permute-start.14 = (bf16[64,1536]{1,0:T(8,128)(2,1)S(1)}, bf16[64,1536]{1,0:T(8,128)(2,1)S(1)}, u32[]{:S(2)}, u32[]{:S(2)}) collective-permute-start(bf16[64,1536]{1,0:T(8,128)(2,1)S(1)} %get-tuple-element.112), channel_id=1, source_target_pairs={{0,1},{1,0},{2,3},{3,2},{4,8},{5,9},{6,10},{7,11},{8,4},{9,5},{10,... | collective-permute-start | bytes 589832 | tf_op jit(solution)/shard_map/ppermute | solution.py:42
  47.5 9.7 %collective-permute-start.11 = (bf16[64,1536]{1,0:T(8,128)(2,1)S(1)}, bf16[64,1536]{1,0:T(8,128)(2,1)S(1)}, u32[]{:S(2)}, u32[]{:S(2)}) collective-permute-start(bf16[64,1536]{1,0:T(8,128)(2,1)S(1)} %get-tuple-element.110.refs_0_), channel_id=1, source_target_pairs={{0,1},{1,0},{2,3},{3,2},{4,8},{5,9},{6,10},{7,11},{8,4},{9,5},{10,... | collective-permute-start | bytes 589832 | tf_op jit(solution)/shard_map/ppermute | solution.py:42
  48.0 9.2 %collective-permute-start.12 = (bf16[64,1536]{1,0:T(8,128)(2,1)S(1)}, bf16[64,1536]{1,0:T(8,128)(2,1)S(1)}, u32[]{:S(2)}, u32[]{:S(2)}) collective-permute-start(bf16[64,1536]{1,0:T(8,128)(2,1)S(1)} %get-tuple-element.110.refs_0_), channel_id=1, source_target_pairs={{0,4},{1,5},{2,6},{3,7},{4,0},{5,1},{6,2},{7,3},{8,12},{9,13},{10,... | collective-permute-start | bytes 589832 | tf_op jit(solution)/shard_map/ppermute | solution.py:42
  51.0 10.0 %collective-permute-start.17 = (bf16[64,1536]{1,0:T(8,128)(2,1)S(1)}, bf16[64,1536]{1,0:T(8,128)(2,1)S(1)}, u32[]{:S(2)}, u32[]{:S(2)}) collective-permute-start(bf16[64,1536]{1,0:T(8,128)(2,1)S(1)} %get-tuple-element.118.refs_0_), channel_id=1, source_target_pairs={{0,1},{1,0},{2,3},{3,2},{4,8},{5,9},{6,10},{7,11},{8,4},{9,5},{10,... | collective-permute-start | bytes 589832 | tf_op jit(solution)/shard_map/ppermute | solution.py:42
  51.1 10.2 %collective-permute-start.18 = (bf16[64,1536]{1,0:T(8,128)(2,1)S(1)}, bf16[64,1536]{1,0:T(8,128)(2,1)S(1)}, u32[]{:S(2)}, u32[]{:S(2)}) collective-permute-start(bf16[64,1536]{1,0:T(8,128)(2,1)S(1)} %get-tuple-element.118.refs_0_), channel_id=1, source_target_pairs={{0,4},{1,5},{2,6},{3,7},{4,0},{5,1},{6,2},{7,3},{8,12},{9,13},{10,... | collective-permute-start | bytes 589832 | tf_op jit(solution)/shard_map/ppermute | solution.py:42
  57.2 8.0 %collective-permute-start.15 = (bf16[64,1536]{1,0:T(8,128)(2,1)S(1)}, bf16[64,1536]{1,0:T(8,128)(2,1)S(1)}, u32[]{:S(2)}, u32[]{:S(2)}) collective-permute-start(bf16[64,1536]{1,0:T(8,128)(2,1)S(1)} %get-tuple-element.115), channel_id=1, source_target_pairs={{0,1},{1,0},{2,3},{3,2},{4,8},{5,9},{6,10},{7,11},{8,4},{9,5},{10,... | collective-permute-start | bytes 589832 | tf_op jit(solution)/shard_map/ppermute | solution.py:42
  57.3 8.2 %collective-permute-start.16 = (bf16[64,1536]{1,0:T(8,128)(2,1)S(1)}, bf16[64,1536]{1,0:T(8,128)(2,1)S(1)}, u32[]{:S(2)}, u32[]{:S(2)}) collective-permute-start(bf16[64,1536]{1,0:T(8,128)(2,1)S(1)} %get-tuple-element.116.refs_3_), channel_id=1, source_target_pairs={{0,4},{1,5},{2,6},{3,7},{4,0},{5,1},{6,2},{7,3},{8,12},{9,13},{10,... | collective-permute-start | bytes 589832 | tf_op jit(solution)/shard_map/ppermute | solution.py:42
  61.3 8.1 %collective-permute-start.21 = (bf16[64,1536]{1,0:T(8,128)(2,1)S(1)}, bf16[64,1536]{1,0:T(8,128)(2,1)S(1)}, u32[]{:S(2)}, u32[]{:S(2)}) collective-permute-start(bf16[64,1536]{1,0:T(8,128)(2,1)S(1)} %get-tuple-element.123), channel_id=1, source_target_pairs={{0,1},{1,0},{2,3},{3,2},{4,8},{5,9},{6,10},{7,11},{8,4},{9,5},{10,... | collective-permute-start | bytes 589832 | tf_op jit(solution)/shard_map/ppermute | solution.py:42
  61.4 8.3 %collective-permute-start.22 = (bf16[64,1536]{1,0:T(8,128)(2,1)S(1)}, bf16[64,1536]{1,0:T(8,128)(2,1)S(1)}, u32[]{:S(2)}, u32[]{:S(2)}) collective-permute-start(bf16[64,1536]{1,0:T(8,128)(2,1)S(1)} %get-tuple-element.119.refs_4_), channel_id=1, source_target_pairs={{0,4},{1,5},{2,6},{3,7},{4,0},{5,1},{6,2},{7,3},{8,12},{9,13},{10,... | collective-permute-start | bytes 589832 | tf_op jit(solution)/shard_map/ppermute | solution.py:42
  65.5 8.1 %collective-permute-start.19 = (bf16[64,1536]{1,0:T(8,128)(2,1)S(1)}, bf16[64,1536]{1,0:T(8,128)(2,1)S(1)}, u32[]{:S(2)}, u32[]{:S(2)}) collective-permute-start(bf16[64,1536]{1,0:T(8,128)(2,1)S(1)} %get-tuple-element.120), channel_id=1, source_target_pairs={{0,1},{1,0},{2,3},{3,2},{4,8},{5,9},{6,10},{7,11},{8,4},{9,5},{10,... | collective-permute-start | bytes 589832 | tf_op jit(solution)/shard_map/ppermute | solution.py:42
  65.6 8.3 %collective-permute-start.20 = (bf16[64,1536]{1,0:T(8,128)(2,1)S(1)}, bf16[64,1536]{1,0:T(8,128)(2,1)S(1)}, u32[]{:S(2)}, u32[]{:S(2)}) collective-permute-start(bf16[64,1536]{1,0:T(8,128)(2,1)S(1)} %get-tuple-element.121.refs_4_), channel_id=1, source_target_pairs={{0,4},{1,5},{2,6},{3,7},{4,0},{5,1},{6,2},{7,3},{8,12},{9,13},{10,... | collective-permute-start | bytes 589832 | tf_op jit(solution)/shard_map/ppermute | solution.py:42
  69.8 12.5 %collective-permute-start.25 = (bf16[64,1536]{1,0:T(8,128)(2,1)S(1)}, bf16[64,1536]{1,0:T(8,128)(2,1)S(1)}, u32[]{:S(2)}, u32[]{:S(2)}) collective-permute-start(bf16[64,1536]{1,0:T(8,128)(2,1)S(1)} %get-tuple-element.128), channel_id=1, source_target_pairs={{0,1},{1,0},{2,3},{3,2},{4,8},{5,9},{6,10},{7,11},{8,4},{9,5},{10,... | collective-permute-start | bytes 589832 | tf_op jit(solution)/shard_map/ppermute | solution.py:42
  69.8 12.4 %collective-permute-start.26 = (bf16[64,1536]{1,0:T(8,128)(2,1)S(1)}, bf16[64,1536]{1,0:T(8,128)(2,1)S(1)}, u32[]{:S(2)}, u32[]{:S(2)}) collective-permute-start(bf16[64,1536]{1,0:T(8,128)(2,1)S(1)} %get-tuple-element.124.refs_4_), channel_id=1, source_target_pairs={{0,4},{1,5},{2,6},{3,7},{4,0},{5,1},{6,2},{7,3},{8,12},{9,13},{10,... | collective-permute-start | bytes 589832 | tf_op jit(solution)/shard_map/ppermute | solution.py:42
  74.0 9.9 %collective-permute-start.23 = (bf16[64,1536]{1,0:T(8,128)(2,1)S(1)}, bf16[64,1536]{1,0:T(8,128)(2,1)S(1)}, u32[]{:S(2)}, u32[]{:S(2)}) collective-permute-start(bf16[64,1536]{1,0:T(8,128)(2,1)S(1)} %get-tuple-element.125.refs_9_), channel_id=1, source_target_pairs={{0,4},{1,5},{2,6},{3,7},{4,0},{5,1},{6,2},{7,3},{8,12},{9,13},{10,... | collective-permute-start | bytes 589832 | tf_op jit(solution)/shard_map/ppermute | solution.py:42
  76.5 7.4 %collective-permute-start.24 = (bf16[64,1536]{1,0:T(8,128)(2,1)S(1)}, bf16[64,1536]{1,0:T(8,128)(2,1)S(1)}, u32[]{:S(2)}, u32[]{:S(2)}) collective-permute-start(bf16[64,1536]{1,0:T(8,128)(2,1)S(1)} %get-tuple-element.126), channel_id=1, source_target_pairs={{0,1},{1,0},{2,3},{3,2},{4,8},{5,9},{6,10},{7,11},{8,4},{9,5},{10,... | collective-permute-start | bytes 589832 | tf_op jit(solution)/shard_map/ppermute | solution.py:42
  82.3 9.6 %collective-permute-start.29 = (bf16[64,1536]{1,0:T(8,128)(2,1)S(1)}, bf16[64,1536]{1,0:T(8,128)(2,1)S(1)}, u32[]{:S(2)}, u32[]{:S(2)}) collective-permute-start(bf16[64,1536]{1,0:T(8,128)(2,1)S(1)} %get-tuple-element.130.refs_4_), channel_id=1, source_target_pairs={{0,4},{1,5},{2,6},{3,7},{4,0},{5,1},{6,2},{7,3},{8,12},{9,13},{10,... | collective-permute-start | bytes 589832 | tf_op jit(solution)/shard_map/ppermute | solution.py:42
  83.9 8.1 %collective-permute-start.30 = (bf16[64,1536]{1,0:T(8,128)(2,1)S(1)}, bf16[64,1536]{1,0:T(8,128)(2,1)S(1)}, u32[]{:S(2)}, u32[]{:S(2)}) collective-permute-start(bf16[64,1536]{1,0:T(8,128)(2,1)S(1)} %get-tuple-element.133), channel_id=1, source_target_pairs={{0,1},{1,0},{2,3},{3,2},{4,8},{5,9},{6,10},{7,11},{8,4},{9,5},{10,... | collective-permute-start | bytes 589832 | tf_op jit(solution)/shard_map/ppermute | solution.py:42
  84.3 10.3 %collective-permute-start.27 = (bf16[64,1536]{1,0:T(8,128)(2,1)S(1)}, bf16[64,1536]{1,0:T(8,128)(2,1)S(1)}, u32[]{:S(2)}, u32[]{:S(2)}) collective-permute-start(bf16[64,1536]{1,0:T(8,128)(2,1)S(1)} %get-tuple-element.131.refs_0_), channel_id=1, source_target_pairs={{0,4},{1,5},{2,6},{3,7},{4,0},{5,1},{6,2},{7,3},{8,12},{9,13},{10,... | collective-permute-start | bytes 589832 | tf_op jit(solution)/shard_map/ppermute | solution.py:42
  86.3 8.3 %collective-permute-start.28 = (bf16[64,1536]{1,0:T(8,128)(2,1)S(1)}, bf16[64,1536]{1,0:T(8,128)(2,1)S(1)}, u32[]{:S(2)}, u32[]{:S(2)}) collective-permute-start(bf16[64,1536]{1,0:T(8,128)(2,1)S(1)} %get-tuple-element.131.refs_0_), channel_id=1, source_target_pairs={{0,1},{1,0},{2,3},{3,2},{4,8},{5,9},{6,10},{7,11},{8,4},{9,5},{10,... | collective-permute-start | bytes 589832 | tf_op jit(solution)/shard_map/ppermute | solution.py:42
  92.4 10.5 %collective-permute-start.33 = (bf16[64,1536]{1,0:T(8,128)(2,1)S(1)}, bf16[64,1536]{1,0:T(8,128)(2,1)S(1)}, u32[]{:S(2)}, u32[]{:S(2)}) collective-permute-start(bf16[64,1536]{1,0:T(8,128)(2,1)S(1)} %get-tuple-element.140.refs_0_.refs_6_), channel_id=1, source_target_pairs={{0,1},{1,0},{2,3},{3,2},{4,8},{5,9},{6,10},{7,11},{8,4},{9,5},{10,... | collective-permute-start | bytes 589832 | tf_op jit(solution)/shard_map/ppermute | solution.py:42
  93.0 9.9 %collective-permute-start.34 = (bf16[64,1536]{1,0:T(8,128)(2,1)S(1)}, bf16[64,1536]{1,0:T(8,128)(2,1)S(1)}, u32[]{:S(2)}, u32[]{:S(2)}) collective-permute-start(bf16[64,1536]{1,0:T(8,128)(2,1)S(1)} %get-tuple-element.140.refs_0_.refs_6_), channel_id=1, source_target_pairs={{0,4},{1,5},{2,6},{3,7},{4,0},{5,1},{6,2},{7,3},{8,12},{9,13},{10,... | collective-permute-start | bytes 589832 | tf_op jit(solution)/shard_map/ppermute | solution.py:42
  94.6 9.0 %collective-permute-start.32 = (bf16[64,1536]{1,0:T(8,128)(2,1)S(1)}, bf16[64,1536]{1,0:T(8,128)(2,1)S(1)}, u32[]{:S(2)}, u32[]{:S(2)}) collective-permute-start(bf16[64,1536]{1,0:T(8,128)(2,1)S(1)} %get-tuple-element.139), channel_id=1, source_target_pairs={{0,1},{1,0},{2,3},{3,2},{4,8},{5,9},{6,10},{7,11},{8,4},{9,5},{10,... | collective-permute-start | bytes 589832 | tf_op jit(solution)/shard_map/ppermute | solution.py:42
  94.7 16.8 %collective-permute-start.31 = (bf16[64,1536]{1,0:T(8,128)(2,1)S(1)}, bf16[64,1536]{1,0:T(8,128)(2,1)S(1)}, u32[]{:S(2)}, u32[]{:S(2)}) collective-permute-start(bf16[64,1536]{1,0:T(8,128)(2,1)S(1)} %get-tuple-element.138.refs_12_), channel_id=1, source_target_pairs={{0,4},{1,5},{2,6},{3,7},{4,0},{5,1},{6,2},{7,3},{8,12},{9,13},{10,... | collective-permute-start | bytes 589832 | tf_op jit(solution)/shard_map/ppermute | solution.py:42
  102.9 7.9 %collective-permute-start.37 = (bf16[64,1536]{1,0:T(8,128)(2,1)S(1)}, bf16[64,1536]{1,0:T(8,128)(2,1)S(1)}, u32[]{:S(2)}, u32[]{:S(2)}) collective-permute-start(bf16[64,1536]{1,0:T(8,128)(2,1)S(1)} %get-tuple-element.146), channel_id=1, source_target_pairs={{0,1},{1,0},{2,3},{3,2},{4,8},{5,9},{6,10},{7,11},{8,4},{9,5},{10,... | collective-permute-start | bytes 589832 | tf_op jit(solution)/shard_map/ppermute | solution.py:42
  103.0 18.5 %collective-permute-start.36 = (bf16[64,1536]{1,0:T(8,128)(2,1)S(1)}, bf16[64,1536]{1,0:T(8,128)(2,1)S(1)}, u32[]{:S(2)}, u32[]{:S(2)}) collective-permute-start(bf16[64,1536]{1,0:T(8,128)(2,1)S(1)} %get-tuple-element.145.refs_1_), channel_id=1, source_target_pairs={{0,4},{1,5},{2,6},{3,7},{4,0},{5,1},{6,2},{7,3},{8,12},{9,13},{10,... | collective-permute-start | bytes 589832 | tf_op jit(solution)/shard_map/ppermute | solution.py:42
  103.7 11.4 %collective-permute-start.35 = (bf16[64,1536]{1,0:T(8,128)(2,1)S(1)}, bf16[64,1536]{1,0:T(8,128)(2,1)S(1)}, u32[]{:S(2)}, u32[]{:S(2)}) collective-permute-start(bf16[64,1536]{1,0:T(8,128)(2,1)S(1)} %relay_far.2.refs_10_), channel_id=1, source_target_pairs={{0,4},{1,5},{2,6},{3,7},{4,0},{5,1},{6,2},{7,3},{8,12},{9,13},{10,... | collective-permute-start | bytes 589832 | tf_op jit(solution)/shard_map/ppermute | solution.py:42
  110.9 10.6 %collective-permute-start.38 = (bf16[64,1536]{1,0:T(8,128)(2,1)S(1)}, bf16[64,1536]{1,0:T(8,128)(2,1)S(1)}, u32[]{:S(2)}, u32[]{:S(2)}) collective-permute-start(bf16[64,1536]{1,0:T(8,128)(2,1)S(1)} %relay_far.3.refs_8_), channel_id=1, source_target_pairs={{0,4},{1,5},{2,6},{3,7},{4,0},{5,1},{6,2},{7,3},{8,12},{9,13},{10,... | collective-permute-start | bytes 589832 | tf_op jit(solution)/shard_map/ppermute | solution.py:42
  124.9 4.5 %collective-permute-start.40 = (bf16[64,1536]{1,0:T(8,128)(2,1)S(1)}, bf16[64,1536]{1,0:T(8,128)(2,1)S(1)}, u32[]{:S(2)}, u32[]{:S(2)}) collective-permute-start(bf16[64,1536]{1,0:T(8,128)(2,1)S(1)} %get-tuple-element.162), channel_id=1, source_target_pairs={{0,1},{1,0},{2,3},{3,2},{4,5},{5,4},{6,7},{7,6},{8,9},{9,8},{10,11... | collective-permute-start | bytes 589832 | tf_op jit(solution)/shard_map/ppermute | solution.py:42
  128.3 2.6 %collective-permute-start.39 = (bf16[64,1536]{1,0:T(8,128)(2,1)S(1)}, bf16[64,1536]{1,0:T(8,128)(2,1)S(1)}, u32[]{:S(2)}, u32[]{:S(2)}) collective-permute-start(bf16[64,1536]{1,0:T(8,128)(2,1)S(1)} %get-tuple-element.160), channel_id=1, source_target_pairs={{0,1},{1,0},{2,3},{3,2},{4,5},{5,4},{6,7},{7,6},{8,9},{9,8},{10,11... | collective-permute-start | bytes 589832 | tf_op jit(solution)/shard_map/ppermute | solution.py:42
  128.8 10.7 %collective-permute-start.43 = (bf16[64,1536]{1,0:T(8,128)(2,1)S(1)}, bf16[64,1536]{1,0:T(8,128)(2,1)S(1)}, u32[]{:S(2)}, u32[]{:S(2)}) collective-permute-start(bf16[64,1536]{1,0:T(8,128)(2,1)S(1)} %get-tuple-element.168), channel_id=1, source_target_pairs={{0,1},{1,0},{2,3},{3,2},{4,5},{5,4},{6,7},{7,6},{8,9},{9,8},{10,11... | collective-permute-start | bytes 589832 | tf_op jit(solution)/shard_map/ppermute | solution.py:42
  128.9 10.7 %collective-permute-start.41 = (bf16[64,1536]{1,0:T(8,128)(2,1)S(1)}, bf16[64,1536]{1,0:T(8,128)(2,1)S(1)}, u32[]{:S(2)}, u32[]{:S(2)}) collective-permute-start(bf16[64,1536]{1,0:T(8,128)(2,1)S(1)} %get-tuple-element.166), channel_id=1, source_target_pairs={{0,1},{1,0},{2,3},{3,2},{4,5},{5,4},{6,7},{7,6},{8,9},{9,8},{10,11... | collective-permute-start | bytes 589832 | tf_op jit(solution)/shard_map/ppermute | solution.py:42
  129.4 11.2 %collective-permute-start.42 = (bf16[64,1536]{1,0:T(8,128)(2,1)S(1)}, bf16[64,1536]{1,0:T(8,128)(2,1)S(1)}, u32[]{:S(2)}, u32[]{:S(2)}) collective-permute-start(bf16[64,1536]{1,0:T(8,128)(2,1)S(1)} %far_sum_col.2.refs_2_), channel_id=1, source_target_pairs={{0,2},{2,0},{1,3},{3,1},{4,6},{6,4},{5,7},{7,5},{8,10},{10,8},{9,1... | collective-permute-start | bytes 589832 | tf_op jit(solution)/shard_map/ppermute | solution.py:42
  130.9 9.6 %collective-permute-start.44 = (bf16[64,1536]{1,0:T(8,128)(2,1)S(1)}, bf16[64,1536]{1,0:T(8,128)(2,1)S(1)}, u32[]{:S(2)}, u32[]{:S(2)}) collective-permute-start(bf16[64,1536]{1,0:T(8,128)(2,1)S(1)} %far_sum_col.3.refs_17_), channel_id=1, source_target_pairs={{0,2},{2,0},{1,3},{3,1},{4,6},{6,4},{5,7},{7,5},{8,10},{10,8},{9,1... | collective-permute-start | bytes 589832 | tf_op jit(solution)/shard_map/ppermute | solution.py:42

commit v3 on v2

--- a/solution.py
+++ b/solution.py
@@ -26,6 +26,7 @@
 STREAMS = 2
 ROUNDS = 2
 SPLIT = 2
+EARLY = 2
 
 
 def gelu_both(preact):
@@ -92,11 +93,42 @@
     lax.fori_loop(0, count, run, 0)
 
 
-def forward_kernel(start, tile, parts, first, w_ref, *refs):
-    *refs, buffer, sems = refs
+def preload_kernel(starts, w_ref, *refs):
+    *outs, sems = refs
+    copies = []
+    for k, (start, out) in enumerate(zip(starts, outs)):
+        part = w_ref.at[:, pl.ds(start, out.shape[1])]
+        copies.append(pltpu.make_async_copy(part, out, sems.at[k]))
+        copies[-1].start()
+    for copy in copies:
+        copy.wait()
+
+
+def preload(weight, starts, size, dep):
+    shape = jax.ShapeDtypeStruct((weight.shape[0], size), bf16)
+    return call(
+        functools.partial(preload_kernel, starts),
+        [weight],
+        [pl.BlockSpec(memory_space=pl.ANY)],
+        dep,
+        out_specs=[resident()] * len(starts),
+        out_shape=[shape] * len(starts),
+        scratch_shapes=[pltpu.SemaphoreType.DMA((len(starts),))],
+        compiler_params=params(16),
+        cost_estimate=cost(0, 2 * len(starts) * shape.size),
+        name="preload",
+    )
+
+
+def forward_kernel(start, tile, parts, first, loaded, w_ref, *refs):
+    if loaded:
+        buffer = w_ref
+    else:
+        *refs, buffer, sems = refs
     depth, size = buffer.shape
-    load = functools.partial(fetch, w_ref, (0, depth), (start, size), buffer, sems, tile, False)
-    each(size // tile, lambda i: load(i).start())
+    if not loaded:
+        load = functools.partial(fetch, w_ref, (0, depth), (start, size), buffer, sems, tile, False)
+        each(size // tile, lambda i: load(i).start())
     if first:
         pieces, outs, token, x_ref = refs[:parts], refs[parts : 2 * parts], refs[-2], refs[-1]
         rows = outs[0].shape[0]
@@ -111,7 +143,8 @@
 
     def body(i):
         columns = pl.ds(pl.multiple_of(i * tile, tile), tile)
-        load(i).wait()
+        if not loaded:
+            load(i).wait()
         sums = jnp.dot(x_ref[...], buffer[:, columns], preferred_element_type=f32).astype(bf16)
         for k, out in enumerate(outs):
             out[:, columns] = sums[k * rows : (k + 1) * rows]
@@ -119,24 +152,26 @@
     each(size // tile, body)
 
 
-def forward(x, weight, start, size, tokens, parts, dep=None):
+def forward(x, weight, start, size, tokens, parts, dep=None, loaded=None):
     depth = weight.shape[0]
     tile = tile_of(size, TILE)
     rows = tokens // parts
     first = isinstance(x, tuple)
-    operands = [weight, *x] if first else [weight, x]
+    here = loaded is not None
+    operands = [loaded if here else weight, *(x if first else (x,))]
     out_shape = [jax.ShapeDtypeStruct((rows, size), bf16)] * parts + [TOKEN]
     if first:
         out_shape.append(jax.ShapeDtypeStruct((tokens, depth), bf16))
+    scratch = [pltpu.VMEM((depth, size), bf16), pltpu.SemaphoreType.DMA((size // tile,))]
     return call(
-        functools.partial(forward_kernel, start, tile, parts, first),
+        functools.partial(forward_kernel, start, tile, parts, first, here),
         operands,
-        [pl.BlockSpec(memory_space=pl.ANY)] + [resident()] * (len(operands) - 1),
+        [resident() if here else pl.BlockSpec(memory_space=pl.ANY)] + [resident()] * (len(operands) - 1),
         dep,
         out_specs=[resident()] * len(out_shape),
         out_shape=out_shape,
-        scratch_shapes=[pltpu.VMEM((depth, size), bf16), pltpu.SemaphoreType.DMA((size // tile,))],
-        compiler_params=params(36),
+        scratch_shapes=[] if here else scratch,
+        compiler_params=params(16 if here else 36),
         cost_estimate=cost(2 * tokens * depth * size, 2 * depth * size),
         name="forward_sums",
     )
@@ -162,18 +197,23 @@
             all_ref[3 * rows :, columns] = far_e[...]
 
 
-def grads_kernel(names, start, lo, tile, *refs):
+def grads_kernel(names, start, cuts, tile, *refs):
     ref = {}
     for name, one in zip(names, refs, strict=True):
         ref.setdefault(name, []).append(one)
     blocks, token = ref["block"], ref["token"][0]
-    inputs, weight = "weight" in ref, "grad_weight" in ref
+    inputs, weight = "weight" in ref or "loaded" in ref, "grad_weight" in ref
+    loaded = "loaded" in ref
     delta = ref["delta"][0] if len(blocks) > 1 else blocks[0]
     size = delta.shape[1]
-    tiles = (ref["loads"] if inputs else ref["stores"])[0].shape[0]
+    lo, tiles = cuts[0][0], (cuts[-1][1] - cuts[0][0]) // tile
+    w_first = lo if loaded else 0
     hidden_copies = []
     if inputs:
-        outs, before, w_tiles = ref["grad_inputs"], ref.get("before"), ref["weight_tiles"][0]
+        outs, before = ref["grad_inputs"], ref.get("before")
+        w_tiles = (ref["loaded"] if loaded else ref["weight_tiles"])[0]
+        parts = len(outs) // len(cuts)
+    if inputs and not loaded:
         load = functools.partial(
             fetch, ref["weight"][0], (lo, tiles * tile), (start, size), w_tiles, ref["loads"][0], tile, True
         )
@@ -197,25 +237,8 @@
             ref["stores"][0].at[i],
         )
 
-    def body(i):
+    def body(cut, first, i):
         rows = pl.ds(pl.multiple_of(i * tile, tile), tile)
-        if inputs:
-            load(i).wait()
-            value = lax.dot_general(
-                delta[...], w_tiles[rows, :], (((1,), (1,)), ((), ())), preferred_element_type=f32
-            )
-            if before:
-                value = value + before[0][:, rows]
-            if len(outs) == 1:
-                outs[0][:, rows] = value.astype(outs[0].dtype)
-            else:
-                staged = ref["staged"][0]
-                staged[...] = value.astype(bf16)
-                row, col = lax.axis_index("row"), lax.axis_index("col")
-                tokens = outs[0].shape[0]
-                for k, out in enumerate(outs):
-                    at = pl.multiple_of(place_of(col ^ k, row) * tokens, tokens)
-                    out[:, rows] = staged[pl.ds(at, tokens), :]
         if weight:
             x_t = ref["x"][0][:, pl.ds(pl.multiple_of(lo + i * tile, tile), tile)].T
             for at in range(0, size, step):
@@ -223,12 +246,34 @@
                     x_t, delta[:, at : at + step], preferred_element_type=f32
                 ).astype(bf16)
             store(i).start()
-
-    if weight and UNROLL:
-        for i in range(tiles):
-            body(i)
-    else:
-        each(tiles, body)
+        if inputs:
+            if not loaded:
+                load(i).wait()
+            w_rows = pl.ds(pl.multiple_of(w_first + i * tile, tile), tile)
+            value = lax.dot_general(
+                delta[...], w_tiles[w_rows, :], (((1,), (1,)), ((), ())), preferred_element_type=f32
+            )
+            into = pl.ds(pl.multiple_of((i - first) * tile, tile), tile)
+            if before:
+                value = value + before[cut][:, into]
+            if parts == 1:
+                outs[cut][:, into] = value.astype(outs[cut].dtype)
+            else:
+                staged = ref["staged"][0]
+                staged[...] = value.astype(bf16)
+                row, col = lax.axis_index("row"), lax.axis_index("col")
+                tokens = outs[0].shape[0]
+                for k in range(parts):
+                    at = pl.multiple_of(place_of(col ^ k, row) * tokens, tokens)
+                    outs[cut * parts + k][:, into] = staged[pl.ds(at, tokens), :]
+
+    for cut, (low, high) in enumerate(cuts):
+        first, past = (low - lo) // tile, (high - lo) // tile
+        if weight and UNROLL:
+            for i in range(first, past):
+                body(cut, first, i)
+        else:
+            each(past - first, lambda i: body(cut, first, first + i))
     if weight:
         each(tiles, lambda i: store(i).wait())
     for copy in hidden_copies:
@@ -236,12 +281,13 @@
 
 
 def grads(
-    start, lo, hi, blocks, dep=None, *, weight=None, before=None, last=False, parts=1, x=None, into=None, hidden=(), all_hidden=None
+    start, cuts, blocks, dep=None, *, weight=None, loaded=None, before=None, last=False, parts=1, x=None, into=None, hidden=(), all_hidden=None
 ):
     hbm = pl.BlockSpec(memory_space=pl.ANY)
     size = sum(b.shape[1] for b in blocks) if len(blocks) == 1 else blocks[0].shape[1] * (len(blocks) // 6)
     tokens = blocks[0].shape[0] * (4 if len(blocks) > 1 else 1)
-    tile = tile_of(hi - lo, TILE)
+    features = cuts[-1][1] - cuts[0][0]
+    tile = tile_of(cuts[0][1] - cuts[0][0], TILE)
     operands, outs, scratch, aliases = [], [], [], {}
 
     def give(name, value, spec=None):
@@ -260,14 +306,19 @@
         give("block", block)
     if len(blocks) > 1:
         scratch.append(("delta", pltpu.VMEM((tokens, size), bf16)))
-    tiles, sems = pltpu.VMEM((hi - lo, size), bf16), pltpu.SemaphoreType.DMA(((hi - lo) // tile,))
-    if weight is not None:
-        give("weight", weight, hbm)
-        if before is not None:
-            give("before", before)
-        for _ in range(parts):
-            make("grad_inputs", jax.ShapeDtypeStruct((tokens // parts, hi - lo), bf16 if last else f32))
-        scratch += [("weight_tiles", tiles), ("loads", sems)]
+    tiles, sems = pltpu.VMEM((features, size), bf16), pltpu.SemaphoreType.DMA((features // tile,))
+    if weight is not None or loaded is not None:
+        if loaded is None:
+            give("weight", weight, hbm)
+            scratch += [("weight_tiles", tiles), ("loads", sems)]
+        else:
+            give("loaded", loaded)
+        for one in before or ():
+            give("before", one)
+        for low, high in cuts:
+            shape = jax.ShapeDtypeStruct((tokens // parts, high - low), bf16 if last else f32)
+            for _ in range(parts):
+                make("grad_inputs", shape)
         if parts > 1:
             scratch.append(("staged", pltpu.VMEM((tokens, tile), bf16)))
     if x is not None:
@@ -281,9 +332,9 @@
         scratch.append(("hidden_sems", pltpu.SemaphoreType.DMA((len(hidden),))))
     make("token", TOKEN)
     names = [name for name, *_ in operands + outs + scratch]
-    work = (weight is not None) + (x is not None)
+    work = (weight is not None or loaded is not None) + (x is not None)
     return call(
-        functools.partial(grads_kernel, names, start, lo, tile),
+        functools.partial(grads_kernel, names, start, cuts, tile),
         [value for _, value, _ in operands],
         [spec for *_, spec in operands],
         dep,
@@ -292,7 +343,7 @@
         scratch_shapes=[shape for _, shape in scratch],
         input_output_aliases=aliases,
         compiler_params=params(36),
-        cost_estimate=cost(2 * work * tokens * (hi - lo) * size, 2 * work * (hi - lo) * size),
+        cost_estimate=cost(2 * work * tokens * features * size, 2 * work * features * size),
         name="grads",
     )
 
@@ -397,8 +448,9 @@
     lax.fori_loop(0, width // step, body, 0)
 
 
-def sum_kernel(a, b, out):
+def sum_kernel(a, b, c, out, relay):
     out[...] = a[...] + b[...]
+    relay[...] = c[...]
 
 
 def finish_kernel(*refs):
@@ -427,12 +479,14 @@
     )
 
 
-def gather_inputs(inputs):
+def gather_inputs(inputs, meanwhile):
     across = send(inputs, "col", ACROSS)
     (local,) = combine("local", pass_on_kernel, (inputs,), 1, None)
     beside = send(local, "col", CORES)
-    corner = send(across, "col", CORES)
-    return (local, beside, across, corner)
+    made = meanwhile(local)
+    (relayed,) = combine("corner", pass_on_kernel, (across,), 1, made[0])
+    corner = send(relayed, "col", CORES)
+    return (local, beside, relayed, corner), made
 
 
 class Order:
@@ -468,32 +522,36 @@
 
     def forward_of(k):
         def run(dep):
-            *sums[k], token = forward(x, weight, k * size, size, tokens, 4, dep)
+            *sums[k], token = forward(x, weight, k * size, size, tokens, 4, dep, loaded.get(k))
             return token
 
         return run
 
-    def grads_of(k, cut=SPLIT, part=0, both=True):
+    def grads_of(k, *which, both=True):
         def run(dep):
-            mine = range(SPLIT) if cut == 1 else [part]
             more = {}
             if both:
                 more = {"x": x, "into": state["weight"]}
-                if part == 0:
+                if which[0] == 0:
                     more |= {"hidden": [hidden[k]], "all_hidden": state["hidden"]}
-            lo, hi = bounds[mine[0]][0], bounds[mine[-1]][1]
-            before = total[mine[0]]
-            if before is not None and cut == 1:
-                before = jnp.concatenate([total[p] for p in mine], axis=1)
+            before = [total[p] for p in which] if total[which[0]] is not None else None
             made = list(
-                grads(k * size, lo, hi, blocks[k], dep, weight=weight, before=before, **more)
+                grads(k * size, [bounds[p] for p in which], blocks[k], dep, weight=weight, before=before, **more)
             )
-            total[mine[0]] = made.pop(0)
+            for p in which:
+                total[p] = made.pop(0)
             if both:
                 state["weight"] = made.pop(0)
-                if part == 0:
+                if which[0] == 0:
                     state["hidden"] = made.pop(0)
             return made.pop(0)
+
+        return run
+
+    def preload_of(k):
+        def run(dep):
+            (loaded[k],) = preload(weight, [k * size], size, dep)
+            return loaded[k]
 
         return run
 
@@ -548,8 +606,13 @@
                 order.work()
                 yield
 
-    *sums[0], order.token, x = forward(gather_inputs(inputs), weight, 0, size, tokens, 4)
-    plan.update(planned(forward_of, grads_of))
+    early = range(EARLY)
+    pieces, made = gather_inputs(
+        inputs, lambda dep: preload(weight, [k * size for k in early], size, dep)
+    )
+    loaded = dict(zip(early, made))
+    *sums[0], order.token, x = forward(pieces, weight, 0, size, tokens, 4, None, loaded.get(0))
+    plan.update(planned(forward_of, grads_of, preload_of))
     chains = [chain(list(range(s, chunks, STREAMS))) for s in range(STREAMS)]
     live = list(chains)
     while live:
@@ -559,24 +622,35 @@
 
     final = chunks - 1
     for k in range(chunks - STREAMS, final):
-        for part in range(SPLIT):
-            order.token = grads_of(k, part=part, both=False)(order.token)
-    parts, given = [], []
-    for part, (lo, hi) in enumerate(bounds):
+        order.token = grads_of(k, *range(SPLIT), both=False)(order.token)
+    finals, parts, far_in = [], [], []
+
+    def across(part):
+        keep, give, keep_far, _ = parts[part]
+        far_sum, give = order.between("far_sum_col", sum_kernel, (keep_far, far_in[part], give))
+        finals.extend([keep, send(far_sum, "col", ACROSS), send(give, "col", CORES)])
+
+    for part, cut in enumerate(bounds):
         *pieces, order.token = grads(
-            final * size, lo, hi, blocks[final], order.token, weight=weight, before=total[part], last=True, parts=4
+            final * size,
+            [cut],
+            blocks[final],
+            order.token,
+            weight=weight,
+            loaded=loaded.get(final),
+            before=[total[part]],
+            last=True,
+            parts=4,
         )
+        if part:
+            across(part - 1)
         parts.append(pieces)
-        given.append((send(pieces[3], "col", CORES), send(pieces[1], "col", CORES)))
-    finals = []
-    for (keep, _, keep_far, _), (far_in, near_in) in zip(parts, given):
-        (far_sum,) = order.between("far_sum_col", sum_kernel, (keep_far, far_in), 1)
-        finals += [keep, near_in, send(far_sum, "col", ACROSS)]
+        far_in.append(send(pieces[3], "col", CORES))
+    across(SPLIT - 1)
     late = range(chunks - STREAMS, chunks)
     grad_weight, all_hidden, order.token = grads(
         late[0] * size,
-        0,
-        depth,
+        [(0, depth)],
         [block for k in late for block in blocks[k]],
         order.token,
         x=x,
@@ -588,15 +662,16 @@
     return (all_hidden, grad_inputs, grad_weight)
 
 
-def planned(forward_of, grads_of):
+def planned(forward_of, grads_of, preload_of):
     return {
         0: [forward_of(1)],
         2: [forward_of(2)],
         4: [forward_of(3)],
-        12: [grads_of(0, part=0)],
-        14: [grads_of(0, part=1)],
-        16: [grads_of(1, part=0)],
-        18: [grads_of(1, part=1)],
+        12: [grads_of(0, 0)],
+        14: [grads_of(0, 1)],
+        16: [grads_of(1, 0)],
+        18: [grads_of(1, 1)],
+        19: [preload_of(3)],
     }
 
 
@@ -610,7 +685,7 @@
     delta = (cotangent.astype(f32) * slope).astype(bf16)
     blocks = [lax.all_gather(delta, "row", axis=0, tiled=True)]
     made = jax.ShapeDtypeStruct(weight.shape, bf16)
-    sums, grad_weight, _ = grads(0, 0, depth, blocks, weight=weight, last=True, x=x, into=made)
+    sums, grad_weight, _ = grads(0, [(0, depth)], blocks, weight=weight, last=True, x=x, into=made)
     grad_inputs = lax.psum_scatter(sums, "col", scatter_dimension=0, tiled=True)
     return (value.astype(bf16), grad_inputs, grad_weight)
 

time: 142 us -> 132 us (0.930)
  waiting for transfers between devices: 18.2 us -> 9.54 us
  Pallas kernels: 66.7 us -> 64.8 us
    ppermute x45, waiting for transfers between devices: 18.2 us -> 9.54 us  [send(): return lax.ppermute(value, axis, pairs)]
    pallas_call x2, Pallas kernels: 4.95 us -> 3.08 us  [call(): return pl.pallas_call(kernel, in_specs=in_specs, **options)(*operands)]
    pallas_call x33 -> x35, Pallas kernels: 61.8 us -> 61.8 us  [call(): return pl.pallas_call(ordered, in_specs=in_specs, **options)(*operands, dep)]
  transfers between devices with their start and end apart: 45 -> 45, of which waited for: 11 -> 10; matrix products, arithmetic and copies ran while one was open for 0% -> 0% of each run, Pallas kernels for 41% -> 45%
where the time goes in v3:
time: 132 us
  Pallas kernels  64.8 us (49%)
  starting transfers between devices  55.5 us (42%)
  waiting for transfers between devices  9.54 us (7%)
    pallas_call x35, Pallas kernels, call(): return pl.pallas_call(ordered, in_specs=in_specs, **options)(*operands, dep)  61.8 us
    ppermute x45, starting transfers between devices, send(): return lax.ppermute(value, axis, pairs)  55.5 us
    ppermute x45, waiting for transfers between devices, send(): return lax.ppermute(value, axis, pairs)  9.54 us
    pallas_call x2, Pallas kernels, call(): return pl.pallas_call(kernel, in_specs=in_specs, **options)(*operands)  3.08 us
  transfers between devices with their start and end apart: 45, of which 10 were waited for; matrix products, arithmetic and copies ran while one was open for 0% of the time, Pallas kernels for 45%

profile of v3, /device:TPU:0, one launch (start us, length us, event | category | flops | bytes accessed | tf_op | source)
XLA Modules:
  0.0 132.1 jit_solution(277000901433634511)
XLA Ops:
  0.6 3.0 %collective-permute-start.1 = (bf16[64,3072]{1,0:T(8,128)(2,1)}, bf16[64,3072]{1,0:T(8,128)(2,1)S(1)}, u32[]{:S(2)}, u32[]{:S(2)}) collective-permute-start(bf16[64,3072]{1,0:T(8,128)(2,1)} %a.1), channel_id=1, source_target_pairs={{0,2},{2,0},{1,3},{3,1},{4,6},{6,4},{5,7},{7,5},{8,10},{10,8},{9,1... | collective-permute-start | bytes 1179656 | tf_op jit(solution)/shard_map/ppermute | solution.py:43
  3.6 1.0 copy-done
  4.8 6.4 %preload.2 = (bf16[3072,1536]{1,0:T(8,128)(2,1)S(1)}, bf16[3072,1536]{1,0:T(8,128)(2,1)S(1)}) custom-call(bf16[3072,6144]{1,0:T(8,128)(2,1)} %refs_6_.9, bf16[64,3072]{1,0:T(8,128)(2,1)S(1)} %local.1.refs_1_.refs_0_), custom_call_target="tpu_custom_call" | custom-call | bytes 18874368 | tf_op jit(solution)/shard_map/preload/pallas_call | solution.py:360
  11.2 1.8 %collective-permute-done.1.refs_0_ = bf16[64,3072]{1,0:T(8,128)(2,1)S(1)} collective-permute-done((bf16[64,3072]{1,0:T(8,128)(2,1)}, bf16[64,3072]{1,0:T(8,128)(2,1)S(1)}, u32[]{:S(2)}, u32[]{:S(2)}) %collective-permute-start.1) | collective-permute-done | bytes 393248 | tf_op jit(solution)/shard_map/ppermute | solution.py:43
  13.1 1.7 %collective-permute-done.2.refs_3_ = bf16[64,3072]{1,0:T(8,128)(2,1)S(1)} collective-permute-done((bf16[64,3072]{1,0:T(8,128)(2,1)S(1)}, bf16[64,3072]{1,0:T(8,128)(2,1)S(1)}, u32[]{:S(2)}, u32[]{:S(2)}) %collective-permute-start.2) | collective-permute-done | bytes 393248 | tf_op jit(solution)/shard_map/ppermute | solution.py:43
  14.8 3.1 %forward_sums.4 = (bf16[64,1536]{1,0:T(8,128)(2,1)S(1)}, bf16[64,1536]{1,0:T(8,128)(2,1)S(1)}, bf16[64,1536]{1,0:T(8,128)(2,1)S(1)}, bf16[64,1536]{1,0:T(8,128)(...) custom-call(bf16[3072,1536]{1,0:T(8,128)(2,1)S(1)} %get-tuple-element.92.refs_1_.w_ref, ...), custom_call_target="tpu_custom_call" | custom-call | flops 2415919104 | bytes 9437184 | tf_op jit(solution)/shard_map/forward_sums/pallas_call | solution.py:358
  17.8 1.9 %collective-permute-start.3 = (bf16[64,1536]{1,0:T(8,128)(2,1)S(1)}, bf16[64,1536]{1,0:T(8,128)(2,1)S(1)}, u32[]{:S(2)}, u32[]{:S(2)}) collective-permute-start(bf16[64,1536]{1,0:T(8,128)(2,1)S(1)} %get-tuple-element.95.refs_1_), channel_id=1, source_target_pairs={{0,4},{1,5},{2,6},{3,7},{4,0},{5,1},{6,2},{7,3},{8,12},{9,13},{10,... | collective-permute-start | bytes 589832 | tf_op jit(solution)/shard_map/ppermute | solution.py:43
  19.7 3.0 %forward_sums.5 = (bf16[64,1536]{1,0:T(8,128)(2,1)S(1)}, bf16[64,1536]{1,0:T(8,128)(2,1)S(1)}, bf16[64,1536]{1,0:T(8,128)(2,1)S(1)}, bf16[64,1536]{1,0:T(8,128)(2,1)S(1)}, f32[8,128]{1,0:T(8,128)S(1)}) custom-call(bf16[3072,1536]{1,0:T(8,128)(2,1)S(1)} %get-tuple-element.96.refs_0_, bf16[256,3072]{1,0:T(8,128)(2,1)S(1)} %get-tuple-element.93.refs_1_.refs_7_.refs_8_.refs_12_, ...), custom_call_target="tpu_custom_call" | custom-call | flops 2415919104 | bytes 9437184 | tf_op jit(solution)/shard_map/forward_sums/pallas_call | solution.py:360
  22.8 0.3 collective-permute-start.6
  23.0 2.0 %collective-permute-done.3.refs_2_ = bf16[64,1536]{1,0:T(8,128)(2,1)S(1)} collective-permute-done((bf16[64,1536]{1,0:T(8,128)(2,1)S(1)}, bf16[64,1536]{1,0:T(8,128)(2,1)S(1)}, u32[]{:S(2)}, u32[]{:S(2)}) %collective-permute-start.3) | collective-permute-done | bytes 196640 | tf_op jit(solution)/shard_map/ppermute | solution.py:43
  25.0 2.5 %collective-permute-start.5 = (bf16[64,1536]{1,0:T(8,128)(2,1)S(1)}, bf16[64,1536]{1,0:T(8,128)(2,1)S(1)}, u32[]{:S(2)}, u32[]{:S(2)}) collective-permute-start(bf16[64,1536]{1,0:T(8,128)(2,1)S(1)} %get-tuple-element.99.refs_2_), channel_id=1, source_target_pairs={{0,4},{1,5},{2,6},{3,7},{4,0},{5,1},{6,2},{7,3},{8,12},{9,13},{10,... | collective-permute-start | bytes 589832 | tf_op jit(solution)/shard_map/ppermute | solution.py:43
  27.6 4.9 %forward_sums.6 = (bf16[64,1536]{1,0:T(8,128)(2,1)S(1)}, bf16[64,1536]{1,0:T(8,128)(2,1)S(1)}, bf16[64,1536]{1,0:T(8,128)(2,1)S(1)}, bf16[64,1536]{1,0:T(8,128)(2,1)S(1)}, f32[8,128]{1,0:T(8,128)S(1)}) custom-call(bf16[3072,6144]{1,0:T(8,128)(2,1)} %refs_6_.9, bf16[256,3072]{1,0:T(8,128)(2,1)S(1)} %get-tuple-element.93.refs_1_.refs_7_.refs_8_.refs_12_, ...), custom_call_target="tpu_custom_call" | custom-call | flops 2415919104 | bytes 9437184 | tf_op jit(solution)/shard_map/forward_sums/pallas_call | solution.py:360
  32.6 3.2 %collective-permute-start.10 = (bf16[64,1536]{1,0:T(8,128)(2,1)S(1)}, bf16[64,1536]{1,0:T(8,128)(2,1)S(1)}, u32[]{:S(2)}, u32[]{:S(2)}) collective-permute-start(bf16[64,1536]{1,0:T(8,128)(2,1)S(1)} %get-tuple-element.110.refs_4_), channel_id=1, source_target_pairs={{0,4},{1,5},{2,6},{3,7},{4,0},{5,1},{6,2},{7,3},{8,12},{9,13},{10,... | collective-permute-start | bytes 589832 | tf_op jit(solution)/shard_map/ppermute | solution.py:43
  35.9 0.2 collective-permute-start.7
  36.0 0.5 collective-permute-start.8
  36.5 4.9 %forward_sums.7 = (bf16[64,1536]{1,0:T(8,128)(2,1)S(1)}, bf16[64,1536]{1,0:T(8,128)(2,1)S(1)}, bf16[64,1536]{1,0:T(8,128)(2,1)S(1)}, bf16[64,1536]{1,0:T(8,128)(2,1)S(1)}, f32[8,128]{1,0:T(8,128)S(1)}) custom-call(bf16[3072,6144]{1,0:T(8,128)(2,1)} %refs_6_.9, bf16[256,3072]{1,0:T(8,128)(2,1)S(1)} %get-tuple-element.93.refs_1_.refs_7_.refs_8_.refs_12_, ...), custom_call_target="tpu_custom_call" | custom-call | flops 2415919104 | bytes 9437184 | tf_op jit(solution)/shard_map/forward_sums/pallas_call | solution.py:360
  41.5 2.1 %collective-permute-start.13 = (bf16[64,1536]{1,0:T(8,128)(2,1)S(1)}, bf16[64,1536]{1,0:T(8,128)(2,1)S(1)}, u32[]{:S(2)}, u32[]{:S(2)}) collective-permute-start(bf16[64,1536]{1,0:T(8,128)(2,1)S(1)} %get-tuple-element.116.refs_4_), channel_id=1, source_target_pairs={{0,4},{1,5},{2,6},{3,7},{4,0},{5,1},{6,2},{7,3},{8,12},{9,13},{10,... | collective-permute-start | bytes 589832 | tf_op jit(solution)/shard_map/ppermute | solution.py:43
  43.7 0.5 collective-permute-done.7.refs_1_
  44.2 0.4 gelu.4
  44.6 0.1 collective-permute-start.11
  44.7 2.9 %collective-permute-start.12 = (bf16[64,1536]{1,0:T(8,128)(2,1)S(1)}, bf16[64,1536]{1,0:T(8,128)(2,1)S(1)}, u32[]{:S(2)}, u32[]{:S(2)}) collective-permute-start(bf16[64,1536]{1,0:T(8,128)(2,1)S(1)} %get-tuple-element.117.refs_0_), channel_id=1, source_target_pairs={{0,4},{1,5},{2,6},{3,7},{4,0},{5,1},{6,2},{7,3},{8,12},{9,13},{10,... | collective-permute-start | bytes 589832 | tf_op jit(solution)/shard_map/ppermute | solution.py:43
  47.6 1.5 %collective-permute-done.13.refs_1_ = bf16[64,1536]{1,0:T(8,128)(2,1)S(1)} collective-permute-done((bf16[64,1536]{1,0:T(8,128)(2,1)S(1)}, bf16[64,1536]{1,0:T(8,128)(2,1)S(1)}, u32[]{:S(2)}, u32[]{:S(2)}) %collective-permute-start.13) | collective-permute-done | bytes 196640 | tf_op jit(solution)/shard_map/ppermute | solution.py:43
  49.1 0.4 gelu.5
  49.6 3.8 %collective-permute-start.18 = (bf16[64,1536]{1,0:T(8,128)(2,1)S(1)}, bf16[64,1536]{1,0:T(8,128)(2,1)S(1)}, u32[]{:S(2)}, u32[]{:S(2)}) collective-permute-start(bf16[64,1536]{1,0:T(8,128)(2,1)S(1)} %get-tuple-element.125.refs_0_), channel_id=1, source_target_pairs={{0,4},{1,5},{2,6},{3,7},{4,0},{5,1},{6,2},{7,3},{8,12},{9,13},{10,... | collective-permute-start | bytes 589832 | tf_op jit(solution)/shard_map/ppermute | solution.py:43
  53.5 0.1 collective-permute-start.15
  53.5 3.7 %collective-permute-start.16 = (bf16[64,1536]{1,0:T(8,128)(2,1)S(1)}, bf16[64,1536]{1,0:T(8,128)(2,1)S(1)}, u32[]{:S(2)}, u32[]{:S(2)}) collective-permute-start(bf16[64,1536]{1,0:T(8,128)(2,1)S(1)} %get-tuple-element.123.refs_3_), channel_id=1, source_target_pairs={{0,4},{1,5},{2,6},{3,7},{4,0},{5,1},{6,2},{7,3},{8,12},{9,13},{10,... | collective-permute-start | bytes 589832 | tf_op jit(solution)/shard_map/ppermute | solution.py:43
  57.3 0.3 collective-permute-done.18.refs_2_.refs_1_
  57.7 4.2 %collective-permute-start.22 = (bf16[64,1536]{1,0:T(8,128)(2,1)S(1)}, bf16[64,1536]{1,0:T(8,128)(2,1)S(1)}, u32[]{:S(2)}, u32[]{:S(2)}) collective-permute-start(bf16[64,1536]{1,0:T(8,128)(2,1)S(1)} %get-tuple-element.126.refs_4_), channel_id=1, source_target_pairs={{0,4},{1,5},{2,6},{3,7},{4,0},{5,1},{6,2},{7,3},{8,12},{9,13},{10,... | collective-permute-start | bytes 589832 | tf_op jit(solution)/shard_map/ppermute | solution.py:43
  62.0 0.1 collective-permute-start.19
  62.1 3.6 %collective-permute-start.20 = (bf16[64,1536]{1,0:T(8,128)(2,1)S(1)}, bf16[64,1536]{1,0:T(8,128)(2,1)S(1)}, u32[]{:S(2)}, u32[]{:S(2)}) collective-permute-start(bf16[64,1536]{1,0:T(8,128)(2,1)S(1)} %get-tuple-element.128.refs_4_), channel_id=1, source_target_pairs={{0,4},{1,5},{2,6},{3,7},{4,0},{5,1},{6,2},{7,3},{8,12},{9,13},{10,... | collective-permute-start | bytes 589832 | tf_op jit(solution)/shard_map/ppermute | solution.py:43
  65.7 0.4 collective-permute-done.22.refs_3_
  66.2 0.1 collective-permute-start.25
  66.3 3.8 %collective-permute-start.26 = (bf16[64,1536]{1,0:T(8,128)(2,1)S(1)}, bf16[64,1536]{1,0:T(8,128)(2,1)S(1)}, u32[]{:S(2)}, u32[]{:S(2)}) collective-permute-start(bf16[64,1536]{1,0:T(8,128)(2,1)S(1)} %get-tuple-element.131.refs_4_), channel_id=1, source_target_pairs={{0,4},{1,5},{2,6},{3,7},{4,0},{5,1},{6,2},{7,3},{8,12},{9,13},{10,... | collective-permute-start | bytes 589832 | tf_op jit(solution)/shard_map/ppermute | solution.py:43
  70.1 0.2 collective-permute-done.20.refs_3_.refs_5_
  70.3 2.6 %collective-permute-start.23 = (bf16[64,1536]{1,0:T(8,128)(2,1)S(1)}, bf16[64,1536]{1,0:T(8,128)(2,1)S(1)}, u32[]{:S(2)}, u32[]{:S(2)}) collective-permute-start(bf16[64,1536]{1,0:T(8,128)(2,1)S(1)} %get-tuple-element.132.refs_9_), channel_id=1, source_target_pairs={{0,4},{1,5},{2,6},{3,7},{4,0},{5,1},{6,2},{7,3},{8,12},{9,13},{10,... | collective-permute-start | bytes 589832 | tf_op jit(solution)/shard_map/ppermute | solution.py:43
  72.9 4.7 %grads.8 = (f32[256,1536]{1,0:T(8,128)S(1)}, bf16[3072,6144]{1,0:T(8,128)(2,1)}, bf16[64,6144]{1,0:T(8,128)(2,1)}, f32[8,128]{1,0:T(8,128)S(1)}) custom-call(bf16[64,1536]{1,0:T(8,128)(2,1)S(1)} %get-tuple-element.117.refs_0_, bf16[64,1536]{1,0:T(8,128)(2,1)S(1)} %collective-permute-done.12.refs_2_.refs_1_, ...), custom_call_target="tpu_custom_call" | custom-call | flops 2415919104 | bytes 9437184 | tf_op jit(solution)/shard_map/grads/pallas_call | solution.py:360
  77.7 1.6 %collective-permute-start.29 = (bf16[64,1536]{1,0:T(8,128)(2,1)S(1)}, bf16[64,1536]{1,0:T(8,128)(2,1)S(1)}, u32[]{:S(2)}, u32[]{:S(2)}) collective-permute-start(bf16[64,1536]{1,0:T(8,128)(2,1)S(1)} %get-tuple-element.137.refs_4_), channel_id=1, source_target_pairs={{0,4},{1,5},{2,6},{3,7},{4,0},{5,1},{6,2},{7,3},{8,12},{9,13},{10,... | collective-permute-start | bytes 589832 | tf_op jit(solution)/shard_map/ppermute | solution.py:43
  79.3 0.4 gelu.6
  79.7 2.0 %collective-permute-start.27 = (bf16[64,1536]{1,0:T(8,128)(2,1)S(1)}, bf16[64,1536]{1,0:T(8,128)(2,1)S(1)}, u32[]{:S(2)}, u32[]{:S(2)}) collective-permute-start(bf16[64,1536]{1,0:T(8,128)(2,1)S(1)} %get-tuple-element.138.refs_0_), channel_id=1, source_target_pairs={{0,4},{1,5},{2,6},{3,7},{4,0},{5,1},{6,2},{7,3},{8,12},{9,13},{10,... | collective-permute-start | bytes 589832 | tf_op jit(solution)/shard_map/ppermute | solution.py:43
  81.7 4.7 %grads.9 = (f32[256,1536]{1,0:T(8,128)S(1)}, bf16[3072,6144]{1,0:T(8,128)(2,1)}, f32[8,128]{1,0:T(8,128)S(1)}) custom-call(bf16[64,1536]{1,0:T(8,128)(2,1)S(1)} %get-tuple-element.117.refs_0_, bf16[64,1536]{1,0:T(8,128)(2,1)S(1)} %collective-permute-done.12.refs_2_.refs_1_, ...), custom_call_target="tpu_custom_call", output_to_operand_aliasing={{1}: (8, {})} | custom-call | flops 2415919104 | bytes 9437184 | tf_op jit(solution)/shard_map/grads/pallas_call | solution.py:360
  86.4 0.4 gelu.7
  86.8 0.6 collective-permute-start.33
  87.4 2.0 %collective-permute-start.34 = (bf16[64,1536]{1,0:T(8,128)(2,1)S(1)}, bf16[64,1536]{1,0:T(8,128)(2,1)S(1)}, u32[]{:S(2)}, u32[]{:S(2)}) collective-permute-start(bf16[64,1536]{1,0:T(8,128)(2,1)S(1)} %get-tuple-element.147.refs_0_.refs_6_), channel_id=1, source_target_pairs={{0,4},{1,5},{2,6},{3,7},{4,0},{5,1},{6,2},{7,3},{8,12},{9,13},{10,... | collective-permute-start | bytes 589832 | tf_op jit(solution)/shard_map/ppermute | solution.py:43
  89.5 0.1 collective-permute-start.32
  89.6 3.7 %collective-permute-start.31 = (bf16[64,1536]{1,0:T(8,128)(2,1)S(1)}, bf16[64,1536]{1,0:T(8,128)(2,1)S(1)}, u32[]{:S(2)}, u32[]{:S(2)}) collective-permute-start(bf16[64,1536]{1,0:T(8,128)(2,1)S(1)} %get-tuple-element.145.refs_12_), channel_id=1, source_target_pairs={{0,4},{1,5},{2,6},{3,7},{4,0},{5,1},{6,2},{7,3},{8,12},{9,13},{10,... | collective-permute-start | bytes 589832 | tf_op jit(solution)/shard_map/ppermute | solution.py:43
  93.3 4.7 %grads.10 = (f32[256,1536]{1,0:T(8,128)S(1)}, bf16[3072,6144]{1,0:T(8,128)(2,1)}, bf16[64,6144]{1,0:T(8,128)(2,1)}, f32[8,128]{1,0:T(8,128)S(1)}) custom-call(bf16[64,1536]{1,0:T(8,128)(2,1)S(1)} %get-tuple-element.125.refs_0_, bf16[64,1536]{1,0:T(8,128)(2,1)S(1)} %collective-permute-done.18.refs_2_.refs_1_, ...), custom_call_target="tpu_custom_call", output_to_operand_aliasing={{1}: (9, {}), {2}: (11, {})} | custom-call | flops 2415919104 | bytes 9437184 | tf_op jit(solution)/shard_map/grads/pallas_call | solution.py:360
  98.2 0.6 collective-permute-start.36
  98.8 1.6 %collective-permute-start.35 = (bf16[64,1536]{1,0:T(8,128)(2,1)S(1)}, bf16[64,1536]{1,0:T(8,128)(2,1)S(1)}, u32[]{:S(2)}, u32[]{:S(2)}) collective-permute-start(bf16[64,1536]{1,0:T(8,128)(2,1)S(1)} %relay_far.2.refs_10_), channel_id=1, source_target_pairs={{0,4},{1,5},{2,6},{3,7},{4,0},{5,1},{6,2},{7,3},{8,12},{9,13},{10,... | collective-permute-start | bytes 589832 | tf_op jit(solution)/shard_map/ppermute | solution.py:43
  100.3 4.7 %grads.11 = (f32[256,1536]{1,0:T(8,128)S(1)}, bf16[3072,6144]{1,0:T(8,128)(2,1)}, f32[8,128]{1,0:T(8,128)S(1)}) custom-call(bf16[64,1536]{1,0:T(8,128)(2,1)S(1)} %get-tuple-element.125.refs_0_, bf16[64,1536]{1,0:T(8,128)(2,1)S(1)} %collective-permute-done.18.refs_2_.refs_1_, ...), custom_call_target="tpu_custom_call", output_to_operand_aliasing={{1}: (9, {})} | custom-call | flops 2415919104 | bytes 9437184 | tf_op jit(solution)/shard_map/grads/pallas_call | solution.py:360
  105.0 3.7 %preload.3.refs_9_.refs_6_ = bf16[3072,1536]{1,0:T(8,128)(2,1)S(1)} custom-call(bf16[3072,6144]{1,0:T(8,128)(2,1)} %refs_6_.9, bf16[64,1536]{1,0:T(8,128)(2,1)S(1)} %relay_far.3.refs_1_), custom_call_target="tpu_custom_call" | custom-call | bytes 9437184 | tf_op jit(solution)/shard_map/preload/pallas_call | solution.py:360
  108.7 0.6 collective-permute-start.38
  109.3 0.4 collective-permute-done.35.refs_5_
  109.7 5.1 %grads.12 = (f32[256,1536]{1,0:T(8,128)S(1)}, f32[256,1536]{1,0:T(8,128)S(1)}, f32[8,128]{1,0:T(8,128)S(1)}) custom-call(bf16[64,1536]{1,0:T(8,128)(2,1)S(1)} %get-tuple-element.138.refs_0_, bf16[64,1536]{1,0:T(8,128)(2,1)S(1)} %collective-permute-done.27.refs_1_, bf16[64,1536]{1,0:T(8,128)(2,1)S(1)} %collective-permute-done.28.refs_0_.refs_2_, ...), custom_call_target="tpu_custom_call" | custom-call | flops 2415919104 | bytes 9437184 | tf_op jit(solution)/shard_map/grads/pallas_call | solution.py:360
  114.8 0.7 collective-permute-done.38.refs_5_.refs_11_
  115.5 1.9 %grads.13 = (bf16[64,1536]{1,0:T(8,128)(2,1)S(1)}, bf16[64,1536]{1,0:T(8,128)(2,1)S(1)}, bf16[64,1536]{1,0:T(8,128)(2,1)S(1)}, bf16[64,1536]{1,0:T(8,128)(2,1)S(1)}, f32[8,128]{1,0:T(8,128)S(1)}) custom-call(bf16[64,1536]{1,0:T(8,128)(2,1)S(1)} %get-tuple-element.147.refs_0_.refs_6_, bf16[64,1536]{1,0:T(8,128)(2,1)S(1)} %collective-permute-done.34.refs_1_.refs_7_, ...), custom_call_target="tpu_custom_call" | custom-call | flops 1207959552 | bytes 4718592 | tf_op jit(solution)/shard_map/grads/pallas_call | solution.py:360
  117.4 0.1 collective-permute-start.40
  117.5 1.9 %grads.14 = (bf16[64,1536]{1,0:T(8,128)(2,1)S(1)}, bf16[64,1536]{1,0:T(8,128)(2,1)S(1)}, bf16[64,1536]{1,0:T(8,128)(2,1)S(1)}, bf16[64,1536]{1,0:T(8,128)(2,1)S(1)}, f32[8,128]{1,0:T(8,128)S(1)}) custom-call(bf16[64,1536]{1,0:T(8,128)(2,1)S(1)} %get-tuple-element.147.refs_0_.refs_6_, bf16[64,1536]{1,0:T(8,128)(2,1)S(1)} %collective-permute-done.34.refs_1_.refs_7_, ...), custom_call_target="tpu_custom_call" | custom-call | flops 1207959552 | bytes 4718592 | tf_op jit(solution)/shard_map/grads/pallas_call | solution.py:360
  119.4 0.6 collective-permute-start.39
  120.0 1.5 %collective-permute-start.41 = (bf16[64,1536]{1,0:T(8,128)(2,1)S(1)}, bf16[64,1536]{1,0:T(8,128)(2,1)S(1)}, u32[]{:S(2)}, u32[]{:S(2)}) collective-permute-start(bf16[64,1536]{1,0:T(8,128)(2,1)S(1)} %get-tuple-element.172.refs_3_), channel_id=1, source_target_pairs={{0,2},{2,0},{1,3},{3,1},{4,6},{6,4},{5,7},{7,5},{8,10},{10,8},{9,1... | collective-permute-start | bytes 589832 | tf_op jit(solution)/shard_map/ppermute | solution.py:43
  121.6 1.0 collective-permute-start.43
  122.7 0.1 collective-permute-start.44
  122.7 0.4 collective-permute-start.42
  123.2 8.0 %grads.15 = (bf16[3072,6144]{1,0:T(8,128)(2,1)}, bf16[64,6144]{1,0:T(8,128)(2,1)}, f32[8,128]{1,0:T(8,128)S(1)}) custom-call(bf16[64,1536]{1,0:T(8,128)(2,1)S(1)} %get-tuple-element.138.refs_0_, bf16[64,1536]{1,0:T(8,128)(2,1)S(1)} %collective-permute-done.27.refs_1_, ...), custom_call_target="tpu_custom_call", output_to_operand_aliasing={{0}: (13, {}), {1}: (16, {})} | custom-call | flops 4831838208 | bytes 18874368 | tf_op jit(solution)/shard_map/grads/pallas_call | solution.py:360
  131.2 0.9 finish.1
  (68 shorter events, 1.1 us)
Async XLA Ops:
  0.6 12.3 %collective-permute-start.1 = (bf16[64,3072]{1,0:T(8,128)(2,1)}, bf16[64,3072]{1,0:T(8,128)(2,1)S(1)}, u32[]{:S(2)}, u32[]{:S(2)}) collective-permute-start(bf16[64,3072]{1,0:T(8,128)(2,1)} %a.1), channel_id=1, source_target_pairs={{0,2},{2,0},{1,3},{3,1},{4,6},{6,4},{5,7},{7,5},{8,10},{10,8},{9,1... | collective-permute-start | bytes 1179656 | tf_op jit(solution)/shard_map/ppermute | solution.py:43
  3.6 1.0 copy-start
  4.7 8.4 %collective-permute-start = (bf16[64,3072]{1,0:T(8,128)(2,1)S(1)}, bf16[64,3072]{1,0:T(8,128)(2,1)S(1)}, u32[]{:S(2)}, u32[]{:S(2)}) collective-permute-start(bf16[64,3072]{1,0:T(8,128)(2,1)S(1)} %local.1.refs_1_.refs_0_), channel_id=1, source_target_pairs={{0,1},{1,0},{2,3},{3,2},{4,5},{5,4},{6,7},{7,6},{8,9},{9,8},{10,11... | collective-permute-start | bytes 1179656 | tf_op jit(solution)/shard_map/ppermute | solution.py:43
  13.0 1.8 %collective-permute-start.2 = (bf16[64,3072]{1,0:T(8,128)(2,1)S(1)}, bf16[64,3072]{1,0:T(8,128)(2,1)S(1)}, u32[]{:S(2)}, u32[]{:S(2)}) collective-permute-start(bf16[64,3072]{1,0:T(8,128)(2,1)S(1)} %corner.1.refs_2_), channel_id=1, source_target_pairs={{0,1},{1,0},{2,3},{3,2},{4,5},{5,4},{6,7},{7,6},{8,9},{9,8},{10,11... | collective-permute-start | bytes 1179656 | tf_op jit(solution)/shard_map/ppermute | solution.py:43
  17.8 7.2 %collective-permute-start.3 = (bf16[64,1536]{1,0:T(8,128)(2,1)S(1)}, bf16[64,1536]{1,0:T(8,128)(2,1)S(1)}, u32[]{:S(2)}, u32[]{:S(2)}) collective-permute-start(bf16[64,1536]{1,0:T(8,128)(2,1)S(1)} %get-tuple-element.95.refs_1_), channel_id=1, source_target_pairs={{0,4},{1,5},{2,6},{3,7},{4,0},{5,1},{6,2},{7,3},{8,12},{9,13},{10,... | collective-permute-start | bytes 589832 | tf_op jit(solution)/shard_map/ppermute | solution.py:43
  22.8 9.8 %collective-permute-start.6 = (bf16[64,1536]{1,0:T(8,128)(2,1)S(1)}, bf16[64,1536]{1,0:T(8,128)(2,1)S(1)}, u32[]{:S(2)}, u32[]{:S(2)}) collective-permute-start(bf16[64,1536]{1,0:T(8,128)(2,1)S(1)} %get-tuple-element.108.refs_1_), channel_id=1, source_target_pairs={{0,4},{1,5},{2,6},{3,7},{4,0},{5,1},{6,2},{7,3},{8,12},{9,13},{10,... | collective-permute-start | bytes 589832 | tf_op jit(solution)/shard_map/ppermute | solution.py:43
  25.0 10.8 %collective-permute-start.5 = (bf16[64,1536]{1,0:T(8,128)(2,1)S(1)}, bf16[64,1536]{1,0:T(8,128)(2,1)S(1)}, u32[]{:S(2)}, u32[]{:S(2)}) collective-permute-start(bf16[64,1536]{1,0:T(8,128)(2,1)S(1)} %get-tuple-element.99.refs_2_), channel_id=1, source_target_pairs={{0,4},{1,5},{2,6},{3,7},{4,0},{5,1},{6,2},{7,3},{8,12},{9,13},{10,... | collective-permute-start | bytes 589832 | tf_op jit(solution)/shard_map/ppermute | solution.py:43
  27.6 8.2 %collective-permute-start.4 = (bf16[64,1536]{1,0:T(8,128)(2,1)S(1)}, bf16[64,1536]{1,0:T(8,128)(2,1)S(1)}, u32[]{:S(2)}, u32[]{:S(2)}) collective-permute-start(bf16[64,1536]{1,0:T(8,128)(2,1)S(1)} %get-tuple-element.106), channel_id=1, source_target_pairs={{0,1},{1,0},{2,3},{3,2},{4,8},{5,9},{6,10},{7,11},{8,4},{9,5},{10,... | collective-permute-start | bytes 589832 | tf_op jit(solution)/shard_map/ppermute | solution.py:43
  32.6 8.9 %collective-permute-start.10 = (bf16[64,1536]{1,0:T(8,128)(2,1)S(1)}, bf16[64,1536]{1,0:T(8,128)(2,1)S(1)}, u32[]{:S(2)}, u32[]{:S(2)}) collective-permute-start(bf16[64,1536]{1,0:T(8,128)(2,1)S(1)} %get-tuple-element.110.refs_4_), channel_id=1, source_target_pairs={{0,4},{1,5},{2,6},{3,7},{4,0},{5,1},{6,2},{7,3},{8,12},{9,13},{10,... | collective-permute-start | bytes 589832 | tf_op jit(solution)/shard_map/ppermute | solution.py:43
  35.8 5.7 %collective-permute-start.9 = (bf16[64,1536]{1,0:T(8,128)(2,1)S(1)}, bf16[64,1536]{1,0:T(8,128)(2,1)S(1)}, u32[]{:S(2)}, u32[]{:S(2)}) collective-permute-start(bf16[64,1536]{1,0:T(8,128)(2,1)S(1)} %get-tuple-element.114), channel_id=1, source_target_pairs={{0,1},{1,0},{2,3},{3,2},{4,8},{5,9},{6,10},{7,11},{8,4},{9,5},{10,... | collective-permute-start | bytes 589832 | tf_op jit(solution)/shard_map/ppermute | solution.py:43
  35.9 8.3 %collective-permute-start.7 = (bf16[64,1536]{1,0:T(8,128)(2,1)S(1)}, bf16[64,1536]{1,0:T(8,128)(2,1)S(1)}, u32[]{:S(2)}, u32[]{:S(2)}) collective-permute-start(bf16[64,1536]{1,0:T(8,128)(2,1)S(1)} %get-tuple-element.111.refs_2_), channel_id=1, source_target_pairs={{0,4},{1,5},{2,6},{3,7},{4,0},{5,1},{6,2},{7,3},{8,12},{9,13},{10,... | collective-permute-start | bytes 589832 | tf_op jit(solution)/shard_map/ppermute | solution.py:43
  36.0 7.6 %copy-start.1 = (bf16[64,6144]{1,0:T(8,128)(2,1)S(1)}, bf16[64,6144]{1,0:T(8,128)(2,1)}, u32[]{:S(2)}) copy-start(bf16[64,6144]{1,0:T(8,128)(2,1)} %param.5) | copy-start | bytes 2359300
  36.0 8.1 %collective-permute-start.8 = (bf16[64,1536]{1,0:T(8,128)(2,1)S(1)}, bf16[64,1536]{1,0:T(8,128)(2,1)S(1)}, u32[]{:S(2)}, u32[]{:S(2)}) collective-permute-start(bf16[64,1536]{1,0:T(8,128)(2,1)S(1)} %get-tuple-element.112), channel_id=1, source_target_pairs={{0,1},{1,0},{2,3},{3,2},{4,8},{5,9},{6,10},{7,11},{8,4},{9,5},{10,... | collective-permute-start | bytes 589832 | tf_op jit(solution)/shard_map/ppermute | solution.py:43
  41.5 7.6 %collective-permute-start.13 = (bf16[64,1536]{1,0:T(8,128)(2,1)S(1)}, bf16[64,1536]{1,0:T(8,128)(2,1)S(1)}, u32[]{:S(2)}, u32[]{:S(2)}) collective-permute-start(bf16[64,1536]{1,0:T(8,128)(2,1)S(1)} %get-tuple-element.116.refs_4_), channel_id=1, source_target_pairs={{0,4},{1,5},{2,6},{3,7},{4,0},{5,1},{6,2},{7,3},{8,12},{9,13},{10,... | collective-permute-start | bytes 589832 | tf_op jit(solution)/shard_map/ppermute | solution.py:43
  43.6 5.5 %collective-permute-start.14 = (bf16[64,1536]{1,0:T(8,128)(2,1)S(1)}, bf16[64,1536]{1,0:T(8,128)(2,1)S(1)}, u32[]{:S(2)}, u32[]{:S(2)}) collective-permute-start(bf16[64,1536]{1,0:T(8,128)(2,1)S(1)} %get-tuple-element.119), channel_id=1, source_target_pairs={{0,1},{1,0},{2,3},{3,2},{4,8},{5,9},{6,10},{7,11},{8,4},{9,5},{10,... | collective-permute-start | bytes 589832 | tf_op jit(solution)/shard_map/ppermute | solution.py:43
  44.6 8.8 %collective-permute-start.11 = (bf16[64,1536]{1,0:T(8,128)(2,1)S(1)}, bf16[64,1536]{1,0:T(8,128)(2,1)S(1)}, u32[]{:S(2)}, u32[]{:S(2)}) collective-permute-start(bf16[64,1536]{1,0:T(8,128)(2,1)S(1)} %get-tuple-element.117.refs_0_), channel_id=1, source_target_pairs={{0,1},{1,0},{2,3},{3,2},{4,8},{5,9},{6,10},{7,11},{8,4},{9,5},{10,... | collective-permute-start | bytes 589832 | tf_op jit(solution)/shard_map/ppermute | solution.py:43
  44.7 8.7 %collective-permute-start.12 = (bf16[64,1536]{1,0:T(8,128)(2,1)S(1)}, bf16[64,1536]{1,0:T(8,128)(2,1)S(1)}, u32[]{:S(2)}, u32[]{:S(2)}) collective-permute-start(bf16[64,1536]{1,0:T(8,128)(2,1)S(1)} %get-tuple-element.117.refs_0_), channel_id=1, source_target_pairs={{0,4},{1,5},{2,6},{3,7},{4,0},{5,1},{6,2},{7,3},{8,12},{9,13},{10,... | collective-permute-start | bytes 589832 | tf_op jit(solution)/shard_map/ppermute | solution.py:43
  49.5 7.7 %collective-permute-start.17 = (bf16[64,1536]{1,0:T(8,128)(2,1)S(1)}, bf16[64,1536]{1,0:T(8,128)(2,1)S(1)}, u32[]{:S(2)}, u32[]{:S(2)}) collective-permute-start(bf16[64,1536]{1,0:T(8,128)(2,1)S(1)} %get-tuple-element.125.refs_0_), channel_id=1, source_target_pairs={{0,1},{1,0},{2,3},{3,2},{4,8},{5,9},{6,10},{7,11},{8,4},{9,5},{10,... | collective-permute-start | bytes 589832 | tf_op jit(solution)/shard_map/ppermute | solution.py:43
  49.6 8.0 %collective-permute-start.18 = (bf16[64,1536]{1,0:T(8,128)(2,1)S(1)}, bf16[64,1536]{1,0:T(8,128)(2,1)S(1)}, u32[]{:S(2)}, u32[]{:S(2)}) collective-permute-start(bf16[64,1536]{1,0:T(8,128)(2,1)S(1)} %get-tuple-element.125.refs_0_), channel_id=1, source_target_pairs={{0,4},{1,5},{2,6},{3,7},{4,0},{5,1},{6,2},{7,3},{8,12},{9,13},{10,... | collective-permute-start | bytes 589832 | tf_op jit(solution)/shard_map/ppermute | solution.py:43
  53.5 8.5 %collective-permute-start.15 = (bf16[64,1536]{1,0:T(8,128)(2,1)S(1)}, bf16[64,1536]{1,0:T(8,128)(2,1)S(1)}, u32[]{:S(2)}, u32[]{:S(2)}) collective-permute-start(bf16[64,1536]{1,0:T(8,128)(2,1)S(1)} %get-tuple-element.122), channel_id=1, source_target_pairs={{0,1},{1,0},{2,3},{3,2},{4,8},{5,9},{6,10},{7,11},{8,4},{9,5},{10,... | collective-permute-start | bytes 589832 | tf_op jit(solution)/shard_map/ppermute | solution.py:43
  53.5 8.4 %collective-permute-start.16 = (bf16[64,1536]{1,0:T(8,128)(2,1)S(1)}, bf16[64,1536]{1,0:T(8,128)(2,1)S(1)}, u32[]{:S(2)}, u32[]{:S(2)}) collective-permute-start(bf16[64,1536]{1,0:T(8,128)(2,1)S(1)} %get-tuple-element.123.refs_3_), channel_id=1, source_target_pairs={{0,4},{1,5},{2,6},{3,7},{4,0},{5,1},{6,2},{7,3},{8,12},{9,13},{10,... | collective-permute-start | bytes 589832 | tf_op jit(solution)/shard_map/ppermute | solution.py:43
  57.6 8.1 %collective-permute-start.21 = (bf16[64,1536]{1,0:T(8,128)(2,1)S(1)}, bf16[64,1536]{1,0:T(8,128)(2,1)S(1)}, u32[]{:S(2)}, u32[]{:S(2)}) collective-permute-start(bf16[64,1536]{1,0:T(8,128)(2,1)S(1)} %get-tuple-element.130), channel_id=1, source_target_pairs={{0,1},{1,0},{2,3},{3,2},{4,8},{5,9},{6,10},{7,11},{8,4},{9,5},{10,... | collective-permute-start | bytes 589832 | tf_op jit(solution)/shard_map/ppermute | solution.py:43
  57.7 8.5 %collective-permute-start.22 = (bf16[64,1536]{1,0:T(8,128)(2,1)S(1)}, bf16[64,1536]{1,0:T(8,128)(2,1)S(1)}, u32[]{:S(2)}, u32[]{:S(2)}) collective-permute-start(bf16[64,1536]{1,0:T(8,128)(2,1)S(1)} %get-tuple-element.126.refs_4_), channel_id=1, source_target_pairs={{0,4},{1,5},{2,6},{3,7},{4,0},{5,1},{6,2},{7,3},{8,12},{9,13},{10,... | collective-permute-start | bytes 589832 | tf_op jit(solution)/shard_map/ppermute | solution.py:43
  62.0 8.1 %collective-permute-start.19 = (bf16[64,1536]{1,0:T(8,128)(2,1)S(1)}, bf16[64,1536]{1,0:T(8,128)(2,1)S(1)}, u32[]{:S(2)}, u32[]{:S(2)}) collective-permute-start(bf16[64,1536]{1,0:T(8,128)(2,1)S(1)} %get-tuple-element.127), channel_id=1, source_target_pairs={{0,1},{1,0},{2,3},{3,2},{4,8},{5,9},{6,10},{7,11},{8,4},{9,5},{10,... | collective-permute-start | bytes 589832 | tf_op jit(solution)/shard_map/ppermute | solution.py:43
  62.1 8.2 %collective-permute-start.20 = (bf16[64,1536]{1,0:T(8,128)(2,1)S(1)}, bf16[64,1536]{1,0:T(8,128)(2,1)S(1)}, u32[]{:S(2)}, u32[]{:S(2)}) collective-permute-start(bf16[64,1536]{1,0:T(8,128)(2,1)S(1)} %get-tuple-element.128.refs_4_), channel_id=1, source_target_pairs={{0,4},{1,5},{2,6},{3,7},{4,0},{5,1},{6,2},{7,3},{8,12},{9,13},{10,... | collective-permute-start | bytes 589832 | tf_op jit(solution)/shard_map/ppermute | solution.py:43
  66.2 11.5 %collective-permute-start.25 = (bf16[64,1536]{1,0:T(8,128)(2,1)S(1)}, bf16[64,1536]{1,0:T(8,128)(2,1)S(1)}, u32[]{:S(2)}, u32[]{:S(2)}) collective-permute-start(bf16[64,1536]{1,0:T(8,128)(2,1)S(1)} %get-tuple-element.135), channel_id=1, source_target_pairs={{0,1},{1,0},{2,3},{3,2},{4,8},{5,9},{6,10},{7,11},{8,4},{9,5},{10,... | collective-permute-start | bytes 589832 | tf_op jit(solution)/shard_map/ppermute | solution.py:43
  66.3 11.4 %collective-permute-start.26 = (bf16[64,1536]{1,0:T(8,128)(2,1)S(1)}, bf16[64,1536]{1,0:T(8,128)(2,1)S(1)}, u32[]{:S(2)}, u32[]{:S(2)}) collective-permute-start(bf16[64,1536]{1,0:T(8,128)(2,1)S(1)} %get-tuple-element.131.refs_4_), channel_id=1, source_target_pairs={{0,4},{1,5},{2,6},{3,7},{4,0},{5,1},{6,2},{7,3},{8,12},{9,13},{10,... | collective-permute-start | bytes 589832 | tf_op jit(solution)/shard_map/ppermute | solution.py:43
  70.3 9.0 %collective-permute-start.23 = (bf16[64,1536]{1,0:T(8,128)(2,1)S(1)}, bf16[64,1536]{1,0:T(8,128)(2,1)S(1)}, u32[]{:S(2)}, u32[]{:S(2)}) collective-permute-start(bf16[64,1536]{1,0:T(8,128)(2,1)S(1)} %get-tuple-element.132.refs_9_), channel_id=1, source_target_pairs={{0,4},{1,5},{2,6},{3,7},{4,0},{5,1},{6,2},{7,3},{8,12},{9,13},{10,... | collective-permute-start | bytes 589832 | tf_op jit(solution)/shard_map/ppermute | solution.py:43
  72.9 6.4 %collective-permute-start.24 = (bf16[64,1536]{1,0:T(8,128)(2,1)S(1)}, bf16[64,1536]{1,0:T(8,128)(2,1)S(1)}, u32[]{:S(2)}, u32[]{:S(2)}) collective-permute-start(bf16[64,1536]{1,0:T(8,128)(2,1)S(1)} %get-tuple-element.133), channel_id=1, source_target_pairs={{0,1},{1,0},{2,3},{3,2},{4,8},{5,9},{6,10},{7,11},{8,4},{9,5},{10,... | collective-permute-start | bytes 589832 | tf_op jit(solution)/shard_map/ppermute | solution.py:43
  77.7 8.7 %collective-permute-start.29 = (bf16[64,1536]{1,0:T(8,128)(2,1)S(1)}, bf16[64,1536]{1,0:T(8,128)(2,1)S(1)}, u32[]{:S(2)}, u32[]{:S(2)}) collective-permute-start(bf16[64,1536]{1,0:T(8,128)(2,1)S(1)} %get-tuple-element.137.refs_4_), channel_id=1, source_target_pairs={{0,4},{1,5},{2,6},{3,7},{4,0},{5,1},{6,2},{7,3},{8,12},{9,13},{10,... | collective-permute-start | bytes 589832 | tf_op jit(solution)/shard_map/ppermute | solution.py:43
  79.3 7.1 %collective-permute-start.30 = (bf16[64,1536]{1,0:T(8,128)(2,1)S(1)}, bf16[64,1536]{1,0:T(8,128)(2,1)S(1)}, u32[]{:S(2)}, u32[]{:S(2)}) collective-permute-start(bf16[64,1536]{1,0:T(8,128)(2,1)S(1)} %get-tuple-element.140), channel_id=1, source_target_pairs={{0,1},{1,0},{2,3},{3,2},{4,8},{5,9},{6,10},{7,11},{8,4},{9,5},{10,... | collective-permute-start | bytes 589832 | tf_op jit(solution)/shard_map/ppermute | solution.py:43
  79.7 9.7 %collective-permute-start.27 = (bf16[64,1536]{1,0:T(8,128)(2,1)S(1)}, bf16[64,1536]{1,0:T(8,128)(2,1)S(1)}, u32[]{:S(2)}, u32[]{:S(2)}) collective-permute-start(bf16[64,1536]{1,0:T(8,128)(2,1)S(1)} %get-tuple-element.138.refs_0_), channel_id=1, source_target_pairs={{0,4},{1,5},{2,6},{3,7},{4,0},{5,1},{6,2},{7,3},{8,12},{9,13},{10,... | collective-permute-start | bytes 589832 | tf_op jit(solution)/shard_map/ppermute | solution.py:43
  81.7 7.7 %collective-permute-start.28 = (bf16[64,1536]{1,0:T(8,128)(2,1)S(1)}, bf16[64,1536]{1,0:T(8,128)(2,1)S(1)}, u32[]{:S(2)}, u32[]{:S(2)}) collective-permute-start(bf16[64,1536]{1,0:T(8,128)(2,1)S(1)} %get-tuple-element.138.refs_0_), channel_id=1, source_target_pairs={{0,1},{1,0},{2,3},{3,2},{4,8},{5,9},{6,10},{7,11},{8,4},{9,5},{10,... | collective-permute-start | bytes 589832 | tf_op jit(solution)/shard_map/ppermute | solution.py:43
  86.8 11.2 %collective-permute-start.33 = (bf16[64,1536]{1,0:T(8,128)(2,1)S(1)}, bf16[64,1536]{1,0:T(8,128)(2,1)S(1)}, u32[]{:S(2)}, u32[]{:S(2)}) collective-permute-start(bf16[64,1536]{1,0:T(8,128)(2,1)S(1)} %get-tuple-element.147.refs_0_.refs_6_), channel_id=1, source_target_pairs={{0,1},{1,0},{2,3},{3,2},{4,8},{5,9},{6,10},{7,11},{8,4},{9,5},{10,... | collective-permute-start | bytes 589832 | tf_op jit(solution)/shard_map/ppermute | solution.py:43
  87.4 10.6 %collective-permute-start.34 = (bf16[64,1536]{1,0:T(8,128)(2,1)S(1)}, bf16[64,1536]{1,0:T(8,128)(2,1)S(1)}, u32[]{:S(2)}, u32[]{:S(2)}) collective-permute-start(bf16[64,1536]{1,0:T(8,128)(2,1)S(1)} %get-tuple-element.147.refs_0_.refs_6_), channel_id=1, source_target_pairs={{0,4},{1,5},{2,6},{3,7},{4,0},{5,1},{6,2},{7,3},{8,12},{9,13},{10,... | collective-permute-start | bytes 589832 | tf_op jit(solution)/shard_map/ppermute | solution.py:43
  89.5 9.2 %collective-permute-start.32 = (bf16[64,1536]{1,0:T(8,128)(2,1)S(1)}, bf16[64,1536]{1,0:T(8,128)(2,1)S(1)}, u32[]{:S(2)}, u32[]{:S(2)}) collective-permute-start(bf16[64,1536]{1,0:T(8,128)(2,1)S(1)} %get-tuple-element.146), channel_id=1, source_target_pairs={{0,1},{1,0},{2,3},{3,2},{4,8},{5,9},{6,10},{7,11},{8,4},{9,5},{10,... | collective-permute-start | bytes 589832 | tf_op jit(solution)/shard_map/ppermute | solution.py:43
  89.6 19.7 %collective-permute-start.31 = (bf16[64,1536]{1,0:T(8,128)(2,1)S(1)}, bf16[64,1536]{1,0:T(8,128)(2,1)S(1)}, u32[]{:S(2)}, u32[]{:S(2)}) collective-permute-start(bf16[64,1536]{1,0:T(8,128)(2,1)S(1)} %get-tuple-element.145.refs_12_), channel_id=1, source_target_pairs={{0,4},{1,5},{2,6},{3,7},{4,0},{5,1},{6,2},{7,3},{8,12},{9,13},{10,... | collective-permute-start | bytes 589832 | tf_op jit(solution)/shard_map/ppermute | solution.py:43
  98.1 6.9 %collective-permute-start.37 = (bf16[64,1536]{1,0:T(8,128)(2,1)S(1)}, bf16[64,1536]{1,0:T(8,128)(2,1)S(1)}, u32[]{:S(2)}, u32[]{:S(2)}) collective-permute-start(bf16[64,1536]{1,0:T(8,128)(2,1)S(1)} %get-tuple-element.153), channel_id=1, source_target_pairs={{0,1},{1,0},{2,3},{3,2},{4,8},{5,9},{6,10},{7,11},{8,4},{9,5},{10,... | collective-permute-start | bytes 589832 | tf_op jit(solution)/shard_map/ppermute | solution.py:43
  98.2 16.6 %collective-permute-start.36 = (bf16[64,1536]{1,0:T(8,128)(2,1)S(1)}, bf16[64,1536]{1,0:T(8,128)(2,1)S(1)}, u32[]{:S(2)}, u32[]{:S(2)}) collective-permute-start(bf16[64,1536]{1,0:T(8,128)(2,1)S(1)} %get-tuple-element.152.refs_1_), channel_id=1, source_target_pairs={{0,4},{1,5},{2,6},{3,7},{4,0},{5,1},{6,2},{7,3},{8,12},{9,13},{10,... | collective-permute-start | bytes 589832 | tf_op jit(solution)/shard_map/ppermute | solution.py:43
  98.8 10.9 %collective-permute-start.35 = (bf16[64,1536]{1,0:T(8,128)(2,1)S(1)}, bf16[64,1536]{1,0:T(8,128)(2,1)S(1)}, u32[]{:S(2)}, u32[]{:S(2)}) collective-permute-start(bf16[64,1536]{1,0:T(8,128)(2,1)S(1)} %relay_far.2.refs_10_), channel_id=1, source_target_pairs={{0,4},{1,5},{2,6},{3,7},{4,0},{5,1},{6,2},{7,3},{8,12},{9,13},{10,... | collective-permute-start | bytes 589832 | tf_op jit(solution)/shard_map/ppermute | solution.py:43
  108.7 6.8 %collective-permute-start.38 = (bf16[64,1536]{1,0:T(8,128)(2,1)S(1)}, bf16[64,1536]{1,0:T(8,128)(2,1)S(1)}, u32[]{:S(2)}, u32[]{:S(2)}) collective-permute-start(bf16[64,1536]{1,0:T(8,128)(2,1)S(1)} %relay_far.3.refs_1_), channel_id=1, source_target_pairs={{0,4},{1,5},{2,6},{3,7},{4,0},{5,1},{6,2},{7,3},{8,12},{9,13},{10,... | collective-permute-start | bytes 589832 | tf_op jit(solution)/shard_map/ppermute | solution.py:43
  117.4 2.6 %collective-permute-start.40 = (bf16[64,1536]{1,0:T(8,128)(2,1)S(1)}, bf16[64,1536]{1,0:T(8,128)(2,1)S(1)}, u32[]{:S(2)}, u32[]{:S(2)}) collective-permute-start(bf16[64,1536]{1,0:T(8,128)(2,1)S(1)} %get-tuple-element.169), channel_id=1, source_target_pairs={{0,1},{1,0},{2,3},{3,2},{4,5},{5,4},{6,7},{7,6},{8,9},{9,8},{10,11... | collective-permute-start | bytes 589832 | tf_op jit(solution)/shard_map/ppermute | solution.py:43
  119.4 2.1 %collective-permute-start.39 = (bf16[64,1536]{1,0:T(8,128)(2,1)S(1)}, bf16[64,1536]{1,0:T(8,128)(2,1)S(1)}, u32[]{:S(2)}, u32[]{:S(2)}) collective-permute-start(bf16[64,1536]{1,0:T(8,128)(2,1)S(1)} %get-tuple-element.166), channel_id=1, source_target_pairs={{0,1},{1,0},{2,3},{3,2},{4,5},{5,4},{6,7},{7,6},{8,9},{9,8},{10,11... | collective-permute-start | bytes 589832 | tf_op jit(solution)/shard_map/ppermute | solution.py:43
  120.0 11.2 %collective-permute-start.41 = (bf16[64,1536]{1,0:T(8,128)(2,1)S(1)}, bf16[64,1536]{1,0:T(8,128)(2,1)S(1)}, u32[]{:S(2)}, u32[]{:S(2)}) collective-permute-start(bf16[64,1536]{1,0:T(8,128)(2,1)S(1)} %get-tuple-element.172.refs_3_), channel_id=1, source_target_pairs={{0,2},{2,0},{1,3},{3,1},{4,6},{6,4},{5,7},{7,5},{8,10},{10,8},{9,1... | collective-permute-start | bytes 589832 | tf_op jit(solution)/shard_map/ppermute | solution.py:43
  121.6 9.6 %collective-permute-start.43 = (bf16[64,1536]{1,0:T(8,128)(2,1)S(1)}, bf16[64,1536]{1,0:T(8,128)(2,1)S(1)}, u32[]{:S(2)}, u32[]{:S(2)}) collective-permute-start(bf16[64,1536]{1,0:T(8,128)(2,1)S(1)} %get-tuple-element.173.refs_17_), channel_id=1, source_target_pairs={{0,2},{2,0},{1,3},{3,1},{4,6},{6,4},{5,7},{7,5},{8,10},{10,8},{9,1... | collective-permute-start | bytes 589832 | tf_op jit(solution)/shard_map/ppermute | solution.py:43
  122.7 8.5 %collective-permute-start.44 = (bf16[64,1536]{1,0:T(8,128)(2,1)S(1)}, bf16[64,1536]{1,0:T(8,128)(2,1)S(1)}, u32[]{:S(2)}, u32[]{:S(2)}) collective-permute-start(bf16[64,1536]{1,0:T(8,128)(2,1)S(1)} %get-tuple-element.178), channel_id=1, source_target_pairs={{0,1},{1,0},{2,3},{3,2},{4,5},{5,4},{6,7},{7,6},{8,9},{9,8},{10,11... | collective-permute-start | bytes 589832 | tf_op jit(solution)/shard_map/ppermute | solution.py:43
  122.7 8.5 %collective-permute-start.42 = (bf16[64,1536]{1,0:T(8,128)(2,1)S(1)}, bf16[64,1536]{1,0:T(8,128)(2,1)S(1)}, u32[]{:S(2)}, u32[]{:S(2)}) collective-permute-start(bf16[64,1536]{1,0:T(8,128)(2,1)S(1)} %get-tuple-element.176), channel_id=1, source_target_pairs={{0,1},{1,0},{2,3},{3,2},{4,5},{5,4},{6,7},{7,6},{8,9},{9,8},{10,11... | collective-permute-start | bytes 589832 | tf_op jit(solution)/shard_map/ppermute | solution.py:43

commit v4 on v3

--- a/solution.py
+++ b/solution.py
@@ -1,4 +1,5 @@
 import functools
+import math
 
 import jax
 import jax.numpy as jnp
@@ -72,6 +73,7 @@
 
 
 TILE = 512
+EXTRA = 4
 UNROLL = True
 TOKEN = jax.ShapeDtypeStruct((8, 128), f32)
 
@@ -120,7 +122,14 @@
     )
 
 
-def forward_kernel(start, tile, parts, first, loaded, w_ref, *refs):
+def forward_kernel(start, tile, parts, first, loaded, following, w_ref, *refs):
+    ahead = None
+    if following is not None:
+        source, *refs, made, sem = refs
+        ahead = pltpu.make_async_copy(
+            source.at[:, pl.ds(following, made.shape[1])], made, sem.at[0]
+        )
+        ahead.start()
     if loaded:
         buffer = w_ref
     else:
@@ -150,28 +159,38 @@
             out[:, columns] = sums[k * rows : (k + 1) * rows]
 
     each(size // tile, body)
-
-
-def forward(x, weight, start, size, tokens, parts, dep=None, loaded=None):
+    if ahead is not None:
+        ahead.wait()
+
+
+def forward(x, weight, start, size, tokens, parts, dep=None, loaded=None, following=None):
     depth = weight.shape[0]
     tile = tile_of(size, TILE)
     rows = tokens // parts
     first = isinstance(x, tuple)
     here = loaded is not None
     operands = [loaded if here else weight, *(x if first else (x,))]
+    specs = [resident() if here else pl.BlockSpec(memory_space=pl.ANY)] + [resident()] * (len(operands) - 1)
+    if following is not None:
+        operands.insert(1, weight)
+        specs.insert(1, pl.BlockSpec(memory_space=pl.ANY))
     out_shape = [jax.ShapeDtypeStruct((rows, size), bf16)] * parts + [TOKEN]
     if first:
         out_shape.append(jax.ShapeDtypeStruct((tokens, depth), bf16))
-    scratch = [pltpu.VMEM((depth, size), bf16), pltpu.SemaphoreType.DMA((size // tile,))]
+    scratch = [] if here else [pltpu.VMEM((depth, size), bf16), pltpu.SemaphoreType.DMA((size // tile,))]
+    if following is not None:
+        assert here and not first
+        out_shape.append(jax.ShapeDtypeStruct((depth, size), bf16))
+        scratch.append(pltpu.SemaphoreType.DMA((1,)))
     return call(
-        functools.partial(forward_kernel, start, tile, parts, first, here),
+        functools.partial(forward_kernel, start, tile, parts, first, here, following),
         operands,
-        [resident() if here else pl.BlockSpec(memory_space=pl.ANY)] + [resident()] * (len(operands) - 1),
+        specs,
         dep,
         out_specs=[resident()] * len(out_shape),
         out_shape=out_shape,
-        scratch_shapes=[] if here else scratch,
-        compiler_params=params(16 if here else 36),
+        scratch_shapes=scratch,
+        compiler_params=params(12 if here else 36),
         cost_estimate=cost(2 * tokens * depth * size, 2 * depth * size),
         name="forward_sums",
     )
@@ -332,6 +351,8 @@
         scratch.append(("hidden_sems", pltpu.SemaphoreType.DMA((len(hidden),))))
     make("token", TOKEN)
     names = [name for name, *_ in operands + outs + scratch]
+    held = [shape for _, shape in scratch if not shape.dtype == sems.dtype]
+    room = EXTRA + sum(math.prod(shape.shape) * 2 for shape in held) // MIB
     work = (weight is not None or loaded is not None) + (x is not None)
     return call(
         functools.partial(grads_kernel, names, start, cuts, tile),
@@ -342,7 +363,7 @@
         out_shape=[shape for _, shape, _ in outs],
         scratch_shapes=[shape for _, shape in scratch],
         input_output_aliases=aliases,
-        compiler_params=params(36),
+        compiler_params=params(room),
         cost_estimate=cost(2 * work * tokens * features * size, 2 * work * features * size),
         name="grads",
     )
@@ -522,21 +543,27 @@
 
     def forward_of(k):
         def run(dep):
-            *sums[k], token = forward(x, weight, k * size, size, tokens, 4, dep, loaded.get(k))
+            following = (k + 1) * size if EARLY <= k + 1 < chunks else None
+            made = forward(x, weight, k * size, size, tokens, 4, dep, loaded.get(k), following)
+            if following is not None:
+                *made, loaded[k + 1] = made
+            *sums[k], token = made
             return token
 
         return run
 
     def grads_of(k, *which, both=True):
         def run(dep):
-            more = {}
+            more = {"weight": weight}
+            if k in loaded:
+                more = {"loaded": loaded[k]}
             if both:
-                more = {"x": x, "into": state["weight"]}
+                more |= {"x": x, "into": state["weight"]}
                 if which[0] == 0:
                     more |= {"hidden": [hidden[k]], "all_hidden": state["hidden"]}
             before = [total[p] for p in which] if total[which[0]] is not None else None
             made = list(
-                grads(k * size, [bounds[p] for p in which], blocks[k], dep, weight=weight, before=before, **more)
+                grads(k * size, [bounds[p] for p in which], blocks[k], dep, before=before, **more)
             )
             for p in which:
                 total[p] = made.pop(0)
@@ -545,13 +572,6 @@
                 if which[0] == 0:
                     state["hidden"] = made.pop(0)
             return made.pop(0)
-
-        return run
-
-    def preload_of(k):
-        def run(dep):
-            (loaded[k],) = preload(weight, [k * size], size, dep)
-            return loaded[k]
 
         return run
 
@@ -612,7 +632,7 @@
     )
     loaded = dict(zip(early, made))
     *sums[0], order.token, x = forward(pieces, weight, 0, size, tokens, 4, None, loaded.get(0))
-    plan.update(planned(forward_of, grads_of, preload_of))
+    plan.update(planned(forward_of, grads_of))
     chains = [chain(list(range(s, chunks, STREAMS))) for s in range(STREAMS)]
     live = list(chains)
     while live:
@@ -662,7 +682,7 @@
     return (all_hidden, grad_inputs, grad_weight)
 
 
-def planned(forward_of, grads_of, preload_of):
+def planned(forward_of, grads_of):
     return {
         0: [forward_of(1)],
         2: [forward_of(2)],
@@ -671,7 +691,6 @@
         14: [grads_of(0, 1)],
         16: [grads_of(1, 0)],
         18: [grads_of(1, 1)],
-        19: [preload_of(3)],
     }
 
 

time: 132 us -> 128 us (0.970)
  waiting for transfers between devices: 9.54 us -> 26.1 us
  Pallas kernels: 64.8 us -> 53 us
  starting transfers between devices: 55.5 us -> 45.9 us
    ppermute x45, waiting for transfers between devices: 9.54 us -> 26.1 us  [send(): return lax.ppermute(value, axis, pairs)]
    pallas_call x35 -> x34, Pallas kernels: 61.8 us -> 49.9 us  [call(): return pl.pallas_call(ordered, in_specs=in_specs, **options)(*operands, dep)]
    ppermute x45, starting transfers between devices: 55.5 us -> 45.9 us  [send(): return lax.ppermute(value, axis, pairs)]
  transfers between devices with their start and end apart: 45 -> 45, of which waited for: 10 -> 15; matrix products, arithmetic and copies ran while one was open for 0% -> 0% of each run, Pallas kernels for 45% -> 37%
where the time goes in v4:
time: 128 us; the launch traced here: 127 us
  Pallas kernels  53 us (41%)
  starting transfers between devices  45.9 us (36%)
  waiting for transfers between devices  26.1 us (20%)
    pallas_call x34, Pallas kernels, call(): return pl.pallas_call(ordered, in_specs=in_specs, **options)(*operands, dep)  49.9 us
    ppermute x45, starting transfers between devices, send(): return lax.ppermute(value, axis, pairs)  45.9 us
    ppermute x45, waiting for transfers between devices, send(): return lax.ppermute(value, axis, pairs)  26.1 us
    pallas_call x2, Pallas kernels, call(): return pl.pallas_call(kernel, in_specs=in_specs, **options)(*operands)  3.17 us
  transfers between devices with their start and end apart: 45, of which 15 were waited for; matrix products, arithmetic and copies ran while one was open for 0% of the time, Pallas kernels for 37%

profile of v4, /device:TPU:0, one launch (start us, length us, event | category | flops | bytes accessed | tf_op | source)
XLA Modules:
  0.0 127.3 jit_solution(4496929355055066256)
XLA Ops:
  0.6 3.0 %collective-permute-start.1 = (bf16[64,3072]{1,0:T(8,128)(2,1)}, bf16[64,3072]{1,0:T(8,128)(2,1)S(1)}, u32[]{:S(2)}, u32[]{:S(2)}) collective-permute-start(bf16[64,3072]{1,0:T(8,128)(2,1)} %a.1), channel_id=1, source_target_pairs={{0,2},{2,0},{1,3},{3,1},{4,6},{6,4},{5,7},{7,5},{8,10},{10,8},{9,1... | collective-permute-start | bytes 1179656 | tf_op jit(solution)/shard_map/ppermute | solution.py:44
  3.6 1.0 copy-done.1
  4.8 6.4 %preload.1 = (bf16[3072,1536]{1,0:T(8,128)(2,1)S(1)}, bf16[3072,1536]{1,0:T(8,128)(2,1)S(1)}) custom-call(bf16[3072,6144]{1,0:T(8,128)(2,1)} %refs_1_.3, bf16[64,3072]{1,0:T(8,128)(2,1)S(1)} %local.1.refs_1_.refs_0_), custom_call_target="tpu_custom_call" | custom-call | bytes 18874368 | tf_op jit(solution)/shard_map/preload/pallas_call | solution.py:381
  11.2 1.8 %collective-permute-done.1.refs_0_ = bf16[64,3072]{1,0:T(8,128)(2,1)S(1)} collective-permute-done((bf16[64,3072]{1,0:T(8,128)(2,1)}, bf16[64,3072]{1,0:T(8,128)(2,1)S(1)}, u32[]{:S(2)}, u32[]{:S(2)}) %collective-permute-start.1) | collective-permute-done | bytes 393248 | tf_op jit(solution)/shard_map/ppermute | solution.py:44
  13.1 1.7 %collective-permute-done.2.refs_3_ = bf16[64,3072]{1,0:T(8,128)(2,1)S(1)} collective-permute-done((bf16[64,3072]{1,0:T(8,128)(2,1)S(1)}, bf16[64,3072]{1,0:T(8,128)(2,1)S(1)}, u32[]{:S(2)}, u32[]{:S(2)}) %collective-permute-start.2) | collective-permute-done | bytes 393248 | tf_op jit(solution)/shard_map/ppermute | solution.py:44
  14.8 3.1 %forward_sums.4 = (bf16[64,1536]{1,0:T(8,128)(2,1)S(1)}, bf16[64,1536]{1,0:T(8,128)(2,1)S(1)}, bf16[64,1536]{1,0:T(8,128)(2,1)S(1)}, bf16[64,1536]{1,0:T(8,128)(...) custom-call(bf16[3072,1536]{1,0:T(8,128)(2,1)S(1)} %get-tuple-element.95.refs_1_.w_ref.refs_6_, ...), custom_call_target="tpu_custom_call" | custom-call | flops 2415919104 | bytes 9437184 | tf_op jit(solution)/shard_map/forward_sums/pallas_call | solution.py:379
  17.9 1.9 %collective-permute-start.3 = (bf16[64,1536]{1,0:T(8,128)(2,1)S(1)}, bf16[64,1536]{1,0:T(8,128)(2,1)S(1)}, u32[]{:S(2)}, u32[]{:S(2)}) collective-permute-start(bf16[64,1536]{1,0:T(8,128)(2,1)S(1)} %get-tuple-element.100.refs_1_), channel_id=1, source_target_pairs={{0,4},{1,5},{2,6},{3,7},{4,0},{5,1},{6,2},{7,3},{8,12},{9,13},{10,... | collective-permute-start | bytes 589832 | tf_op jit(solution)/shard_map/ppermute | solution.py:44
  19.8 3.7 %forward_sums.5 = (bf16[64,1536]{1,0:T(8,128)(2,1)S(1)}, bf16[64,1536]{1,0:T(8,128)(2,1)S(1)}, bf16[64,1536]{1,0:T(8,128)(2,1)S(1)}, bf16[64,1536]{1,0:T(8,128)(...) custom-call(bf16[3072,1536]{1,0:T(8,128)(2,1)S(1)} %get-tuple-element.94.refs_0_.refs_6_, ...), custom_call_target="tpu_custom_call" | custom-call | flops 2415919104 | bytes 9437184 | tf_op jit(solution)/shard_map/forward_sums/pallas_call | solution.py:381
  23.5 0.3 collective-permute-start.6
  23.8 1.2 collective-permute-done.3.refs_2_
  25.1 0.1 collective-permute-start.4
  25.1 3.3 %collective-permute-start.5 = (bf16[64,1536]{1,0:T(8,128)(2,1)S(1)}, bf16[64,1536]{1,0:T(8,128)(2,1)S(1)}, u32[]{:S(2)}, u32[]{:S(2)}) collective-permute-start(bf16[64,1536]{1,0:T(8,128)(2,1)S(1)} %get-tuple-element.102.refs_3_), channel_id=1, source_target_pairs={{0,4},{1,5},{2,6},{3,7},{4,0},{5,1},{6,2},{7,3},{8,12},{9,13},{10,... | collective-permute-start | bytes 589832 | tf_op jit(solution)/shard_map/ppermute | solution.py:44
  28.4 3.7 %forward_sums.6 = (bf16[64,1536]{1,0:T(8,128)(2,1)S(1)}, bf16[64,1536]{1,0:T(8,128)(2,1)S(1)}, bf16[64,1536]{1,0:T(8,128)(2,1)S(1)}, bf16[64,1536]{1,0:T(8,128)(...) custom-call(bf16[3072,1536]{1,0:T(8,128)(2,1)S(1)} %get-tuple-element.98.refs_0_.refs_6_, ...), custom_call_target="tpu_custom_call" | custom-call | flops 2415919104 | bytes 9437184 | tf_op jit(solution)/shard_map/forward_sums/pallas_call | solution.py:381
  32.2 0.1 collective-permute-start.9
  32.3 2.4 %collective-permute-start.10 = (bf16[64,1536]{1,0:T(8,128)(2,1)S(1)}, bf16[64,1536]{1,0:T(8,128)(2,1)S(1)}, u32[]{:S(2)}, u32[]{:S(2)}) collective-permute-start(bf16[64,1536]{1,0:T(8,128)(2,1)S(1)} %get-tuple-element.113.refs_4_), channel_id=1, source_target_pairs={{0,4},{1,5},{2,6},{3,7},{4,0},{5,1},{6,2},{7,3},{8,12},{9,13},{10,... | collective-permute-start | bytes 589832 | tf_op jit(solution)/shard_map/ppermute | solution.py:44
  34.7 0.1 collective-permute-start.8
  34.8 3.6 %collective-permute-start.7 = (bf16[64,1536]{1,0:T(8,128)(2,1)S(1)}, bf16[64,1536]{1,0:T(8,128)(2,1)S(1)}, u32[]{:S(2)}, u32[]{:S(2)}) collective-permute-start(bf16[64,1536]{1,0:T(8,128)(2,1)S(1)} %get-tuple-element.114.refs_2_), channel_id=1, source_target_pairs={{0,4},{1,5},{2,6},{3,7},{4,0},{5,1},{6,2},{7,3},{8,12},{9,13},{10,... | collective-permute-start | bytes 589832 | tf_op jit(solution)/shard_map/ppermute | solution.py:44
  38.4 3.0 %forward_sums.7 = (bf16[64,1536]{1,0:T(8,128)(2,1)S(1)}, bf16[64,1536]{1,0:T(8,128)(2,1)S(1)}, bf16[64,1536]{1,0:T(8,128)(2,1)S(1)}, bf16[64,1536]{1,0:T(8,128)(2,1)S(1)}, f32[8,128]{1,0:T(8,128)S(1)}) custom-call(bf16[3072,1536]{1,0:T(8,128)(2,1)S(1)} %get-tuple-element.118.refs_0_.refs_6_, ...), custom_call_target="tpu_custom_call" | custom-call | flops 2415919104 | bytes 9437184 | tf_op jit(solution)/shard_map/forward_sums/pallas_call | solution.py:381
  41.5 0.1 collective-permute-start.14
  41.5 1.2 collective-permute-start.13
  42.8 1.1 collective-permute-done.7.refs_1_
  43.8 0.4 gelu.4
  44.2 1.3 %collective-permute-start.12 = (bf16[64,1536]{1,0:T(8,128)(2,1)S(1)}, bf16[64,1536]{1,0:T(8,128)(2,1)S(1)}, u32[]{:S(2)}, u32[]{:S(2)}) collective-permute-start(bf16[64,1536]{1,0:T(8,128)(2,1)S(1)} %get-tuple-element.121.refs_0_), channel_id=1, source_target_pairs={{0,4},{1,5},{2,6},{3,7},{4,0},{5,1},{6,2},{7,3},{8,12},{9,13},{10,... | collective-permute-start | bytes 589832 | tf_op jit(solution)/shard_map/ppermute | solution.py:44
  45.6 3.7 %collective-permute-done.13.refs_1_ = bf16[64,1536]{1,0:T(8,128)(2,1)S(1)} collective-permute-done((bf16[64,1536]{1,0:T(8,128)(2,1)S(1)}, bf16[64,1536]{1,0:T(8,128)(2,1)S(1)}, u32[]{:S(2)}, u32[]{:S(2)}) %collective-permute-start.13) | collective-permute-done | bytes 196640 | tf_op jit(solution)/shard_map/ppermute | solution.py:44
  49.3 0.4 gelu.5
  49.7 1.3 %collective-permute-start.18 = (bf16[64,1536]{1,0:T(8,128)(2,1)S(1)}, bf16[64,1536]{1,0:T(8,128)(2,1)S(1)}, u32[]{:S(2)}, u32[]{:S(2)}) collective-permute-start(bf16[64,1536]{1,0:T(8,128)(2,1)S(1)} %get-tuple-element.129.refs_0_), channel_id=1, source_target_pairs={{0,4},{1,5},{2,6},{3,7},{4,0},{5,1},{6,2},{7,3},{8,12},{9,13},{10,... | collective-permute-start | bytes 589832 | tf_op jit(solution)/shard_map/ppermute | solution.py:44
  51.0 2.5 %collective-permute-done.12.refs_2_.refs_1_ = bf16[64,1536]{1,0:T(8,128)(2,1)S(1)} collective-permute-done((bf16[64,1536]{1,0:T(8,128)(2,1)S(1)}, bf16[64,1536]{1,0:T(8,128)(2,1)S(1)}, u32[]{:S(2)}, u32[]{:S(2)}) %collective-permute-start.12) | collective-permute-done | bytes 196640 | tf_op jit(solution)/shard_map/ppermute | solution.py:44
  53.5 0.1 collective-permute-start.15
  53.6 2.8 %collective-permute-start.16 = (bf16[64,1536]{1,0:T(8,128)(2,1)S(1)}, bf16[64,1536]{1,0:T(8,128)(2,1)S(1)}, u32[]{:S(2)}, u32[]{:S(2)}) collective-permute-start(bf16[64,1536]{1,0:T(8,128)(2,1)S(1)} %get-tuple-element.127.refs_3_), channel_id=1, source_target_pairs={{0,4},{1,5},{2,6},{3,7},{4,0},{5,1},{6,2},{7,3},{8,12},{9,13},{10,... | collective-permute-start | bytes 589832 | tf_op jit(solution)/shard_map/ppermute | solution.py:44
  56.4 1.3 %collective-permute-done.18.refs_2_.refs_1_ = bf16[64,1536]{1,0:T(8,128)(2,1)S(1)} collective-permute-done((bf16[64,1536]{1,0:T(8,128)(2,1)S(1)}, bf16[64,1536]{1,0:T(8,128)(2,1)S(1)}, u32[]{:S(2)}, u32[]{:S(2)}) %collective-permute-start.18) | collective-permute-done | bytes 196640 | tf_op jit(solution)/shard_map/ppermute | solution.py:44
  57.8 0.1 collective-permute-start.21
  57.8 2.5 %collective-permute-start.22 = (bf16[64,1536]{1,0:T(8,128)(2,1)S(1)}, bf16[64,1536]{1,0:T(8,128)(2,1)S(1)}, u32[]{:S(2)}, u32[]{:S(2)}) collective-permute-start(bf16[64,1536]{1,0:T(8,128)(2,1)S(1)} %get-tuple-element.130.refs_4_), channel_id=1, source_target_pairs={{0,4},{1,5},{2,6},{3,7},{4,0},{5,1},{6,2},{7,3},{8,12},{9,13},{10,... | collective-permute-start | bytes 589832 | tf_op jit(solution)/shard_map/ppermute | solution.py:44
  60.4 1.6 %collective-permute-done.16.refs_3_ = bf16[64,1536]{1,0:T(8,128)(2,1)S(1)} collective-permute-done((bf16[64,1536]{1,0:T(8,128)(2,1)S(1)}, bf16[64,1536]{1,0:T(8,128)(2,1)S(1)}, u32[]{:S(2)}, u32[]{:S(2)}) %collective-permute-start.16) | collective-permute-done | bytes 196640 | tf_op jit(solution)/shard_map/ppermute | solution.py:44
  62.1 2.7 %collective-permute-start.20 = (bf16[64,1536]{1,0:T(8,128)(2,1)S(1)}, bf16[64,1536]{1,0:T(8,128)(2,1)S(1)}, u32[]{:S(2)}, u32[]{:S(2)}) collective-permute-start(bf16[64,1536]{1,0:T(8,128)(2,1)S(1)} %get-tuple-element.132.refs_4_), channel_id=1, source_target_pairs={{0,4},{1,5},{2,6},{3,7},{4,0},{5,1},{6,2},{7,3},{8,12},{9,13},{10,... | collective-permute-start | bytes 589832 | tf_op jit(solution)/shard_map/ppermute | solution.py:44
  64.8 1.4 %collective-permute-done.22.refs_3_ = bf16[64,1536]{1,0:T(8,128)(2,1)S(1)} collective-permute-done((bf16[64,1536]{1,0:T(8,128)(2,1)S(1)}, bf16[64,1536]{1,0:T(8,128)(2,1)S(1)}, u32[]{:S(2)}, u32[]{:S(2)}) %collective-permute-start.22) | collective-permute-done | bytes 196640 | tf_op jit(solution)/shard_map/ppermute | solution.py:44
  66.3 2.6 %collective-permute-start.26 = (bf16[64,1536]{1,0:T(8,128)(2,1)S(1)}, bf16[64,1536]{1,0:T(8,128)(2,1)S(1)}, u32[]{:S(2)}, u32[]{:S(2)}) collective-permute-start(bf16[64,1536]{1,0:T(8,128)(2,1)S(1)} %get-tuple-element.135.refs_4_), channel_id=1, source_target_pairs={{0,4},{1,5},{2,6},{3,7},{4,0},{5,1},{6,2},{7,3},{8,12},{9,13},{10,... | collective-permute-start | bytes 589832 | tf_op jit(solution)/shard_map/ppermute | solution.py:44
  68.9 1.4 %collective-permute-done.20.refs_3_.refs_5_ = bf16[64,1536]{1,0:T(8,128)(2,1)S(1)} collective-permute-done((bf16[64,1536]{1,0:T(8,128)(2,1)S(1)}, bf16[64,1536]{1,0:T(8,128)(2,1)S(1)}, u32[]{:S(2)}, u32[]{:S(2)}) %collective-permute-start.20) | collective-permute-done | bytes 196640 | tf_op jit(solution)/shard_map/ppermute | solution.py:44
  70.5 3.1 %collective-permute-start.23 = (bf16[64,1536]{1,0:T(8,128)(2,1)S(1)}, bf16[64,1536]{1,0:T(8,128)(2,1)S(1)}, u32[]{:S(2)}, u32[]{:S(2)}) collective-permute-start(bf16[64,1536]{1,0:T(8,128)(2,1)S(1)} %get-tuple-element.136.refs_9_), channel_id=1, source_target_pairs={{0,4},{1,5},{2,6},{3,7},{4,0},{5,1},{6,2},{7,3},{8,12},{9,13},{10,... | collective-permute-start | bytes 589832 | tf_op jit(solution)/shard_map/ppermute | solution.py:44
  73.5 3.7 %grads.8 = (f32[256,1536]{1,0:T(8,128)S(1)}, bf16[3072,6144]{1,0:T(8,128)(2,1)}, bf16[64,6144]{1,0:T(8,128)(2,1)}, f32[8,128]{1,0:T(8,128)S(1)}) custom-call(bf16[64,1536]{1,0:T(8,128)(2,1)S(1)} %get-tuple-element.121.refs_0_, bf16[64,1536]{1,0:T(8,128)(2,1)S(1)} %collective-permute-done.12.refs_2_.refs_1_, ...), custom_call_target="tpu_custom_call" | custom-call | flops 2415919104 | bytes 9437184 | tf_op jit(solution)/shard_map/grads/pallas_call | solution.py:381
  77.4 0.9 collective-permute-start.29
  78.2 0.1 collective-permute-done.23.refs_1_
  78.3 0.4 gelu.6
  78.8 2.0 %collective-permute-start.27 = (bf16[64,1536]{1,0:T(8,128)(2,1)S(1)}, bf16[64,1536]{1,0:T(8,128)(2,1)S(1)}, u32[]{:S(2)}, u32[]{:S(2)}) collective-permute-start(bf16[64,1536]{1,0:T(8,128)(2,1)S(1)} %get-tuple-element.142.refs_0_), channel_id=1, source_target_pairs={{0,4},{1,5},{2,6},{3,7},{4,0},{5,1},{6,2},{7,3},{8,12},{9,13},{10,... | collective-permute-start | bytes 589832 | tf_op jit(solution)/shard_map/ppermute | solution.py:44
  80.8 3.7 %grads.9 = (f32[256,1536]{1,0:T(8,128)S(1)}, bf16[3072,6144]{1,0:T(8,128)(2,1)}, f32[8,128]{1,0:T(8,128)S(1)}) custom-call(bf16[64,1536]{1,0:T(8,128)(2,1)S(1)} %get-tuple-element.121.refs_0_, bf16[64,1536]{1,0:T(8,128)(2,1)S(1)} %collective-permute-done.12.refs_2_.refs_1_, ...), custom_call_target="tpu_custom_call", output_to_operand_aliasing={{1}: (8, {})} | custom-call | flops 2415919104 | bytes 9437184 | tf_op jit(solution)/shard_map/grads/pallas_call | solution.py:381
  84.5 0.6 collective-permute-done.29.refs_1_
  85.1 0.4 gelu.7
  85.5 1.0 collective-permute-start.34
  86.5 2.8 %collective-permute-done.27.refs_1_ = bf16[64,1536]{1,0:T(8,128)(2,1)S(1)} collective-permute-done((bf16[64,1536]{1,0:T(8,128)(2,1)S(1)}, bf16[64,1536]{1,0:T(8,128)(2,1)S(1)}, u32[]{:S(2)}, u32[]{:S(2)}) %collective-permute-start.27) | collective-permute-done | bytes 196640 | tf_op jit(solution)/shard_map/ppermute | solution.py:44
  89.4 1.8 %collective-permute-start.31 = (bf16[64,1536]{1,0:T(8,128)(2,1)S(1)}, bf16[64,1536]{1,0:T(8,128)(2,1)S(1)}, u32[]{:S(2)}, u32[]{:S(2)}) collective-permute-start(bf16[64,1536]{1,0:T(8,128)(2,1)S(1)} %get-tuple-element.149.refs_12_), channel_id=1, source_target_pairs={{0,4},{1,5},{2,6},{3,7},{4,0},{5,1},{6,2},{7,3},{8,12},{9,13},{10,... | collective-permute-start | bytes 589832 | tf_op jit(solution)/shard_map/ppermute | solution.py:44
  91.2 3.7 %grads.10 = (f32[256,1536]{1,0:T(8,128)S(1)}, bf16[3072,6144]{1,0:T(8,128)(2,1)}, bf16[64,6144]{1,0:T(8,128)(2,1)}, f32[8,128]{1,0:T(8,128)S(1)}) custom-call(bf16[64,1536]{1,0:T(8,128)(2,1)S(1)} %get-tuple-element.129.refs_0_, bf16[64,1536]{1,0:T(8,128)(2,1)S(1)} %collective-permute-done.18.refs_2_.refs_1_, ...), custom_call_target="tpu_custom_call", output_to_operand_aliasing={{1}: (9, {}), {2}: (11, {})} | custom-call | flops 2415919104 | bytes 9437184 | tf_op jit(solution)/shard_map/grads/pallas_call | solution.py:381
  95.0 1.4 %collective-permute-start.36 = (bf16[64,1536]{1,0:T(8,128)(2,1)S(1)}, bf16[64,1536]{1,0:T(8,128)(2,1)S(1)}, u32[]{:S(2)}, u32[]{:S(2)}) collective-permute-start(bf16[64,1536]{1,0:T(8,128)(2,1)S(1)} %get-tuple-element.156.refs_1_), channel_id=1, source_target_pairs={{0,4},{1,5},{2,6},{3,7},{4,0},{5,1},{6,2},{7,3},{8,12},{9,13},{10,... | collective-permute-start | bytes 589832 | tf_op jit(solution)/shard_map/ppermute | solution.py:44
  96.5 1.2 collective-permute-start.35
  97.7 3.5 %grads.11 = (f32[256,1536]{1,0:T(8,128)S(1)}, bf16[3072,6144]{1,0:T(8,128)(2,1)}, f32[8,128]{1,0:T(8,128)S(1)}) custom-call(bf16[64,1536]{1,0:T(8,128)(2,1)S(1)} %get-tuple-element.129.refs_0_, bf16[64,1536]{1,0:T(8,128)(2,1)S(1)} %collective-permute-done.18.refs_2_.refs_1_, ...), custom_call_target="tpu_custom_call", output_to_operand_aliasing={{1}: (9, {})} | custom-call | flops 2415919104 | bytes 9437184 | tf_op jit(solution)/shard_map/grads/pallas_call | solution.py:381
  101.2 1.2 collective-permute-start.38
  102.4 4.6 %collective-permute-done.35.refs_5_ = bf16[64,1536]{1,0:T(8,128)(2,1)S(1)} collective-permute-done((bf16[64,1536]{1,0:T(8,128)(2,1)S(1)}, bf16[64,1536]{1,0:T(8,128)(2,1)S(1)}, u32[]{:S(2)}, u32[]{:S(2)}) %collective-permute-start.35) | collective-permute-done | bytes 196640 | tf_op jit(solution)/shard_map/ppermute | solution.py:44
  107.0 3.7 %grads.12 = (f32[256,1536]{1,0:T(8,128)S(1)}, f32[256,1536]{1,0:T(8,128)S(1)}, f32[8,128]{1,0:T(8,128)S(1)}) custom-call(bf16[64,1536]{1,0:T(8,128)(2,1)S(1)} %get-tuple-element.142.refs_0_, bf16[64,1536]{1,0:T(8,128)(2,1)S(1)} %collective-permute-done.27.refs_1_, bf16[64,1536]{1,0:T(8,128)(2,1)S(1)} %collective-permute-done.28.refs_0_.refs_2_, ...), custom_call_target="tpu_custom_call" | custom-call | flops 2415919104 | bytes 9437184 | tf_op jit(solution)/shard_map/grads/pallas_call | solution.py:381
  110.8 1.9 %grads.13 = (bf16[64,1536]{1,0:T(8,128)(2,1)S(1)}, bf16[64,1536]{1,0:T(8,128)(2,1)S(1)}, bf16[64,1536]{1,0:T(8,128)(2,1)S(1)}, bf16[64,1536]{1,0:T(8,128)(2,1)S(1)}, f32[8,128]{1,0:T(8,128)S(1)}) custom-call(bf16[64,1536]{1,0:T(8,128)(2,1)S(1)} %get-tuple-element.151.refs_0_.refs_6_, bf16[64,1536]{1,0:T(8,128)(2,1)S(1)} %collective-permute-done.34.refs_1_.refs_7_, ...), custom_call_target="tpu_custom_call" | custom-call | flops 1207959552 | bytes 4718592 | tf_op jit(solution)/shard_map/grads/pallas_call | solution.py:381
  112.8 1.9 %grads.14 = (bf16[64,1536]{1,0:T(8,128)(2,1)S(1)}, bf16[64,1536]{1,0:T(8,128)(2,1)S(1)}, bf16[64,1536]{1,0:T(8,128)(2,1)S(1)}, bf16[64,1536]{1,0:T(8,128)(2,1)S(1)}, f32[8,128]{1,0:T(8,128)S(1)}) custom-call(bf16[64,1536]{1,0:T(8,128)(2,1)S(1)} %get-tuple-element.151.refs_0_.refs_6_, bf16[64,1536]{1,0:T(8,128)(2,1)S(1)} %collective-permute-done.34.refs_1_.refs_7_, ...), custom_call_target="tpu_custom_call" | custom-call | flops 1207959552 | bytes 4718592 | tf_op jit(solution)/shard_map/grads/pallas_call | solution.py:381
  114.7 0.6 collective-permute-start.39
  115.3 1.5 %collective-permute-start.41 = (bf16[64,1536]{1,0:T(8,128)(2,1)S(1)}, bf16[64,1536]{1,0:T(8,128)(2,1)S(1)}, u32[]{:S(2)}, u32[]{:S(2)}) collective-permute-start(bf16[64,1536]{1,0:T(8,128)(2,1)S(1)} %get-tuple-element.176.refs_3_), channel_id=1, source_target_pairs={{0,2},{2,0},{1,3},{3,1},{4,6},{6,4},{5,7},{7,5},{8,10},{10,8},{9,1... | collective-permute-start | bytes 589832 | tf_op jit(solution)/shard_map/ppermute | solution.py:44
  117.0 1.3 %collective-permute-start.43 = (bf16[64,1536]{1,0:T(8,128)(2,1)S(1)}, bf16[64,1536]{1,0:T(8,128)(2,1)S(1)}, u32[]{:S(2)}, u32[]{:S(2)}) collective-permute-start(bf16[64,1536]{1,0:T(8,128)(2,1)S(1)} %get-tuple-element.177.refs_17_), channel_id=1, source_target_pairs={{0,2},{2,0},{1,3},{3,1},{4,6},{6,4},{5,7},{7,5},{8,10},{10,8},{9,1... | collective-permute-start | bytes 589832 | tf_op jit(solution)/shard_map/ppermute | solution.py:44
  118.3 8.0 %grads.15 = (bf16[3072,6144]{1,0:T(8,128)(2,1)}, bf16[64,6144]{1,0:T(8,128)(2,1)}, f32[8,128]{1,0:T(8,128)S(1)}) custom-call(bf16[64,1536]{1,0:T(8,128)(2,1)S(1)} %get-tuple-element.142.refs_0_, bf16[64,1536]{1,0:T(8,128)(2,1)S(1)} %collective-permute-done.27.refs_1_, ...), custom_call_target="tpu_custom_call", output_to_operand_aliasing={{0}: (13, {}), {1}: (16, {})} | custom-call | flops 4831838208 | bytes 18874368 | tf_op jit(solution)/shard_map/grads/pallas_call | solution.py:381
  126.3 0.1 collective-permute-done.43.refs_4_
  126.4 0.9 finish.1
  (76 shorter events, 1.6 us)
Async XLA Ops:
  0.6 12.3 %collective-permute-start.1 = (bf16[64,3072]{1,0:T(8,128)(2,1)}, bf16[64,3072]{1,0:T(8,128)(2,1)S(1)}, u32[]{:S(2)}, u32[]{:S(2)}) collective-permute-start(bf16[64,3072]{1,0:T(8,128)(2,1)} %a.1), channel_id=1, source_target_pairs={{0,2},{2,0},{1,3},{3,1},{4,6},{6,4},{5,7},{7,5},{8,10},{10,8},{9,1... | collective-permute-start | bytes 1179656 | tf_op jit(solution)/shard_map/ppermute | solution.py:44
  3.6 1.0 copy-start.1
  4.7 8.4 %collective-permute-start = (bf16[64,3072]{1,0:T(8,128)(2,1)S(1)}, bf16[64,3072]{1,0:T(8,128)(2,1)S(1)}, u32[]{:S(2)}, u32[]{:S(2)}) collective-permute-start(bf16[64,3072]{1,0:T(8,128)(2,1)S(1)} %local.1.refs_1_.refs_0_), channel_id=1, source_target_pairs={{0,1},{1,0},{2,3},{3,2},{4,5},{5,4},{6,7},{7,6},{8,9},{9,8},{10,11... | collective-permute-start | bytes 1179656 | tf_op jit(solution)/shard_map/ppermute | solution.py:44
  13.0 1.8 %collective-permute-start.2 = (bf16[64,3072]{1,0:T(8,128)(2,1)S(1)}, bf16[64,3072]{1,0:T(8,128)(2,1)S(1)}, u32[]{:S(2)}, u32[]{:S(2)}) collective-permute-start(bf16[64,3072]{1,0:T(8,128)(2,1)S(1)} %corner.1.refs_2_), channel_id=1, source_target_pairs={{0,1},{1,0},{2,3},{3,2},{4,5},{5,4},{6,7},{7,6},{8,9},{9,8},{10,11... | collective-permute-start | bytes 1179656 | tf_op jit(solution)/shard_map/ppermute | solution.py:44
  17.9 7.1 %collective-permute-start.3 = (bf16[64,1536]{1,0:T(8,128)(2,1)S(1)}, bf16[64,1536]{1,0:T(8,128)(2,1)S(1)}, u32[]{:S(2)}, u32[]{:S(2)}) collective-permute-start(bf16[64,1536]{1,0:T(8,128)(2,1)S(1)} %get-tuple-element.100.refs_1_), channel_id=1, source_target_pairs={{0,4},{1,5},{2,6},{3,7},{4,0},{5,1},{6,2},{7,3},{8,12},{9,13},{10,... | collective-permute-start | bytes 589832 | tf_op jit(solution)/shard_map/ppermute | solution.py:44
  23.5 8.6 %copy-start = (bf16[3072,1536]{1,0:T(8,128)(2,1)}, bf16[3072,1536]{1,0:T(8,128)(2,1)S(1)}, u32[]{:S(2)}) copy-start(bf16[3072,1536]{1,0:T(8,128)(2,1)S(1)} %get-tuple-element.98.refs_0_.refs_6_) | copy-start | bytes 28311556
  23.5 8.6 %collective-permute-start.6 = (bf16[64,1536]{1,0:T(8,128)(2,1)S(1)}, bf16[64,1536]{1,0:T(8,128)(2,1)S(1)}, u32[]{:S(2)}, u32[]{:S(2)}) collective-permute-start(bf16[64,1536]{1,0:T(8,128)(2,1)S(1)} %get-tuple-element.111.refs_1_), channel_id=1, source_target_pairs={{0,4},{1,5},{2,6},{3,7},{4,0},{5,1},{6,2},{7,3},{8,12},{9,13},{10,... | collective-permute-start | bytes 589832 | tf_op jit(solution)/shard_map/ppermute | solution.py:44
  25.1 9.6 %collective-permute-start.4 = (bf16[64,1536]{1,0:T(8,128)(2,1)S(1)}, bf16[64,1536]{1,0:T(8,128)(2,1)S(1)}, u32[]{:S(2)}, u32[]{:S(2)}) collective-permute-start(bf16[64,1536]{1,0:T(8,128)(2,1)S(1)} %get-tuple-element.109), channel_id=1, source_target_pairs={{0,1},{1,0},{2,3},{3,2},{4,8},{5,9},{6,10},{7,11},{8,4},{9,5},{10,... | collective-permute-start | bytes 589832 | tf_op jit(solution)/shard_map/ppermute | solution.py:44
  25.1 9.5 %collective-permute-start.5 = (bf16[64,1536]{1,0:T(8,128)(2,1)S(1)}, bf16[64,1536]{1,0:T(8,128)(2,1)S(1)}, u32[]{:S(2)}, u32[]{:S(2)}) collective-permute-start(bf16[64,1536]{1,0:T(8,128)(2,1)S(1)} %get-tuple-element.102.refs_3_), channel_id=1, source_target_pairs={{0,4},{1,5},{2,6},{3,7},{4,0},{5,1},{6,2},{7,3},{8,12},{9,13},{10,... | collective-permute-start | bytes 589832 | tf_op jit(solution)/shard_map/ppermute | solution.py:44
  32.2 10.5 %copy-start.2 = (bf16[64,6144]{1,0:T(8,128)(2,1)S(1)}, bf16[64,6144]{1,0:T(8,128)(2,1)}, u32[]{:S(2)}) copy-start(bf16[64,6144]{1,0:T(8,128)(2,1)} %param.5) | copy-start | bytes 2359300
  32.2 9.2 %collective-permute-start.9 = (bf16[64,1536]{1,0:T(8,128)(2,1)S(1)}, bf16[64,1536]{1,0:T(8,128)(2,1)S(1)}, u32[]{:S(2)}, u32[]{:S(2)}) collective-permute-start(bf16[64,1536]{1,0:T(8,128)(2,1)S(1)} %get-tuple-element.117), channel_id=1, source_target_pairs={{0,1},{1,0},{2,3},{3,2},{4,8},{5,9},{6,10},{7,11},{8,4},{9,5},{10,... | collective-permute-start | bytes 589832 | tf_op jit(solution)/shard_map/ppermute | solution.py:44
  32.3 9.1 %collective-permute-start.10 = (bf16[64,1536]{1,0:T(8,128)(2,1)S(1)}, bf16[64,1536]{1,0:T(8,128)(2,1)S(1)}, u32[]{:S(2)}, u32[]{:S(2)}) collective-permute-start(bf16[64,1536]{1,0:T(8,128)(2,1)S(1)} %get-tuple-element.113.refs_4_), channel_id=1, source_target_pairs={{0,4},{1,5},{2,6},{3,7},{4,0},{5,1},{6,2},{7,3},{8,12},{9,13},{10,... | collective-permute-start | bytes 589832 | tf_op jit(solution)/shard_map/ppermute | solution.py:44
  34.7 8.0 %collective-permute-start.8 = (bf16[64,1536]{1,0:T(8,128)(2,1)S(1)}, bf16[64,1536]{1,0:T(8,128)(2,1)S(1)}, u32[]{:S(2)}, u32[]{:S(2)}) collective-permute-start(bf16[64,1536]{1,0:T(8,128)(2,1)S(1)} %get-tuple-element.115), channel_id=1, source_target_pairs={{0,1},{1,0},{2,3},{3,2},{4,8},{5,9},{6,10},{7,11},{8,4},{9,5},{10,... | collective-permute-start | bytes 589832 | tf_op jit(solution)/shard_map/ppermute | solution.py:44
  34.8 9.0 %collective-permute-start.7 = (bf16[64,1536]{1,0:T(8,128)(2,1)S(1)}, bf16[64,1536]{1,0:T(8,128)(2,1)S(1)}, u32[]{:S(2)}, u32[]{:S(2)}) collective-permute-start(bf16[64,1536]{1,0:T(8,128)(2,1)S(1)} %get-tuple-element.114.refs_2_), channel_id=1, source_target_pairs={{0,4},{1,5},{2,6},{3,7},{4,0},{5,1},{6,2},{7,3},{8,12},{9,13},{10,... | collective-permute-start | bytes 589832 | tf_op jit(solution)/shard_map/ppermute | solution.py:44
  41.5 4.1 %collective-permute-start.14 = (bf16[64,1536]{1,0:T(8,128)(2,1)S(1)}, bf16[64,1536]{1,0:T(8,128)(2,1)S(1)}, u32[]{:S(2)}, u32[]{:S(2)}) collective-permute-start(bf16[64,1536]{1,0:T(8,128)(2,1)S(1)} %get-tuple-element.123), channel_id=1, source_target_pairs={{0,1},{1,0},{2,3},{3,2},{4,8},{5,9},{6,10},{7,11},{8,4},{9,5},{10,... | collective-permute-start | bytes 589832 | tf_op jit(solution)/shard_map/ppermute | solution.py:44
  41.5 7.8 %collective-permute-start.13 = (bf16[64,1536]{1,0:T(8,128)(2,1)S(1)}, bf16[64,1536]{1,0:T(8,128)(2,1)S(1)}, u32[]{:S(2)}, u32[]{:S(2)}) collective-permute-start(bf16[64,1536]{1,0:T(8,128)(2,1)S(1)} %get-tuple-element.120.refs_4_), channel_id=1, source_target_pairs={{0,4},{1,5},{2,6},{3,7},{4,0},{5,1},{6,2},{7,3},{8,12},{9,13},{10,... | collective-permute-start | bytes 589832 | tf_op jit(solution)/shard_map/ppermute | solution.py:44
  44.2 9.3 %collective-permute-start.12 = (bf16[64,1536]{1,0:T(8,128)(2,1)S(1)}, bf16[64,1536]{1,0:T(8,128)(2,1)S(1)}, u32[]{:S(2)}, u32[]{:S(2)}) collective-permute-start(bf16[64,1536]{1,0:T(8,128)(2,1)S(1)} %get-tuple-element.121.refs_0_), channel_id=1, source_target_pairs={{0,4},{1,5},{2,6},{3,7},{4,0},{5,1},{6,2},{7,3},{8,12},{9,13},{10,... | collective-permute-start | bytes 589832 | tf_op jit(solution)/shard_map/ppermute | solution.py:44
  45.6 8.0 %collective-permute-start.11 = (bf16[64,1536]{1,0:T(8,128)(2,1)S(1)}, bf16[64,1536]{1,0:T(8,128)(2,1)S(1)}, u32[]{:S(2)}, u32[]{:S(2)}) collective-permute-start(bf16[64,1536]{1,0:T(8,128)(2,1)S(1)} %get-tuple-element.121.refs_0_), channel_id=1, source_target_pairs={{0,1},{1,0},{2,3},{3,2},{4,8},{5,9},{6,10},{7,11},{8,4},{9,5},{10,... | collective-permute-start | bytes 589832 | tf_op jit(solution)/shard_map/ppermute | solution.py:44
  49.7 8.0 %collective-permute-start.18 = (bf16[64,1536]{1,0:T(8,128)(2,1)S(1)}, bf16[64,1536]{1,0:T(8,128)(2,1)S(1)}, u32[]{:S(2)}, u32[]{:S(2)}) collective-permute-start(bf16[64,1536]{1,0:T(8,128)(2,1)S(1)} %get-tuple-element.129.refs_0_), channel_id=1, source_target_pairs={{0,4},{1,5},{2,6},{3,7},{4,0},{5,1},{6,2},{7,3},{8,12},{9,13},{10,... | collective-permute-start | bytes 589832 | tf_op jit(solution)/shard_map/ppermute | solution.py:44
  51.0 6.7 %collective-permute-start.17 = (bf16[64,1536]{1,0:T(8,128)(2,1)S(1)}, bf16[64,1536]{1,0:T(8,128)(2,1)S(1)}, u32[]{:S(2)}, u32[]{:S(2)}) collective-permute-start(bf16[64,1536]{1,0:T(8,128)(2,1)S(1)} %get-tuple-element.129.refs_0_), channel_id=1, source_target_pairs={{0,1},{1,0},{2,3},{3,2},{4,8},{5,9},{6,10},{7,11},{8,4},{9,5},{10,... | collective-permute-start | bytes 589832 | tf_op jit(solution)/shard_map/ppermute | solution.py:44
  53.5 6.8 %collective-permute-start.15 = (bf16[64,1536]{1,0:T(8,128)(2,1)S(1)}, bf16[64,1536]{1,0:T(8,128)(2,1)S(1)}, u32[]{:S(2)}, u32[]{:S(2)}) collective-permute-start(bf16[64,1536]{1,0:T(8,128)(2,1)S(1)} %get-tuple-element.126), channel_id=1, source_target_pairs={{0,1},{1,0},{2,3},{3,2},{4,8},{5,9},{6,10},{7,11},{8,4},{9,5},{10,... | collective-permute-start | bytes 589832 | tf_op jit(solution)/shard_map/ppermute | solution.py:44
  53.6 8.3 %collective-permute-start.16 = (bf16[64,1536]{1,0:T(8,128)(2,1)S(1)}, bf16[64,1536]{1,0:T(8,128)(2,1)S(1)}, u32[]{:S(2)}, u32[]{:S(2)}) collective-permute-start(bf16[64,1536]{1,0:T(8,128)(2,1)S(1)} %get-tuple-element.127.refs_3_), channel_id=1, source_target_pairs={{0,4},{1,5},{2,6},{3,7},{4,0},{5,1},{6,2},{7,3},{8,12},{9,13},{10,... | collective-permute-start | bytes 589832 | tf_op jit(solution)/shard_map/ppermute | solution.py:44
  57.8 7.0 %collective-permute-start.21 = (bf16[64,1536]{1,0:T(8,128)(2,1)S(1)}, bf16[64,1536]{1,0:T(8,128)(2,1)S(1)}, u32[]{:S(2)}, u32[]{:S(2)}) collective-permute-start(bf16[64,1536]{1,0:T(8,128)(2,1)S(1)} %get-tuple-element.134), channel_id=1, source_target_pairs={{0,1},{1,0},{2,3},{3,2},{4,8},{5,9},{6,10},{7,11},{8,4},{9,5},{10,... | collective-permute-start | bytes 589832 | tf_op jit(solution)/shard_map/ppermute | solution.py:44
  57.8 8.3 %collective-permute-start.22 = (bf16[64,1536]{1,0:T(8,128)(2,1)S(1)}, bf16[64,1536]{1,0:T(8,128)(2,1)S(1)}, u32[]{:S(2)}, u32[]{:S(2)}) collective-permute-start(bf16[64,1536]{1,0:T(8,128)(2,1)S(1)} %get-tuple-element.130.refs_4_), channel_id=1, source_target_pairs={{0,4},{1,5},{2,6},{3,7},{4,0},{5,1},{6,2},{7,3},{8,12},{9,13},{10,... | collective-permute-start | bytes 589832 | tf_op jit(solution)/shard_map/ppermute | solution.py:44
  62.0 6.9 %collective-permute-start.19 = (bf16[64,1536]{1,0:T(8,128)(2,1)S(1)}, bf16[64,1536]{1,0:T(8,128)(2,1)S(1)}, u32[]{:S(2)}, u32[]{:S(2)}) collective-permute-start(bf16[64,1536]{1,0:T(8,128)(2,1)S(1)} %get-tuple-element.131), channel_id=1, source_target_pairs={{0,1},{1,0},{2,3},{3,2},{4,8},{5,9},{6,10},{7,11},{8,4},{9,5},{10,... | collective-permute-start | bytes 589832 | tf_op jit(solution)/shard_map/ppermute | solution.py:44
  62.1 8.3 %collective-permute-start.20 = (bf16[64,1536]{1,0:T(8,128)(2,1)S(1)}, bf16[64,1536]{1,0:T(8,128)(2,1)S(1)}, u32[]{:S(2)}, u32[]{:S(2)}) collective-permute-start(bf16[64,1536]{1,0:T(8,128)(2,1)S(1)} %get-tuple-element.132.refs_4_), channel_id=1, source_target_pairs={{0,4},{1,5},{2,6},{3,7},{4,0},{5,1},{6,2},{7,3},{8,12},{9,13},{10,... | collective-permute-start | bytes 589832 | tf_op jit(solution)/shard_map/ppermute | solution.py:44
  66.2 11.0 %collective-permute-start.25 = (bf16[64,1536]{1,0:T(8,128)(2,1)S(1)}, bf16[64,1536]{1,0:T(8,128)(2,1)S(1)}, u32[]{:S(2)}, u32[]{:S(2)}) collective-permute-start(bf16[64,1536]{1,0:T(8,128)(2,1)S(1)} %get-tuple-element.139), channel_id=1, source_target_pairs={{0,1},{1,0},{2,3},{3,2},{4,8},{5,9},{6,10},{7,11},{8,4},{9,5},{10,... | collective-permute-start | bytes 589832 | tf_op jit(solution)/shard_map/ppermute | solution.py:44
  66.3 10.9 %collective-permute-start.26 = (bf16[64,1536]{1,0:T(8,128)(2,1)S(1)}, bf16[64,1536]{1,0:T(8,128)(2,1)S(1)}, u32[]{:S(2)}, u32[]{:S(2)}) collective-permute-start(bf16[64,1536]{1,0:T(8,128)(2,1)S(1)} %get-tuple-element.135.refs_4_), channel_id=1, source_target_pairs={{0,4},{1,5},{2,6},{3,7},{4,0},{5,1},{6,2},{7,3},{8,12},{9,13},{10,... | collective-permute-start | bytes 589832 | tf_op jit(solution)/shard_map/ppermute | solution.py:44
  70.4 7.8 %collective-permute-start.24 = (bf16[64,1536]{1,0:T(8,128)(2,1)S(1)}, bf16[64,1536]{1,0:T(8,128)(2,1)S(1)}, u32[]{:S(2)}, u32[]{:S(2)}) collective-permute-start(bf16[64,1536]{1,0:T(8,128)(2,1)S(1)} %get-tuple-element.137), channel_id=1, source_target_pairs={{0,1},{1,0},{2,3},{3,2},{4,8},{5,9},{6,10},{7,11},{8,4},{9,5},{10,... | collective-permute-start | bytes 589832 | tf_op jit(solution)/shard_map/ppermute | solution.py:44
  70.5 7.9 %collective-permute-start.23 = (bf16[64,1536]{1,0:T(8,128)(2,1)S(1)}, bf16[64,1536]{1,0:T(8,128)(2,1)S(1)}, u32[]{:S(2)}, u32[]{:S(2)}) collective-permute-start(bf16[64,1536]{1,0:T(8,128)(2,1)S(1)} %get-tuple-element.136.refs_9_), channel_id=1, source_target_pairs={{0,4},{1,5},{2,6},{3,7},{4,0},{5,1},{6,2},{7,3},{8,12},{9,13},{10,... | collective-permute-start | bytes 589832 | tf_op jit(solution)/shard_map/ppermute | solution.py:44
  77.3 7.2 %collective-permute-start.30 = (bf16[64,1536]{1,0:T(8,128)(2,1)S(1)}, bf16[64,1536]{1,0:T(8,128)(2,1)S(1)}, u32[]{:S(2)}, u32[]{:S(2)}) collective-permute-start(bf16[64,1536]{1,0:T(8,128)(2,1)S(1)} %get-tuple-element.144), channel_id=1, source_target_pairs={{0,1},{1,0},{2,3},{3,2},{4,8},{5,9},{6,10},{7,11},{8,4},{9,5},{10,... | collective-permute-start | bytes 589832 | tf_op jit(solution)/shard_map/ppermute | solution.py:44
  77.4 7.8 %collective-permute-start.29 = (bf16[64,1536]{1,0:T(8,128)(2,1)S(1)}, bf16[64,1536]{1,0:T(8,128)(2,1)S(1)}, u32[]{:S(2)}, u32[]{:S(2)}) collective-permute-start(bf16[64,1536]{1,0:T(8,128)(2,1)S(1)} %get-tuple-element.141.refs_4_), channel_id=1, source_target_pairs={{0,4},{1,5},{2,6},{3,7},{4,0},{5,1},{6,2},{7,3},{8,12},{9,13},{10,... | collective-permute-start | bytes 589832 | tf_op jit(solution)/shard_map/ppermute | solution.py:44
  78.7 7.8 %collective-permute-start.28 = (bf16[64,1536]{1,0:T(8,128)(2,1)S(1)}, bf16[64,1536]{1,0:T(8,128)(2,1)S(1)}, u32[]{:S(2)}, u32[]{:S(2)}) collective-permute-start(bf16[64,1536]{1,0:T(8,128)(2,1)S(1)} %get-tuple-element.142.refs_0_), channel_id=1, source_target_pairs={{0,1},{1,0},{2,3},{3,2},{4,8},{5,9},{6,10},{7,11},{8,4},{9,5},{10,... | collective-permute-start | bytes 589832 | tf_op jit(solution)/shard_map/ppermute | solution.py:44
  78.8 10.5 %collective-permute-start.27 = (bf16[64,1536]{1,0:T(8,128)(2,1)S(1)}, bf16[64,1536]{1,0:T(8,128)(2,1)S(1)}, u32[]{:S(2)}, u32[]{:S(2)}) collective-permute-start(bf16[64,1536]{1,0:T(8,128)(2,1)S(1)} %get-tuple-element.142.refs_0_), channel_id=1, source_target_pairs={{0,4},{1,5},{2,6},{3,7},{4,0},{5,1},{6,2},{7,3},{8,12},{9,13},{10,... | collective-permute-start | bytes 589832 | tf_op jit(solution)/shard_map/ppermute | solution.py:44
  85.5 9.4 %collective-permute-start.34 = (bf16[64,1536]{1,0:T(8,128)(2,1)S(1)}, bf16[64,1536]{1,0:T(8,128)(2,1)S(1)}, u32[]{:S(2)}, u32[]{:S(2)}) collective-permute-start(bf16[64,1536]{1,0:T(8,128)(2,1)S(1)} %get-tuple-element.151.refs_0_.refs_6_), channel_id=1, source_target_pairs={{0,4},{1,5},{2,6},{3,7},{4,0},{5,1},{6,2},{7,3},{8,12},{9,13},{10,... | collective-permute-start | bytes 589832 | tf_op jit(solution)/shard_map/ppermute | solution.py:44
  86.5 8.4 %collective-permute-start.33 = (bf16[64,1536]{1,0:T(8,128)(2,1)S(1)}, bf16[64,1536]{1,0:T(8,128)(2,1)S(1)}, u32[]{:S(2)}, u32[]{:S(2)}) collective-permute-start(bf16[64,1536]{1,0:T(8,128)(2,1)S(1)} %get-tuple-element.151.refs_0_.refs_6_), channel_id=1, source_target_pairs={{0,1},{1,0},{2,3},{3,2},{4,8},{5,9},{6,10},{7,11},{8,4},{9,5},{10,... | collective-permute-start | bytes 589832 | tf_op jit(solution)/shard_map/ppermute | solution.py:44
  89.4 7.1 %collective-permute-start.32 = (bf16[64,1536]{1,0:T(8,128)(2,1)S(1)}, bf16[64,1536]{1,0:T(8,128)(2,1)S(1)}, u32[]{:S(2)}, u32[]{:S(2)}) collective-permute-start(bf16[64,1536]{1,0:T(8,128)(2,1)S(1)} %get-tuple-element.150), channel_id=1, source_target_pairs={{0,1},{1,0},{2,3},{3,2},{4,8},{5,9},{6,10},{7,11},{8,4},{9,5},{10,... | collective-permute-start | bytes 589832 | tf_op jit(solution)/shard_map/ppermute | solution.py:44
  89.4 13.0 %collective-permute-start.31 = (bf16[64,1536]{1,0:T(8,128)(2,1)S(1)}, bf16[64,1536]{1,0:T(8,128)(2,1)S(1)}, u32[]{:S(2)}, u32[]{:S(2)}) collective-permute-start(bf16[64,1536]{1,0:T(8,128)(2,1)S(1)} %get-tuple-element.149.refs_12_), channel_id=1, source_target_pairs={{0,4},{1,5},{2,6},{3,7},{4,0},{5,1},{6,2},{7,3},{8,12},{9,13},{10,... | collective-permute-start | bytes 589832 | tf_op jit(solution)/shard_map/ppermute | solution.py:44
  91.2 15.8 %slice-start = ((s8[9437184]{0:T(1024)(128)(4,1)}), s8[4194304]{0:T(1024)(128)(4,1)S(1)}, s32[]{:S(2)}) async-start(s8[9437184]{0:T(1024)(128)(4,1)} %bitcast), calls=%async_computation | async-start | bytes 8388608
  91.2 15.8 %slice-start.1 = ((s8[9437184]{0:T(1024)(128)(4,1)}), s8[4194304]{0:T(1024)(128)(4,1)S(1)}, s32[]{:S(2)}) async-start(s8[9437184]{0:T(1024)(128)(4,1)} %bitcast), calls=%async_computation.1 | async-start | bytes 8388608
  95.0 6.2 %collective-permute-start.37 = (bf16[64,1536]{1,0:T(8,128)(2,1)S(1)}, bf16[64,1536]{1,0:T(8,128)(2,1)S(1)}, u32[]{:S(2)}, u32[]{:S(2)}) collective-permute-start(bf16[64,1536]{1,0:T(8,128)(2,1)S(1)} %get-tuple-element.157), channel_id=1, source_target_pairs={{0,1},{1,0},{2,3},{3,2},{4,8},{5,9},{6,10},{7,11},{8,4},{9,5},{10,... | collective-permute-start | bytes 589832 | tf_op jit(solution)/shard_map/ppermute | solution.py:44
  95.0 15.7 %collective-permute-start.36 = (bf16[64,1536]{1,0:T(8,128)(2,1)S(1)}, bf16[64,1536]{1,0:T(8,128)(2,1)S(1)}, u32[]{:S(2)}, u32[]{:S(2)}) collective-permute-start(bf16[64,1536]{1,0:T(8,128)(2,1)S(1)} %get-tuple-element.156.refs_1_), channel_id=1, source_target_pairs={{0,4},{1,5},{2,6},{3,7},{4,0},{5,1},{6,2},{7,3},{8,12},{9,13},{10,... | collective-permute-start | bytes 589832 | tf_op jit(solution)/shard_map/ppermute | solution.py:44
  96.5 10.5 %collective-permute-start.35 = (bf16[64,1536]{1,0:T(8,128)(2,1)S(1)}, bf16[64,1536]{1,0:T(8,128)(2,1)S(1)}, u32[]{:S(2)}, u32[]{:S(2)}) collective-permute-start(bf16[64,1536]{1,0:T(8,128)(2,1)S(1)} %relay_far.2.refs_10_), channel_id=1, source_target_pairs={{0,4},{1,5},{2,6},{3,7},{4,0},{5,1},{6,2},{7,3},{8,12},{9,13},{10,... | collective-permute-start | bytes 589832 | tf_op jit(solution)/shard_map/ppermute | solution.py:44
  97.7 9.4 %slice-start.2 = ((s8[9437184]{0:T(1024)(128)(4,1)}), s8[1048576]{0:T(1024)(128)(4,1)S(1)}, s32[]{:S(2)}) async-start(s8[9437184]{0:T(1024)(128)(4,1)} %bitcast), calls=%async_computation.2 | async-start | bytes 2097152
  101.2 9.6 %collective-permute-start.38 = (bf16[64,1536]{1,0:T(8,128)(2,1)S(1)}, bf16[64,1536]{1,0:T(8,128)(2,1)S(1)}, u32[]{:S(2)}, u32[]{:S(2)}) collective-permute-start(bf16[64,1536]{1,0:T(8,128)(2,1)S(1)} %relay_far.3.refs_9_), channel_id=1, source_target_pairs={{0,4},{1,5},{2,6},{3,7},{4,0},{5,1},{6,2},{7,3},{8,12},{9,13},{10,... | collective-permute-start | bytes 589832 | tf_op jit(solution)/shard_map/ppermute | solution.py:44
  112.7 2.6 %collective-permute-start.40 = (bf16[64,1536]{1,0:T(8,128)(2,1)S(1)}, bf16[64,1536]{1,0:T(8,128)(2,1)S(1)}, u32[]{:S(2)}, u32[]{:S(2)}) collective-permute-start(bf16[64,1536]{1,0:T(8,128)(2,1)S(1)} %get-tuple-element.173), channel_id=1, source_target_pairs={{0,1},{1,0},{2,3},{3,2},{4,5},{5,4},{6,7},{7,6},{8,9},{9,8},{10,11... | collective-permute-start | bytes 589832 | tf_op jit(solution)/shard_map/ppermute | solution.py:44
  114.7 2.1 %collective-permute-start.39 = (bf16[64,1536]{1,0:T(8,128)(2,1)S(1)}, bf16[64,1536]{1,0:T(8,128)(2,1)S(1)}, u32[]{:S(2)}, u32[]{:S(2)}) collective-permute-start(bf16[64,1536]{1,0:T(8,128)(2,1)S(1)} %get-tuple-element.170), channel_id=1, source_target_pairs={{0,1},{1,0},{2,3},{3,2},{4,5},{5,4},{6,7},{7,6},{8,9},{9,8},{10,11... | collective-permute-start | bytes 589832 | tf_op jit(solution)/shard_map/ppermute | solution.py:44
  115.3 11.1 %collective-permute-start.41 = (bf16[64,1536]{1,0:T(8,128)(2,1)S(1)}, bf16[64,1536]{1,0:T(8,128)(2,1)S(1)}, u32[]{:S(2)}, u32[]{:S(2)}) collective-permute-start(bf16[64,1536]{1,0:T(8,128)(2,1)S(1)} %get-tuple-element.176.refs_3_), channel_id=1, source_target_pairs={{0,2},{2,0},{1,3},{3,1},{4,6},{6,4},{5,7},{7,5},{8,10},{10,8},{9,1... | collective-permute-start | bytes 589832 | tf_op jit(solution)/shard_map/ppermute | solution.py:44
  116.9 9.4 %collective-permute-start.44 = (bf16[64,1536]{1,0:T(8,128)(2,1)S(1)}, bf16[64,1536]{1,0:T(8,128)(2,1)S(1)}, u32[]{:S(2)}, u32[]{:S(2)}) collective-permute-start(bf16[64,1536]{1,0:T(8,128)(2,1)S(1)} %get-tuple-element.182), channel_id=1, source_target_pairs={{0,1},{1,0},{2,3},{3,2},{4,5},{5,4},{6,7},{7,6},{8,9},{9,8},{10,11... | collective-permute-start | bytes 589832 | tf_op jit(solution)/shard_map/ppermute | solution.py:44
  117.0 9.5 %collective-permute-start.43 = (bf16[64,1536]{1,0:T(8,128)(2,1)S(1)}, bf16[64,1536]{1,0:T(8,128)(2,1)S(1)}, u32[]{:S(2)}, u32[]{:S(2)}) collective-permute-start(bf16[64,1536]{1,0:T(8,128)(2,1)S(1)} %get-tuple-element.177.refs_17_), channel_id=1, source_target_pairs={{0,2},{2,0},{1,3},{3,1},{4,6},{6,4},{5,7},{7,5},{8,10},{10,8},{9,1... | collective-permute-start | bytes 589832 | tf_op jit(solution)/shard_map/ppermute | solution.py:44
  118.3 8.2 %collective-permute-start.42 = (bf16[64,1536]{1,0:T(8,128)(2,1)S(1)}, bf16[64,1536]{1,0:T(8,128)(2,1)S(1)}, u32[]{:S(2)}, u32[]{:S(2)}) collective-permute-start(bf16[64,1536]{1,0:T(8,128)(2,1)S(1)} %get-tuple-element.180), channel_id=1, source_target_pairs={{0,1},{1,0},{2,3},{3,2},{4,5},{5,4},{6,7},{7,6},{8,9},{9,8},{10,11... | collective-permute-start | bytes 589832 | tf_op jit(solution)/shard_map/ppermute | solution.py:44

commit v5 on v4

--- a/solution.py
+++ b/solution.py
@@ -73,6 +73,7 @@
 
 
 TILE = 512
+LOADED_TILE = 768
 EXTRA = 4
 UNROLL = True
 TOKEN = jax.ShapeDtypeStruct((8, 128), f32)
@@ -165,7 +166,7 @@
 
 def forward(x, weight, start, size, tokens, parts, dep=None, loaded=None, following=None):
     depth = weight.shape[0]
-    tile = tile_of(size, TILE)
+    tile = tile_of(size, LOADED_TILE if loaded is not None else TILE)
     rows = tokens // parts
     first = isinstance(x, tuple)
     here = loaded is not None
@@ -306,7 +307,7 @@
     size = sum(b.shape[1] for b in blocks) if len(blocks) == 1 else blocks[0].shape[1] * (len(blocks) // 6)
     tokens = blocks[0].shape[0] * (4 if len(blocks) > 1 else 1)
     features = cuts[-1][1] - cuts[0][0]
-    tile = tile_of(cuts[0][1] - cuts[0][0], TILE)
+    tile = tile_of(cuts[0][1] - cuts[0][0], LOADED_TILE if loaded is not None else TILE)
     operands, outs, scratch, aliases = [], [], [], {}
 
     def give(name, value, spec=None):

time: 128 us -> 127 us (level)
  waiting for transfers between devices: 26.1 us -> 24.2 us
    ppermute x45, waiting for transfers between devices: 26.1 us -> 24.2 us  [send(): return lax.ppermute(value, axis, pairs)]
where the time goes in v5:
time: 127 us
  Pallas kernels  53 us (42%)
  starting transfers between devices  47.1 us (37%)
  waiting for transfers between devices  24.2 us (19%)
    pallas_call x34, Pallas kernels, call(): return pl.pallas_call(ordered, in_specs=in_specs, **options)(*operands, dep)  50 us
    ppermute x45, starting transfers between devices, send(): return lax.ppermute(value, axis, pairs)  47.1 us
    ppermute x45, waiting for transfers between devices, send(): return lax.ppermute(value, axis, pairs)  24.2 us
    pallas_call x2, Pallas kernels, call(): return pl.pallas_call(kernel, in_specs=in_specs, **options)(*operands)  2.96 us
  transfers between devices with their start and end apart: 45, of which 15 were waited for; matrix products, arithmetic and copies ran while one was open for 0% of the time, Pallas kernels for 37%

profile of v5, /device:TPU:0, one launch (start us, length us, event | category | flops | bytes accessed | tf_op | source)
XLA Modules:
  0.0 126.5 jit_solution(16453040575324309470)
XLA Ops:
  0.6 3.0 %collective-permute-start.1 = (bf16[64,3072]{1,0:T(8,128)(2,1)}, bf16[64,3072]{1,0:T(8,128)(2,1)S(1)}, u32[]{:S(2)}, u32[]{:S(2)}) collective-permute-start(bf16[64,3072]{1,0:T(8,128)(2,1)} %a.1), channel_id=1, source_target_pairs={{0,2},{2,0},{1,3},{3,1},{4,6},{6,4},{5,7},{7,5},{8,10},{10,8},{9,1... | collective-permute-start | bytes 1179656 | tf_op jit(solution)/shard_map/ppermute | solution.py:44
  3.6 1.0 copy-done.1
  4.7 0.1 collective-permute-start
  4.8 6.4 %preload.1 = (bf16[3072,1536]{1,0:T(8,128)(2,1)S(1)}, bf16[3072,1536]{1,0:T(8,128)(2,1)S(1)}) custom-call(bf16[3072,6144]{1,0:T(8,128)(2,1)} %refs_1_.3, bf16[64,3072]{1,0:T(8,128)(2,1)S(1)} %local.1.refs_1_.refs_0_), custom_call_target="tpu_custom_call" | custom-call | bytes 18874368 | tf_op jit(solution)/shard_map/preload/pallas_call | solution.py:382
  11.2 1.8 %collective-permute-done.1.refs_0_ = bf16[64,3072]{1,0:T(8,128)(2,1)S(1)} collective-permute-done((bf16[64,3072]{1,0:T(8,128)(2,1)}, bf16[64,3072]{1,0:T(8,128)(2,1)S(1)}, u32[]{:S(2)}, u32[]{:S(2)}) %collective-permute-start.1) | collective-permute-done | bytes 393248 | tf_op jit(solution)/shard_map/ppermute | solution.py:44
  13.0 0.1 collective-permute-start.2
  13.1 1.7 %collective-permute-done.2.refs_3_ = bf16[64,3072]{1,0:T(8,128)(2,1)S(1)} collective-permute-done((bf16[64,3072]{1,0:T(8,128)(2,1)S(1)}, bf16[64,3072]{1,0:T(8,128)(2,1)S(1)}, u32[]{:S(2)}, u32[]{:S(2)}) %collective-permute-start.2) | collective-permute-done | bytes 393248 | tf_op jit(solution)/shard_map/ppermute | solution.py:44
  14.8 2.9 %forward_sums.4 = (bf16[64,1536]{1,0:T(8,128)(2,1)S(1)}, bf16[64,1536]{1,0:T(8,128)(2,1)S(1)}, bf16[64,1536]{1,0:T(8,128)(2,1)S(1)}, bf16[64,1536]{1,0:T(8,128)(...) custom-call(bf16[3072,1536]{1,0:T(8,128)(2,1)S(1)} %get-tuple-element.95.refs_1_.w_ref.refs_6_, ...), custom_call_target="tpu_custom_call" | custom-call | flops 2415919104 | bytes 9437184 | tf_op jit(solution)/shard_map/forward_sums/pallas_call | solution.py:380
  17.7 1.9 %collective-permute-start.3 = (bf16[64,1536]{1,0:T(8,128)(2,1)S(1)}, bf16[64,1536]{1,0:T(8,128)(2,1)S(1)}, u32[]{:S(2)}, u32[]{:S(2)}) collective-permute-start(bf16[64,1536]{1,0:T(8,128)(2,1)S(1)} %get-tuple-element.100.refs_1_), channel_id=1, source_target_pairs={{0,4},{1,5},{2,6},{3,7},{4,0},{5,1},{6,2},{7,3},{8,12},{9,13},{10,... | collective-permute-start | bytes 589832 | tf_op jit(solution)/shard_map/ppermute | solution.py:44
  19.6 3.7 %forward_sums.5 = (bf16[64,1536]{1,0:T(8,128)(2,1)S(1)}, bf16[64,1536]{1,0:T(8,128)(2,1)S(1)}, bf16[64,1536]{1,0:T(8,128)(2,1)S(1)}, bf16[64,1536]{1,0:T(8,128)(...) custom-call(bf16[3072,1536]{1,0:T(8,128)(2,1)S(1)} %get-tuple-element.94.refs_0_.refs_6_, ...), custom_call_target="tpu_custom_call" | custom-call | flops 2415919104 | bytes 9437184 | tf_op jit(solution)/shard_map/forward_sums/pallas_call | solution.py:382
  23.3 0.3 collective-permute-start.6
  23.6 1.2 collective-permute-done.3.refs_2_
  24.8 0.1 collective-permute-start.4
  24.9 3.3 %collective-permute-start.5 = (bf16[64,1536]{1,0:T(8,128)(2,1)S(1)}, bf16[64,1536]{1,0:T(8,128)(2,1)S(1)}, u32[]{:S(2)}, u32[]{:S(2)}) collective-permute-start(bf16[64,1536]{1,0:T(8,128)(2,1)S(1)} %get-tuple-element.102.refs_3_), channel_id=1, source_target_pairs={{0,4},{1,5},{2,6},{3,7},{4,0},{5,1},{6,2},{7,3},{8,12},{9,13},{10,... | collective-permute-start | bytes 589832 | tf_op jit(solution)/shard_map/ppermute | solution.py:44
  28.2 3.7 %forward_sums.6 = (bf16[64,1536]{1,0:T(8,128)(2,1)S(1)}, bf16[64,1536]{1,0:T(8,128)(2,1)S(1)}, bf16[64,1536]{1,0:T(8,128)(2,1)S(1)}, bf16[64,1536]{1,0:T(8,128)(...) custom-call(bf16[3072,1536]{1,0:T(8,128)(2,1)S(1)} %get-tuple-element.98.refs_0_.refs_6_, ...), custom_call_target="tpu_custom_call" | custom-call | flops 2415919104 | bytes 9437184 | tf_op jit(solution)/shard_map/forward_sums/pallas_call | solution.py:382
  32.0 0.1 collective-permute-start.9
  32.1 2.4 %collective-permute-start.10 = (bf16[64,1536]{1,0:T(8,128)(2,1)S(1)}, bf16[64,1536]{1,0:T(8,128)(2,1)S(1)}, u32[]{:S(2)}, u32[]{:S(2)}) collective-permute-start(bf16[64,1536]{1,0:T(8,128)(2,1)S(1)} %get-tuple-element.113.refs_4_), channel_id=1, source_target_pairs={{0,4},{1,5},{2,6},{3,7},{4,0},{5,1},{6,2},{7,3},{8,12},{9,13},{10,... | collective-permute-start | bytes 589832 | tf_op jit(solution)/shard_map/ppermute | solution.py:44
  34.5 0.1 collective-permute-start.8
  34.6 3.6 %collective-permute-start.7 = (bf16[64,1536]{1,0:T(8,128)(2,1)S(1)}, bf16[64,1536]{1,0:T(8,128)(2,1)S(1)}, u32[]{:S(2)}, u32[]{:S(2)}) collective-permute-start(bf16[64,1536]{1,0:T(8,128)(2,1)S(1)} %get-tuple-element.114.refs_2_), channel_id=1, source_target_pairs={{0,4},{1,5},{2,6},{3,7},{4,0},{5,1},{6,2},{7,3},{8,12},{9,13},{10,... | collective-permute-start | bytes 589832 | tf_op jit(solution)/shard_map/ppermute | solution.py:44
  38.1 2.8 %forward_sums.7 = (bf16[64,1536]{1,0:T(8,128)(2,1)S(1)}, bf16[64,1536]{1,0:T(8,128)(2,1)S(1)}, bf16[64,1536]{1,0:T(8,128)(2,1)S(1)}, bf16[64,1536]{1,0:T(8,128)(2,1)S(1)}, f32[8,128]{1,0:T(8,128)S(1)}) custom-call(bf16[3072,1536]{1,0:T(8,128)(2,1)S(1)} %get-tuple-element.118.refs_0_.refs_6_, ...), custom_call_target="tpu_custom_call" | custom-call | flops 2415919104 | bytes 9437184 | tf_op jit(solution)/shard_map/forward_sums/pallas_call | solution.py:382
  41.1 1.4 %collective-permute-start.13 = (bf16[64,1536]{1,0:T(8,128)(2,1)S(1)}, bf16[64,1536]{1,0:T(8,128)(2,1)S(1)}, u32[]{:S(2)}, u32[]{:S(2)}) collective-permute-start(bf16[64,1536]{1,0:T(8,128)(2,1)S(1)} %get-tuple-element.120.refs_4_), channel_id=1, source_target_pairs={{0,4},{1,5},{2,6},{3,7},{4,0},{5,1},{6,2},{7,3},{8,12},{9,13},{10,... | collective-permute-start | bytes 589832 | tf_op jit(solution)/shard_map/ppermute | solution.py:44
  42.5 1.1 collective-permute-done.7.refs_1_
  43.6 0.4 gelu.4
  44.0 1.5 %collective-permute-start.12 = (bf16[64,1536]{1,0:T(8,128)(2,1)S(1)}, bf16[64,1536]{1,0:T(8,128)(2,1)S(1)}, u32[]{:S(2)}, u32[]{:S(2)}) collective-permute-start(bf16[64,1536]{1,0:T(8,128)(2,1)S(1)} %get-tuple-element.121.refs_0_), channel_id=1, source_target_pairs={{0,4},{1,5},{2,6},{3,7},{4,0},{5,1},{6,2},{7,3},{8,12},{9,13},{10,... | collective-permute-start | bytes 589832 | tf_op jit(solution)/shard_map/ppermute | solution.py:44
  45.6 3.3 %collective-permute-done.13.refs_1_ = bf16[64,1536]{1,0:T(8,128)(2,1)S(1)} collective-permute-done((bf16[64,1536]{1,0:T(8,128)(2,1)S(1)}, bf16[64,1536]{1,0:T(8,128)(2,1)S(1)}, u32[]{:S(2)}, u32[]{:S(2)}) %collective-permute-start.13) | collective-permute-done | bytes 196640 | tf_op jit(solution)/shard_map/ppermute | solution.py:44
  48.9 0.4 gelu.5
  49.3 1.5 %collective-permute-start.18 = (bf16[64,1536]{1,0:T(8,128)(2,1)S(1)}, bf16[64,1536]{1,0:T(8,128)(2,1)S(1)}, u32[]{:S(2)}, u32[]{:S(2)}) collective-permute-start(bf16[64,1536]{1,0:T(8,128)(2,1)S(1)} %get-tuple-element.129.refs_0_), channel_id=1, source_target_pairs={{0,4},{1,5},{2,6},{3,7},{4,0},{5,1},{6,2},{7,3},{8,12},{9,13},{10,... | collective-permute-start | bytes 589832 | tf_op jit(solution)/shard_map/ppermute | solution.py:44
  50.8 2.3 %collective-permute-done.12.refs_2_.refs_1_ = bf16[64,1536]{1,0:T(8,128)(2,1)S(1)} collective-permute-done((bf16[64,1536]{1,0:T(8,128)(2,1)S(1)}, bf16[64,1536]{1,0:T(8,128)(2,1)S(1)}, u32[]{:S(2)}, u32[]{:S(2)}) %collective-permute-start.12) | collective-permute-done | bytes 196640 | tf_op jit(solution)/shard_map/ppermute | solution.py:44
  53.1 0.1 collective-permute-start.15
  53.2 3.0 %collective-permute-start.16 = (bf16[64,1536]{1,0:T(8,128)(2,1)S(1)}, bf16[64,1536]{1,0:T(8,128)(2,1)S(1)}, u32[]{:S(2)}, u32[]{:S(2)}) collective-permute-start(bf16[64,1536]{1,0:T(8,128)(2,1)S(1)} %get-tuple-element.127.refs_3_), channel_id=1, source_target_pairs={{0,4},{1,5},{2,6},{3,7},{4,0},{5,1},{6,2},{7,3},{8,12},{9,13},{10,... | collective-permute-start | bytes 589832 | tf_op jit(solution)/shard_map/ppermute | solution.py:44
  56.2 1.1 collective-permute-done.18.refs_2_.refs_1_
  57.4 2.7 %collective-permute-start.22 = (bf16[64,1536]{1,0:T(8,128)(2,1)S(1)}, bf16[64,1536]{1,0:T(8,128)(2,1)S(1)}, u32[]{:S(2)}, u32[]{:S(2)}) collective-permute-start(bf16[64,1536]{1,0:T(8,128)(2,1)S(1)} %get-tuple-element.130.refs_4_), channel_id=1, source_target_pairs={{0,4},{1,5},{2,6},{3,7},{4,0},{5,1},{6,2},{7,3},{8,12},{9,13},{10,... | collective-permute-start | bytes 589832 | tf_op jit(solution)/shard_map/ppermute | solution.py:44
  60.2 1.4 %collective-permute-done.16.refs_3_ = bf16[64,1536]{1,0:T(8,128)(2,1)S(1)} collective-permute-done((bf16[64,1536]{1,0:T(8,128)(2,1)S(1)}, bf16[64,1536]{1,0:T(8,128)(2,1)S(1)}, u32[]{:S(2)}, u32[]{:S(2)}) %collective-permute-start.16) | collective-permute-done | bytes 196640 | tf_op jit(solution)/shard_map/ppermute | solution.py:44
  61.7 2.9 %collective-permute-start.20 = (bf16[64,1536]{1,0:T(8,128)(2,1)S(1)}, bf16[64,1536]{1,0:T(8,128)(2,1)S(1)}, u32[]{:S(2)}, u32[]{:S(2)}) collective-permute-start(bf16[64,1536]{1,0:T(8,128)(2,1)S(1)} %get-tuple-element.132.refs_4_), channel_id=1, source_target_pairs={{0,4},{1,5},{2,6},{3,7},{4,0},{5,1},{6,2},{7,3},{8,12},{9,13},{10,... | collective-permute-start | bytes 589832 | tf_op jit(solution)/shard_map/ppermute | solution.py:44
  64.6 1.1 collective-permute-done.22.refs_3_
  65.8 2.7 %collective-permute-start.26 = (bf16[64,1536]{1,0:T(8,128)(2,1)S(1)}, bf16[64,1536]{1,0:T(8,128)(2,1)S(1)}, u32[]{:S(2)}, u32[]{:S(2)}) collective-permute-start(bf16[64,1536]{1,0:T(8,128)(2,1)S(1)} %get-tuple-element.135.refs_4_), channel_id=1, source_target_pairs={{0,4},{1,5},{2,6},{3,7},{4,0},{5,1},{6,2},{7,3},{8,12},{9,13},{10,... | collective-permute-start | bytes 589832 | tf_op jit(solution)/shard_map/ppermute | solution.py:44
  68.6 1.4 %collective-permute-done.20.refs_3_.refs_5_ = bf16[64,1536]{1,0:T(8,128)(2,1)S(1)} collective-permute-done((bf16[64,1536]{1,0:T(8,128)(2,1)S(1)}, bf16[64,1536]{1,0:T(8,128)(2,1)S(1)}, u32[]{:S(2)}, u32[]{:S(2)}) %collective-permute-start.20) | collective-permute-done | bytes 196640 | tf_op jit(solution)/shard_map/ppermute | solution.py:44
  70.1 2.9 %collective-permute-start.23 = (bf16[64,1536]{1,0:T(8,128)(2,1)S(1)}, bf16[64,1536]{1,0:T(8,128)(2,1)S(1)}, u32[]{:S(2)}, u32[]{:S(2)}) collective-permute-start(bf16[64,1536]{1,0:T(8,128)(2,1)S(1)} %get-tuple-element.136.refs_9_), channel_id=1, source_target_pairs={{0,4},{1,5},{2,6},{3,7},{4,0},{5,1},{6,2},{7,3},{8,12},{9,13},{10,... | collective-permute-start | bytes 589832 | tf_op jit(solution)/shard_map/ppermute | solution.py:44
  73.0 3.9 %grads.8 = (f32[256,1536]{1,0:T(8,128)S(1)}, bf16[3072,6144]{1,0:T(8,128)(2,1)}, bf16[64,6144]{1,0:T(8,128)(2,1)}, f32[8,128]{1,0:T(8,128)S(1)}) custom-call(bf16[64,1536]{1,0:T(8,128)(2,1)S(1)} %get-tuple-element.121.refs_0_, bf16[64,1536]{1,0:T(8,128)(2,1)S(1)} %collective-permute-done.12.refs_2_.refs_1_, ...), custom_call_target="tpu_custom_call" | custom-call | flops 2415919104 | bytes 9437184 | tf_op jit(solution)/shard_map/grads/pallas_call | solution.py:382
  77.1 1.0 collective-permute-start.29
  78.1 0.4 gelu.6
  78.6 2.1 %collective-permute-start.27 = (bf16[64,1536]{1,0:T(8,128)(2,1)S(1)}, bf16[64,1536]{1,0:T(8,128)(2,1)S(1)}, u32[]{:S(2)}, u32[]{:S(2)}) collective-permute-start(bf16[64,1536]{1,0:T(8,128)(2,1)S(1)} %get-tuple-element.142.refs_0_), channel_id=1, source_target_pairs={{0,4},{1,5},{2,6},{3,7},{4,0},{5,1},{6,2},{7,3},{8,12},{9,13},{10,... | collective-permute-start | bytes 589832 | tf_op jit(solution)/shard_map/ppermute | solution.py:44
  80.7 4.1 %grads.9 = (f32[256,1536]{1,0:T(8,128)S(1)}, bf16[3072,6144]{1,0:T(8,128)(2,1)}, f32[8,128]{1,0:T(8,128)S(1)}) custom-call(bf16[64,1536]{1,0:T(8,128)(2,1)S(1)} %get-tuple-element.121.refs_0_, bf16[64,1536]{1,0:T(8,128)(2,1)S(1)} %collective-permute-done.12.refs_2_.refs_1_, ...), custom_call_target="tpu_custom_call", output_to_operand_aliasing={{1}: (8, {})} | custom-call | flops 2415919104 | bytes 9437184 | tf_op jit(solution)/shard_map/grads/pallas_call | solution.py:382
  84.8 0.4 gelu.7
  85.2 1.1 collective-permute-start.34
  86.4 2.7 %collective-permute-done.27.refs_1_ = bf16[64,1536]{1,0:T(8,128)(2,1)S(1)} collective-permute-done((bf16[64,1536]{1,0:T(8,128)(2,1)S(1)}, bf16[64,1536]{1,0:T(8,128)(2,1)S(1)}, u32[]{:S(2)}, u32[]{:S(2)}) %collective-permute-start.27) | collective-permute-done | bytes 196640 | tf_op jit(solution)/shard_map/ppermute | solution.py:44
  89.2 1.6 %collective-permute-start.31 = (bf16[64,1536]{1,0:T(8,128)(2,1)S(1)}, bf16[64,1536]{1,0:T(8,128)(2,1)S(1)}, u32[]{:S(2)}, u32[]{:S(2)}) collective-permute-start(bf16[64,1536]{1,0:T(8,128)(2,1)S(1)} %get-tuple-element.149.refs_12_), channel_id=1, source_target_pairs={{0,4},{1,5},{2,6},{3,7},{4,0},{5,1},{6,2},{7,3},{8,12},{9,13},{10,... | collective-permute-start | bytes 589832 | tf_op jit(solution)/shard_map/ppermute | solution.py:44
  90.8 3.7 %grads.10 = (f32[256,1536]{1,0:T(8,128)S(1)}, bf16[3072,6144]{1,0:T(8,128)(2,1)}, bf16[64,6144]{1,0:T(8,128)(2,1)}, f32[8,128]{1,0:T(8,128)S(1)}) custom-call(bf16[64,1536]{1,0:T(8,128)(2,1)S(1)} %get-tuple-element.129.refs_0_, bf16[64,1536]{1,0:T(8,128)(2,1)S(1)} %collective-permute-done.18.refs_2_.refs_1_, ...), custom_call_target="tpu_custom_call", output_to_operand_aliasing={{1}: (9, {}), {2}: (11, {})} | custom-call | flops 2415919104 | bytes 9437184 | tf_op jit(solution)/shard_map/grads/pallas_call | solution.py:382
  94.6 1.6 %collective-permute-start.36 = (bf16[64,1536]{1,0:T(8,128)(2,1)S(1)}, bf16[64,1536]{1,0:T(8,128)(2,1)S(1)}, u32[]{:S(2)}, u32[]{:S(2)}) collective-permute-start(bf16[64,1536]{1,0:T(8,128)(2,1)S(1)} %get-tuple-element.156.refs_1_), channel_id=1, source_target_pairs={{0,4},{1,5},{2,6},{3,7},{4,0},{5,1},{6,2},{7,3},{8,12},{9,13},{10,... | collective-permute-start | bytes 589832 | tf_op jit(solution)/shard_map/ppermute | solution.py:44
  96.3 1.4 %collective-permute-start.35 = (bf16[64,1536]{1,0:T(8,128)(2,1)S(1)}, bf16[64,1536]{1,0:T(8,128)(2,1)S(1)}, u32[]{:S(2)}, u32[]{:S(2)}) collective-permute-start(bf16[64,1536]{1,0:T(8,128)(2,1)S(1)} %relay_far.2.refs_10_), channel_id=1, source_target_pairs={{0,4},{1,5},{2,6},{3,7},{4,0},{5,1},{6,2},{7,3},{8,12},{9,13},{10,... | collective-permute-start | bytes 589832 | tf_op jit(solution)/shard_map/ppermute | solution.py:44
  97.7 3.7 %grads.11 = (f32[256,1536]{1,0:T(8,128)S(1)}, bf16[3072,6144]{1,0:T(8,128)(2,1)}, f32[8,128]{1,0:T(8,128)S(1)}) custom-call(bf16[64,1536]{1,0:T(8,128)(2,1)S(1)} %get-tuple-element.129.refs_0_, bf16[64,1536]{1,0:T(8,128)(2,1)S(1)} %collective-permute-done.18.refs_2_.refs_1_, ...), custom_call_target="tpu_custom_call", output_to_operand_aliasing={{1}: (9, {})} | custom-call | flops 2415919104 | bytes 9437184 | tf_op jit(solution)/shard_map/grads/pallas_call | solution.py:382
  101.5 0.7 collective-permute-start.38
  102.2 4.4 %collective-permute-done.35.refs_5_ = bf16[64,1536]{1,0:T(8,128)(2,1)S(1)} collective-permute-done((bf16[64,1536]{1,0:T(8,128)(2,1)S(1)}, bf16[64,1536]{1,0:T(8,128)(2,1)S(1)}, u32[]{:S(2)}, u32[]{:S(2)}) %collective-permute-start.35) | collective-permute-done | bytes 196640 | tf_op jit(solution)/shard_map/ppermute | solution.py:44
  106.6 3.4 %grads.12 = (f32[256,1536]{1,0:T(8,128)S(1)}, f32[256,1536]{1,0:T(8,128)S(1)}, f32[8,128]{1,0:T(8,128)S(1)}) custom-call(bf16[64,1536]{1,0:T(8,128)(2,1)S(1)} %get-tuple-element.142.refs_0_, bf16[64,1536]{1,0:T(8,128)(2,1)S(1)} %collective-permute-done.27.refs_1_, bf16[64,1536]{1,0:T(8,128)(2,1)S(1)} %collective-permute-done.28.refs_0_.refs_2_, ...), custom_call_target="tpu_custom_call" | custom-call | flops 2415919104 | bytes 9437184 | tf_op jit(solution)/shard_map/grads/pallas_call | solution.py:382
  110.1 0.3 collective-permute-done.38.refs_5_.refs_11_
  110.4 1.7 %grads.13 = (bf16[64,1536]{1,0:T(8,128)(2,1)S(1)}, bf16[64,1536]{1,0:T(8,128)(2,1)S(1)}, bf16[64,1536]{1,0:T(8,128)(2,1)S(1)}, bf16[64,1536]{1,0:T(8,128)(2,1)S(1)}, f32[8,128]{1,0:T(8,128)S(1)}) custom-call(bf16[64,1536]{1,0:T(8,128)(2,1)S(1)} %get-tuple-element.151.refs_0_.refs_6_, bf16[64,1536]{1,0:T(8,128)(2,1)S(1)} %collective-permute-done.34.refs_1_.refs_7_, ...), custom_call_target="tpu_custom_call" | custom-call | flops 1207959552 | bytes 4718592 | tf_op jit(solution)/shard_map/grads/pallas_call | solution.py:382
  112.2 1.7 %grads.14 = (bf16[64,1536]{1,0:T(8,128)(2,1)S(1)}, bf16[64,1536]{1,0:T(8,128)(2,1)S(1)}, bf16[64,1536]{1,0:T(8,128)(2,1)S(1)}, bf16[64,1536]{1,0:T(8,128)(2,1)S(1)}, f32[8,128]{1,0:T(8,128)S(1)}) custom-call(bf16[64,1536]{1,0:T(8,128)(2,1)S(1)} %get-tuple-element.151.refs_0_.refs_6_, bf16[64,1536]{1,0:T(8,128)(2,1)S(1)} %collective-permute-done.34.refs_1_.refs_7_, ...), custom_call_target="tpu_custom_call" | custom-call | flops 1207959552 | bytes 4718592 | tf_op jit(solution)/shard_map/grads/pallas_call | solution.py:382
  113.9 0.6 collective-permute-start.39
  114.5 1.4 %collective-permute-start.41 = (bf16[64,1536]{1,0:T(8,128)(2,1)S(1)}, bf16[64,1536]{1,0:T(8,128)(2,1)S(1)}, u32[]{:S(2)}, u32[]{:S(2)}) collective-permute-start(bf16[64,1536]{1,0:T(8,128)(2,1)S(1)} %get-tuple-element.176.refs_3_), channel_id=1, source_target_pairs={{0,2},{2,0},{1,3},{3,1},{4,6},{6,4},{5,7},{7,5},{8,10},{10,8},{9,1... | collective-permute-start | bytes 589832 | tf_op jit(solution)/shard_map/ppermute | solution.py:44
  116.0 0.1 collective-permute-start.44
  116.0 1.3 %collective-permute-start.43 = (bf16[64,1536]{1,0:T(8,128)(2,1)S(1)}, bf16[64,1536]{1,0:T(8,128)(2,1)S(1)}, u32[]{:S(2)}, u32[]{:S(2)}) collective-permute-start(bf16[64,1536]{1,0:T(8,128)(2,1)S(1)} %get-tuple-element.177.refs_17_), channel_id=1, source_target_pairs={{0,2},{2,0},{1,3},{3,1},{4,6},{6,4},{5,7},{7,5},{8,10},{10,8},{9,1... | collective-permute-start | bytes 589832 | tf_op jit(solution)/shard_map/ppermute | solution.py:44
  117.3 8.0 %grads.15 = (bf16[3072,6144]{1,0:T(8,128)(2,1)}, bf16[64,6144]{1,0:T(8,128)(2,1)}, f32[8,128]{1,0:T(8,128)S(1)}) custom-call(bf16[64,1536]{1,0:T(8,128)(2,1)S(1)} %get-tuple-element.142.refs_0_, bf16[64,1536]{1,0:T(8,128)(2,1)S(1)} %collective-permute-done.27.refs_1_, ...), custom_call_target="tpu_custom_call", output_to_operand_aliasing={{0}: (13, {}), {1}: (16, {})} | custom-call | flops 4831838208 | bytes 18874368 | tf_op jit(solution)/shard_map/grads/pallas_call | solution.py:382
  125.4 0.3 collective-permute-done.43.refs_4_
  125.6 0.9 finish.1
  (76 shorter events, 1.5 us)
Async XLA Ops:
  0.6 12.3 %collective-permute-start.1 = (bf16[64,3072]{1,0:T(8,128)(2,1)}, bf16[64,3072]{1,0:T(8,128)(2,1)S(1)}, u32[]{:S(2)}, u32[]{:S(2)}) collective-permute-start(bf16[64,3072]{1,0:T(8,128)(2,1)} %a.1), channel_id=1, source_target_pairs={{0,2},{2,0},{1,3},{3,1},{4,6},{6,4},{5,7},{7,5},{8,10},{10,8},{9,1... | collective-permute-start | bytes 1179656 | tf_op jit(solution)/shard_map/ppermute | solution.py:44
  3.6 1.0 copy-start.1
  4.7 8.4 %collective-permute-start = (bf16[64,3072]{1,0:T(8,128)(2,1)S(1)}, bf16[64,3072]{1,0:T(8,128)(2,1)S(1)}, u32[]{:S(2)}, u32[]{:S(2)}) collective-permute-start(bf16[64,3072]{1,0:T(8,128)(2,1)S(1)} %local.1.refs_1_.refs_0_), channel_id=1, source_target_pairs={{0,1},{1,0},{2,3},{3,2},{4,5},{5,4},{6,7},{7,6},{8,9},{9,8},{10,11... | collective-permute-start | bytes 1179656 | tf_op jit(solution)/shard_map/ppermute | solution.py:44
  13.0 1.8 %collective-permute-start.2 = (bf16[64,3072]{1,0:T(8,128)(2,1)S(1)}, bf16[64,3072]{1,0:T(8,128)(2,1)S(1)}, u32[]{:S(2)}, u32[]{:S(2)}) collective-permute-start(bf16[64,3072]{1,0:T(8,128)(2,1)S(1)} %corner.1.refs_2_), channel_id=1, source_target_pairs={{0,1},{1,0},{2,3},{3,2},{4,5},{5,4},{6,7},{7,6},{8,9},{9,8},{10,11... | collective-permute-start | bytes 1179656 | tf_op jit(solution)/shard_map/ppermute | solution.py:44
  17.7 7.1 %collective-permute-start.3 = (bf16[64,1536]{1,0:T(8,128)(2,1)S(1)}, bf16[64,1536]{1,0:T(8,128)(2,1)S(1)}, u32[]{:S(2)}, u32[]{:S(2)}) collective-permute-start(bf16[64,1536]{1,0:T(8,128)(2,1)S(1)} %get-tuple-element.100.refs_1_), channel_id=1, source_target_pairs={{0,4},{1,5},{2,6},{3,7},{4,0},{5,1},{6,2},{7,3},{8,12},{9,13},{10,... | collective-permute-start | bytes 589832 | tf_op jit(solution)/shard_map/ppermute | solution.py:44
  23.3 8.6 %copy-start = (bf16[3072,1536]{1,0:T(8,128)(2,1)}, bf16[3072,1536]{1,0:T(8,128)(2,1)S(1)}, u32[]{:S(2)}) copy-start(bf16[3072,1536]{1,0:T(8,128)(2,1)S(1)} %get-tuple-element.98.refs_0_.refs_6_) | copy-start | bytes 28311556
  23.3 8.6 %collective-permute-start.6 = (bf16[64,1536]{1,0:T(8,128)(2,1)S(1)}, bf16[64,1536]{1,0:T(8,128)(2,1)S(1)}, u32[]{:S(2)}, u32[]{:S(2)}) collective-permute-start(bf16[64,1536]{1,0:T(8,128)(2,1)S(1)} %get-tuple-element.111.refs_1_), channel_id=1, source_target_pairs={{0,4},{1,5},{2,6},{3,7},{4,0},{5,1},{6,2},{7,3},{8,12},{9,13},{10,... | collective-permute-start | bytes 589832 | tf_op jit(solution)/shard_map/ppermute | solution.py:44
  24.8 9.6 %collective-permute-start.4 = (bf16[64,1536]{1,0:T(8,128)(2,1)S(1)}, bf16[64,1536]{1,0:T(8,128)(2,1)S(1)}, u32[]{:S(2)}, u32[]{:S(2)}) collective-permute-start(bf16[64,1536]{1,0:T(8,128)(2,1)S(1)} %get-tuple-element.109), channel_id=1, source_target_pairs={{0,1},{1,0},{2,3},{3,2},{4,8},{5,9},{6,10},{7,11},{8,4},{9,5},{10,... | collective-permute-start | bytes 589832 | tf_op jit(solution)/shard_map/ppermute | solution.py:44
  24.9 9.5 %collective-permute-start.5 = (bf16[64,1536]{1,0:T(8,128)(2,1)S(1)}, bf16[64,1536]{1,0:T(8,128)(2,1)S(1)}, u32[]{:S(2)}, u32[]{:S(2)}) collective-permute-start(bf16[64,1536]{1,0:T(8,128)(2,1)S(1)} %get-tuple-element.102.refs_3_), channel_id=1, source_target_pairs={{0,4},{1,5},{2,6},{3,7},{4,0},{5,1},{6,2},{7,3},{8,12},{9,13},{10,... | collective-permute-start | bytes 589832 | tf_op jit(solution)/shard_map/ppermute | solution.py:44
  31.9 10.5 %copy-start.2 = (bf16[64,6144]{1,0:T(8,128)(2,1)S(1)}, bf16[64,6144]{1,0:T(8,128)(2,1)}, u32[]{:S(2)}) copy-start(bf16[64,6144]{1,0:T(8,128)(2,1)} %param.5) | copy-start | bytes 2359300
  32.0 9.0 %collective-permute-start.9 = (bf16[64,1536]{1,0:T(8,128)(2,1)S(1)}, bf16[64,1536]{1,0:T(8,128)(2,1)S(1)}, u32[]{:S(2)}, u32[]{:S(2)}) collective-permute-start(bf16[64,1536]{1,0:T(8,128)(2,1)S(1)} %get-tuple-element.117), channel_id=1, source_target_pairs={{0,1},{1,0},{2,3},{3,2},{4,8},{5,9},{6,10},{7,11},{8,4},{9,5},{10,... | collective-permute-start | bytes 589832 | tf_op jit(solution)/shard_map/ppermute | solution.py:44
  32.1 8.9 %collective-permute-start.10 = (bf16[64,1536]{1,0:T(8,128)(2,1)S(1)}, bf16[64,1536]{1,0:T(8,128)(2,1)S(1)}, u32[]{:S(2)}, u32[]{:S(2)}) collective-permute-start(bf16[64,1536]{1,0:T(8,128)(2,1)S(1)} %get-tuple-element.113.refs_4_), channel_id=1, source_target_pairs={{0,4},{1,5},{2,6},{3,7},{4,0},{5,1},{6,2},{7,3},{8,12},{9,13},{10,... | collective-permute-start | bytes 589832 | tf_op jit(solution)/shard_map/ppermute | solution.py:44
  34.5 8.0 %collective-permute-start.8 = (bf16[64,1536]{1,0:T(8,128)(2,1)S(1)}, bf16[64,1536]{1,0:T(8,128)(2,1)S(1)}, u32[]{:S(2)}, u32[]{:S(2)}) collective-permute-start(bf16[64,1536]{1,0:T(8,128)(2,1)S(1)} %get-tuple-element.115), channel_id=1, source_target_pairs={{0,1},{1,0},{2,3},{3,2},{4,8},{5,9},{6,10},{7,11},{8,4},{9,5},{10,... | collective-permute-start | bytes 589832 | tf_op jit(solution)/shard_map/ppermute | solution.py:44
  34.6 9.0 %collective-permute-start.7 = (bf16[64,1536]{1,0:T(8,128)(2,1)S(1)}, bf16[64,1536]{1,0:T(8,128)(2,1)S(1)}, u32[]{:S(2)}, u32[]{:S(2)}) collective-permute-start(bf16[64,1536]{1,0:T(8,128)(2,1)S(1)} %get-tuple-element.114.refs_2_), channel_id=1, source_target_pairs={{0,4},{1,5},{2,6},{3,7},{4,0},{5,1},{6,2},{7,3},{8,12},{9,13},{10,... | collective-permute-start | bytes 589832 | tf_op jit(solution)/shard_map/ppermute | solution.py:44
  41.0 4.5 %collective-permute-start.14 = (bf16[64,1536]{1,0:T(8,128)(2,1)S(1)}, bf16[64,1536]{1,0:T(8,128)(2,1)S(1)}, u32[]{:S(2)}, u32[]{:S(2)}) collective-permute-start(bf16[64,1536]{1,0:T(8,128)(2,1)S(1)} %get-tuple-element.123), channel_id=1, source_target_pairs={{0,1},{1,0},{2,3},{3,2},{4,8},{5,9},{6,10},{7,11},{8,4},{9,5},{10,... | collective-permute-start | bytes 589832 | tf_op jit(solution)/shard_map/ppermute | solution.py:44
  41.1 7.8 %collective-permute-start.13 = (bf16[64,1536]{1,0:T(8,128)(2,1)S(1)}, bf16[64,1536]{1,0:T(8,128)(2,1)S(1)}, u32[]{:S(2)}, u32[]{:S(2)}) collective-permute-start(bf16[64,1536]{1,0:T(8,128)(2,1)S(1)} %get-tuple-element.120.refs_4_), channel_id=1, source_target_pairs={{0,4},{1,5},{2,6},{3,7},{4,0},{5,1},{6,2},{7,3},{8,12},{9,13},{10,... | collective-permute-start | bytes 589832 | tf_op jit(solution)/shard_map/ppermute | solution.py:44
  44.0 9.1 %collective-permute-start.12 = (bf16[64,1536]{1,0:T(8,128)(2,1)S(1)}, bf16[64,1536]{1,0:T(8,128)(2,1)S(1)}, u32[]{:S(2)}, u32[]{:S(2)}) collective-permute-start(bf16[64,1536]{1,0:T(8,128)(2,1)S(1)} %get-tuple-element.121.refs_0_), channel_id=1, source_target_pairs={{0,4},{1,5},{2,6},{3,7},{4,0},{5,1},{6,2},{7,3},{8,12},{9,13},{10,... | collective-permute-start | bytes 589832 | tf_op jit(solution)/shard_map/ppermute | solution.py:44
  45.6 7.5 %collective-permute-start.11 = (bf16[64,1536]{1,0:T(8,128)(2,1)S(1)}, bf16[64,1536]{1,0:T(8,128)(2,1)S(1)}, u32[]{:S(2)}, u32[]{:S(2)}) collective-permute-start(bf16[64,1536]{1,0:T(8,128)(2,1)S(1)} %get-tuple-element.121.refs_0_), channel_id=1, source_target_pairs={{0,1},{1,0},{2,3},{3,2},{4,8},{5,9},{6,10},{7,11},{8,4},{9,5},{10,... | collective-permute-start | bytes 589832 | tf_op jit(solution)/shard_map/ppermute | solution.py:44
  49.3 8.0 %collective-permute-start.18 = (bf16[64,1536]{1,0:T(8,128)(2,1)S(1)}, bf16[64,1536]{1,0:T(8,128)(2,1)S(1)}, u32[]{:S(2)}, u32[]{:S(2)}) collective-permute-start(bf16[64,1536]{1,0:T(8,128)(2,1)S(1)} %get-tuple-element.129.refs_0_), channel_id=1, source_target_pairs={{0,4},{1,5},{2,6},{3,7},{4,0},{5,1},{6,2},{7,3},{8,12},{9,13},{10,... | collective-permute-start | bytes 589832 | tf_op jit(solution)/shard_map/ppermute | solution.py:44
  50.8 6.5 %collective-permute-start.17 = (bf16[64,1536]{1,0:T(8,128)(2,1)S(1)}, bf16[64,1536]{1,0:T(8,128)(2,1)S(1)}, u32[]{:S(2)}, u32[]{:S(2)}) collective-permute-start(bf16[64,1536]{1,0:T(8,128)(2,1)S(1)} %get-tuple-element.129.refs_0_), channel_id=1, source_target_pairs={{0,1},{1,0},{2,3},{3,2},{4,8},{5,9},{6,10},{7,11},{8,4},{9,5},{10,... | collective-permute-start | bytes 589832 | tf_op jit(solution)/shard_map/ppermute | solution.py:44
  53.1 7.0 %collective-permute-start.15 = (bf16[64,1536]{1,0:T(8,128)(2,1)S(1)}, bf16[64,1536]{1,0:T(8,128)(2,1)S(1)}, u32[]{:S(2)}, u32[]{:S(2)}) collective-permute-start(bf16[64,1536]{1,0:T(8,128)(2,1)S(1)} %get-tuple-element.126), channel_id=1, source_target_pairs={{0,1},{1,0},{2,3},{3,2},{4,8},{5,9},{6,10},{7,11},{8,4},{9,5},{10,... | collective-permute-start | bytes 589832 | tf_op jit(solution)/shard_map/ppermute | solution.py:44
  53.2 8.3 %collective-permute-start.16 = (bf16[64,1536]{1,0:T(8,128)(2,1)S(1)}, bf16[64,1536]{1,0:T(8,128)(2,1)S(1)}, u32[]{:S(2)}, u32[]{:S(2)}) collective-permute-start(bf16[64,1536]{1,0:T(8,128)(2,1)S(1)} %get-tuple-element.127.refs_3_), channel_id=1, source_target_pairs={{0,4},{1,5},{2,6},{3,7},{4,0},{5,1},{6,2},{7,3},{8,12},{9,13},{10,... | collective-permute-start | bytes 589832 | tf_op jit(solution)/shard_map/ppermute | solution.py:44
  57.3 7.3 %collective-permute-start.21 = (bf16[64,1536]{1,0:T(8,128)(2,1)S(1)}, bf16[64,1536]{1,0:T(8,128)(2,1)S(1)}, u32[]{:S(2)}, u32[]{:S(2)}) collective-permute-start(bf16[64,1536]{1,0:T(8,128)(2,1)S(1)} %get-tuple-element.134), channel_id=1, source_target_pairs={{0,1},{1,0},{2,3},{3,2},{4,8},{5,9},{6,10},{7,11},{8,4},{9,5},{10,... | collective-permute-start | bytes 589832 | tf_op jit(solution)/shard_map/ppermute | solution.py:44
  57.4 8.3 %collective-permute-start.22 = (bf16[64,1536]{1,0:T(8,128)(2,1)S(1)}, bf16[64,1536]{1,0:T(8,128)(2,1)S(1)}, u32[]{:S(2)}, u32[]{:S(2)}) collective-permute-start(bf16[64,1536]{1,0:T(8,128)(2,1)S(1)} %get-tuple-element.130.refs_4_), channel_id=1, source_target_pairs={{0,4},{1,5},{2,6},{3,7},{4,0},{5,1},{6,2},{7,3},{8,12},{9,13},{10,... | collective-permute-start | bytes 589832 | tf_op jit(solution)/shard_map/ppermute | solution.py:44
  61.6 7.0 %collective-permute-start.19 = (bf16[64,1536]{1,0:T(8,128)(2,1)S(1)}, bf16[64,1536]{1,0:T(8,128)(2,1)S(1)}, u32[]{:S(2)}, u32[]{:S(2)}) collective-permute-start(bf16[64,1536]{1,0:T(8,128)(2,1)S(1)} %get-tuple-element.131), channel_id=1, source_target_pairs={{0,1},{1,0},{2,3},{3,2},{4,8},{5,9},{6,10},{7,11},{8,4},{9,5},{10,... | collective-permute-start | bytes 589832 | tf_op jit(solution)/shard_map/ppermute | solution.py:44
  61.7 8.3 %collective-permute-start.20 = (bf16[64,1536]{1,0:T(8,128)(2,1)S(1)}, bf16[64,1536]{1,0:T(8,128)(2,1)S(1)}, u32[]{:S(2)}, u32[]{:S(2)}) collective-permute-start(bf16[64,1536]{1,0:T(8,128)(2,1)S(1)} %get-tuple-element.132.refs_4_), channel_id=1, source_target_pairs={{0,4},{1,5},{2,6},{3,7},{4,0},{5,1},{6,2},{7,3},{8,12},{9,13},{10,... | collective-permute-start | bytes 589832 | tf_op jit(solution)/shard_map/ppermute | solution.py:44
  65.8 11.1 %collective-permute-start.25 = (bf16[64,1536]{1,0:T(8,128)(2,1)S(1)}, bf16[64,1536]{1,0:T(8,128)(2,1)S(1)}, u32[]{:S(2)}, u32[]{:S(2)}) collective-permute-start(bf16[64,1536]{1,0:T(8,128)(2,1)S(1)} %get-tuple-element.139), channel_id=1, source_target_pairs={{0,1},{1,0},{2,3},{3,2},{4,8},{5,9},{6,10},{7,11},{8,4},{9,5},{10,... | collective-permute-start | bytes 589832 | tf_op jit(solution)/shard_map/ppermute | solution.py:44
  65.8 11.1 %collective-permute-start.26 = (bf16[64,1536]{1,0:T(8,128)(2,1)S(1)}, bf16[64,1536]{1,0:T(8,128)(2,1)S(1)}, u32[]{:S(2)}, u32[]{:S(2)}) collective-permute-start(bf16[64,1536]{1,0:T(8,128)(2,1)S(1)} %get-tuple-element.135.refs_4_), channel_id=1, source_target_pairs={{0,4},{1,5},{2,6},{3,7},{4,0},{5,1},{6,2},{7,3},{8,12},{9,13},{10,... | collective-permute-start | bytes 589832 | tf_op jit(solution)/shard_map/ppermute | solution.py:44
  70.0 8.1 %collective-permute-start.24 = (bf16[64,1536]{1,0:T(8,128)(2,1)S(1)}, bf16[64,1536]{1,0:T(8,128)(2,1)S(1)}, u32[]{:S(2)}, u32[]{:S(2)}) collective-permute-start(bf16[64,1536]{1,0:T(8,128)(2,1)S(1)} %get-tuple-element.137), channel_id=1, source_target_pairs={{0,1},{1,0},{2,3},{3,2},{4,8},{5,9},{6,10},{7,11},{8,4},{9,5},{10,... | collective-permute-start | bytes 589832 | tf_op jit(solution)/shard_map/ppermute | solution.py:44
  70.1 8.0 %collective-permute-start.23 = (bf16[64,1536]{1,0:T(8,128)(2,1)S(1)}, bf16[64,1536]{1,0:T(8,128)(2,1)S(1)}, u32[]{:S(2)}, u32[]{:S(2)}) collective-permute-start(bf16[64,1536]{1,0:T(8,128)(2,1)S(1)} %get-tuple-element.136.refs_9_), channel_id=1, source_target_pairs={{0,4},{1,5},{2,6},{3,7},{4,0},{5,1},{6,2},{7,3},{8,12},{9,13},{10,... | collective-permute-start | bytes 589832 | tf_op jit(solution)/shard_map/ppermute | solution.py:44
  77.0 7.8 %collective-permute-start.30 = (bf16[64,1536]{1,0:T(8,128)(2,1)S(1)}, bf16[64,1536]{1,0:T(8,128)(2,1)S(1)}, u32[]{:S(2)}, u32[]{:S(2)}) collective-permute-start(bf16[64,1536]{1,0:T(8,128)(2,1)S(1)} %get-tuple-element.144), channel_id=1, source_target_pairs={{0,1},{1,0},{2,3},{3,2},{4,8},{5,9},{6,10},{7,11},{8,4},{9,5},{10,... | collective-permute-start | bytes 589832 | tf_op jit(solution)/shard_map/ppermute | solution.py:44
  77.1 7.8 %collective-permute-start.29 = (bf16[64,1536]{1,0:T(8,128)(2,1)S(1)}, bf16[64,1536]{1,0:T(8,128)(2,1)S(1)}, u32[]{:S(2)}, u32[]{:S(2)}) collective-permute-start(bf16[64,1536]{1,0:T(8,128)(2,1)S(1)} %get-tuple-element.141.refs_4_), channel_id=1, source_target_pairs={{0,4},{1,5},{2,6},{3,7},{4,0},{5,1},{6,2},{7,3},{8,12},{9,13},{10,... | collective-permute-start | bytes 589832 | tf_op jit(solution)/shard_map/ppermute | solution.py:44
  78.5 7.9 %collective-permute-start.28 = (bf16[64,1536]{1,0:T(8,128)(2,1)S(1)}, bf16[64,1536]{1,0:T(8,128)(2,1)S(1)}, u32[]{:S(2)}, u32[]{:S(2)}) collective-permute-start(bf16[64,1536]{1,0:T(8,128)(2,1)S(1)} %get-tuple-element.142.refs_0_), channel_id=1, source_target_pairs={{0,1},{1,0},{2,3},{3,2},{4,8},{5,9},{6,10},{7,11},{8,4},{9,5},{10,... | collective-permute-start | bytes 589832 | tf_op jit(solution)/shard_map/ppermute | solution.py:44
  78.6 10.5 %collective-permute-start.27 = (bf16[64,1536]{1,0:T(8,128)(2,1)S(1)}, bf16[64,1536]{1,0:T(8,128)(2,1)S(1)}, u32[]{:S(2)}, u32[]{:S(2)}) collective-permute-start(bf16[64,1536]{1,0:T(8,128)(2,1)S(1)} %get-tuple-element.142.refs_0_), channel_id=1, source_target_pairs={{0,4},{1,5},{2,6},{3,7},{4,0},{5,1},{6,2},{7,3},{8,12},{9,13},{10,... | collective-permute-start | bytes 589832 | tf_op jit(solution)/shard_map/ppermute | solution.py:44
  85.2 9.3 %collective-permute-start.34 = (bf16[64,1536]{1,0:T(8,128)(2,1)S(1)}, bf16[64,1536]{1,0:T(8,128)(2,1)S(1)}, u32[]{:S(2)}, u32[]{:S(2)}) collective-permute-start(bf16[64,1536]{1,0:T(8,128)(2,1)S(1)} %get-tuple-element.151.refs_0_.refs_6_), channel_id=1, source_target_pairs={{0,4},{1,5},{2,6},{3,7},{4,0},{5,1},{6,2},{7,3},{8,12},{9,13},{10,... | collective-permute-start | bytes 589832 | tf_op jit(solution)/shard_map/ppermute | solution.py:44
  86.4 8.2 %collective-permute-start.33 = (bf16[64,1536]{1,0:T(8,128)(2,1)S(1)}, bf16[64,1536]{1,0:T(8,128)(2,1)S(1)}, u32[]{:S(2)}, u32[]{:S(2)}) collective-permute-start(bf16[64,1536]{1,0:T(8,128)(2,1)S(1)} %get-tuple-element.151.refs_0_.refs_6_), channel_id=1, source_target_pairs={{0,1},{1,0},{2,3},{3,2},{4,8},{5,9},{6,10},{7,11},{8,4},{9,5},{10,... | collective-permute-start | bytes 589832 | tf_op jit(solution)/shard_map/ppermute | solution.py:44
  89.1 7.2 %collective-permute-start.32 = (bf16[64,1536]{1,0:T(8,128)(2,1)S(1)}, bf16[64,1536]{1,0:T(8,128)(2,1)S(1)}, u32[]{:S(2)}, u32[]{:S(2)}) collective-permute-start(bf16[64,1536]{1,0:T(8,128)(2,1)S(1)} %get-tuple-element.150), channel_id=1, source_target_pairs={{0,1},{1,0},{2,3},{3,2},{4,8},{5,9},{6,10},{7,11},{8,4},{9,5},{10,... | collective-permute-start | bytes 589832 | tf_op jit(solution)/shard_map/ppermute | solution.py:44
  89.2 13.1 %collective-permute-start.31 = (bf16[64,1536]{1,0:T(8,128)(2,1)S(1)}, bf16[64,1536]{1,0:T(8,128)(2,1)S(1)}, u32[]{:S(2)}, u32[]{:S(2)}) collective-permute-start(bf16[64,1536]{1,0:T(8,128)(2,1)S(1)} %get-tuple-element.149.refs_12_), channel_id=1, source_target_pairs={{0,4},{1,5},{2,6},{3,7},{4,0},{5,1},{6,2},{7,3},{8,12},{9,13},{10,... | collective-permute-start | bytes 589832 | tf_op jit(solution)/shard_map/ppermute | solution.py:44
  90.7 15.9 %slice-start = ((s8[9437184]{0:T(1024)(128)(4,1)}), s8[4194304]{0:T(1024)(128)(4,1)S(1)}, s32[]{:S(2)}) async-start(s8[9437184]{0:T(1024)(128)(4,1)} %bitcast), calls=%async_computation | async-start | bytes 8388608
  90.7 15.9 %slice-start.1 = ((s8[9437184]{0:T(1024)(128)(4,1)}), s8[4194304]{0:T(1024)(128)(4,1)S(1)}, s32[]{:S(2)}) async-start(s8[9437184]{0:T(1024)(128)(4,1)} %bitcast), calls=%async_computation.1 | async-start | bytes 8388608
  94.6 6.9 %collective-permute-start.37 = (bf16[64,1536]{1,0:T(8,128)(2,1)S(1)}, bf16[64,1536]{1,0:T(8,128)(2,1)S(1)}, u32[]{:S(2)}, u32[]{:S(2)}) collective-permute-start(bf16[64,1536]{1,0:T(8,128)(2,1)S(1)} %get-tuple-element.157), channel_id=1, source_target_pairs={{0,1},{1,0},{2,3},{3,2},{4,8},{5,9},{6,10},{7,11},{8,4},{9,5},{10,... | collective-permute-start | bytes 589832 | tf_op jit(solution)/shard_map/ppermute | solution.py:44
  94.6 15.4 %collective-permute-start.36 = (bf16[64,1536]{1,0:T(8,128)(2,1)S(1)}, bf16[64,1536]{1,0:T(8,128)(2,1)S(1)}, u32[]{:S(2)}, u32[]{:S(2)}) collective-permute-start(bf16[64,1536]{1,0:T(8,128)(2,1)S(1)} %get-tuple-element.156.refs_1_), channel_id=1, source_target_pairs={{0,4},{1,5},{2,6},{3,7},{4,0},{5,1},{6,2},{7,3},{8,12},{9,13},{10,... | collective-permute-start | bytes 589832 | tf_op jit(solution)/shard_map/ppermute | solution.py:44
  96.3 10.3 %collective-permute-start.35 = (bf16[64,1536]{1,0:T(8,128)(2,1)S(1)}, bf16[64,1536]{1,0:T(8,128)(2,1)S(1)}, u32[]{:S(2)}, u32[]{:S(2)}) collective-permute-start(bf16[64,1536]{1,0:T(8,128)(2,1)S(1)} %relay_far.2.refs_10_), channel_id=1, source_target_pairs={{0,4},{1,5},{2,6},{3,7},{4,0},{5,1},{6,2},{7,3},{8,12},{9,13},{10,... | collective-permute-start | bytes 589832 | tf_op jit(solution)/shard_map/ppermute | solution.py:44
  97.7 8.9 %slice-start.2 = ((s8[9437184]{0:T(1024)(128)(4,1)}), s8[1048576]{0:T(1024)(128)(4,1)S(1)}, s32[]{:S(2)}) async-start(s8[9437184]{0:T(1024)(128)(4,1)} %bitcast), calls=%async_computation.2 | async-start | bytes 2097152
  101.5 8.9 %collective-permute-start.38 = (bf16[64,1536]{1,0:T(8,128)(2,1)S(1)}, bf16[64,1536]{1,0:T(8,128)(2,1)S(1)}, u32[]{:S(2)}, u32[]{:S(2)}) collective-permute-start(bf16[64,1536]{1,0:T(8,128)(2,1)S(1)} %relay_far.3.refs_9_), channel_id=1, source_target_pairs={{0,4},{1,5},{2,6},{3,7},{4,0},{5,1},{6,2},{7,3},{8,12},{9,13},{10,... | collective-permute-start | bytes 589832 | tf_op jit(solution)/shard_map/ppermute | solution.py:44
  112.1 2.4 %collective-permute-start.40 = (bf16[64,1536]{1,0:T(8,128)(2,1)S(1)}, bf16[64,1536]{1,0:T(8,128)(2,1)S(1)}, u32[]{:S(2)}, u32[]{:S(2)}) collective-permute-start(bf16[64,1536]{1,0:T(8,128)(2,1)S(1)} %get-tuple-element.173), channel_id=1, source_target_pairs={{0,1},{1,0},{2,3},{3,2},{4,5},{5,4},{6,7},{7,6},{8,9},{9,8},{10,11... | collective-permute-start | bytes 589832 | tf_op jit(solution)/shard_map/ppermute | solution.py:44
  113.9 2.0 %collective-permute-start.39 = (bf16[64,1536]{1,0:T(8,128)(2,1)S(1)}, bf16[64,1536]{1,0:T(8,128)(2,1)S(1)}, u32[]{:S(2)}, u32[]{:S(2)}) collective-permute-start(bf16[64,1536]{1,0:T(8,128)(2,1)S(1)} %get-tuple-element.170), channel_id=1, source_target_pairs={{0,1},{1,0},{2,3},{3,2},{4,5},{5,4},{6,7},{7,6},{8,9},{9,8},{10,11... | collective-permute-start | bytes 589832 | tf_op jit(solution)/shard_map/ppermute | solution.py:44
  114.5 11.1 %collective-permute-start.41 = (bf16[64,1536]{1,0:T(8,128)(2,1)S(1)}, bf16[64,1536]{1,0:T(8,128)(2,1)S(1)}, u32[]{:S(2)}, u32[]{:S(2)}) collective-permute-start(bf16[64,1536]{1,0:T(8,128)(2,1)S(1)} %get-tuple-element.176.refs_3_), channel_id=1, source_target_pairs={{0,2},{2,0},{1,3},{3,1},{4,6},{6,4},{5,7},{7,5},{8,10},{10,8},{9,1... | collective-permute-start | bytes 589832 | tf_op jit(solution)/shard_map/ppermute | solution.py:44
  116.0 9.4 %collective-permute-start.44 = (bf16[64,1536]{1,0:T(8,128)(2,1)S(1)}, bf16[64,1536]{1,0:T(8,128)(2,1)S(1)}, u32[]{:S(2)}, u32[]{:S(2)}) collective-permute-start(bf16[64,1536]{1,0:T(8,128)(2,1)S(1)} %get-tuple-element.182), channel_id=1, source_target_pairs={{0,1},{1,0},{2,3},{3,2},{4,5},{5,4},{6,7},{7,6},{8,9},{9,8},{10,11... | collective-permute-start | bytes 589832 | tf_op jit(solution)/shard_map/ppermute | solution.py:44
  116.0 9.6 %collective-permute-start.43 = (bf16[64,1536]{1,0:T(8,128)(2,1)S(1)}, bf16[64,1536]{1,0:T(8,128)(2,1)S(1)}, u32[]{:S(2)}, u32[]{:S(2)}) collective-permute-start(bf16[64,1536]{1,0:T(8,128)(2,1)S(1)} %get-tuple-element.177.refs_17_), channel_id=1, source_target_pairs={{0,2},{2,0},{1,3},{3,1},{4,6},{6,4},{5,7},{7,5},{8,10},{10,8},{9,1... | collective-permute-start | bytes 589832 | tf_op jit(solution)/shard_map/ppermute | solution.py:44
  117.3 8.3 %collective-permute-start.42 = (bf16[64,1536]{1,0:T(8,128)(2,1)S(1)}, bf16[64,1536]{1,0:T(8,128)(2,1)S(1)}, u32[]{:S(2)}, u32[]{:S(2)}) collective-permute-start(bf16[64,1536]{1,0:T(8,128)(2,1)S(1)} %get-tuple-element.180), channel_id=1, source_target_pairs={{0,1},{1,0},{2,3},{3,2},{4,5},{5,4},{6,7},{7,6},{8,9},{9,8},{10,11... | collective-permute-start | bytes 589832 | tf_op jit(solution)/shard_map/ppermute | solution.py:44
